TPU v7x, 32 devices: a whole 2x2x4 slice. The times are simulated.
32 devices in a mesh: groups: 2 (over y), chaos: 4 (over z), space: 4 (over x, core).
Axes of the slice: x: 2, y: 2, z: 4, core: 2. Of those that a mesh axis runs over, the one named last changes fastest.
Arguments:
- source_chaos_terms: float32 [176, 8, 4096], P(('groups', 'chaos'), 'space'), parts along dimension 0, may hold values from -6 to 6
- mean_conductivity: float32 [8, 4096], P('space'), may hold values from 0.1 to 0.4
- mode_shapes: float32 [6, 8, 4096], P(None, 'space'), may hold values from -0.07 to 0.07
- coupling: int32 [6, 28, 3], replicated, may hold values from 0 to 83, as said below
- slot_term: int32 [88], replicated, may hold values from -1 to 83, as said below
- bounds: float32 [4], P('groups'), parts along dimension 0, may hold values from 0.05 to 14, as said below
Outputs:
- solution_field: float32 [176, 8, 4096], P(('groups', 'chaos'), 'space'), parts along dimension 0
- residual: float32 [176, 8, 4096], P(('groups', 'chaos'), 'space'), parts along dimension 0
There are 2 independent parts, one for each index of `groups`. A program takes and returns all parts, laid end to end along the dimension named above; an argument that names none is the same for every part. Nothing has to cross between parts.
Inputs may be any that keep to these rules, and one draw needn't show every extreme that they name: The basis is the 84 products of normalized Hermite polynomials of total degree at most 3 in 6 variables, numbered in some order. coupling[k] lists, once each, every pair of terms whose multi-indices differ only by one in mode k: the raised term, the lowered term, and the raised term's degree in mode k. `slot_term`: every term 0 to 83 stands in exactly one slot; the other slots hold -1. Slots s * 22 to s * 22 + 21 belong to index s of chaos; some index holds 22 terms. bounds[0] < bounds[1].
All inputs are finite; a program needn't handle non-finite values.
Results may differ from a plain program's by a relative error of at most 0.00011.
Values sent between devices are 32-bit elements; how exact they have to be, the bound alone decides.
No kernel may reach another device: no remote copies, remote signals or barrier semaphores. Data moves between devices by JAX's collectives and lax.ppermute only.
A program may use at most 128 MiB of HBM per device.

v0:
```python
import functools

import jax
import jax.numpy as jnp
from jax import lax
from jax.experimental import pallas as pl
from jax.experimental.pallas import tpu as pltpu
from jax.sharding import PartitionSpec as P

NY = 64
ITERS = 3
LANES = 128
BOTH = ("chaos", "space")


full_precision = lax.Precision.HIGHEST


def with_halo(cells, sides, width):
    for axis, dim in sides:
        count = lax.axis_size(axis)
        ends = count - 1
        head = lax.slice_in_dim(cells, 0, width, axis=dim)
        tail = lax.slice_in_dim(cells, cells.shape[dim] - width, cells.shape[dim], axis=dim)
        cells = jnp.concatenate(
            [
                lax.ppermute(tail, axis, [(i, (i + 1) % count) for i in range(ends)]),
                cells,
                lax.ppermute(head, axis, [((i + 1) % count, i) for i in range(ends)]),
            ],
            axis=dim,
        )
    return cells


def mixing_matrices(coupling, slot_term):
    occupied = (slot_term >= 0).astype(jnp.float32)
    raising = (slot_term[None, None, :] == coupling[:, :, 0:1]).astype(jnp.float32)
    lowering = (slot_term[None, None, :] == coupling[:, :, 1:2]).astype(jnp.float32)
    weight = jnp.sqrt(coupling[:, :, 2].astype(jnp.float32))
    raised = jnp.einsum("kps,kp,kpr->ksr", raising, weight, lowering, precision=full_precision)
    mode_mats = raised + jnp.transpose(raised, (0, 2, 1))
    return jnp.concatenate([jnp.diag(occupied)[None], mode_mats], axis=0)


def shift_cells(values, offset, edge_mask):
    fill = jnp.zeros(values.shape[:-1] + (abs(offset),), values.dtype)
    if offset > 0:
        shifted = jnp.concatenate([values[..., offset:], fill], axis=-1)
    else:
        shifted = jnp.concatenate([fill, values[..., :offset]], axis=-1)
    return shifted * edge_mask


def diffuse(field_padded, conduct_padded):
    centre = field_padded[..., 1:-1, :]
    conduct = conduct_padded[..., 1:-1, :]
    accumulated = (
        0.5 * (conduct + conduct_padded[..., :-2, :]) * (centre - field_padded[..., :-2, :])
    )
    accumulated = accumulated + 0.5 * (conduct + conduct_padded[..., 2:, :]) * (
        centre - field_padded[..., 2:, :]
    )
    cells = centre.shape[-1]
    column_in_row = lax.iota(jnp.int32, cells) % NY
    upper_mask = (column_in_row < NY - 1).astype(centre.dtype)
    lower_mask = (column_in_row > 0).astype(centre.dtype)
    all_mask = jnp.ones((cells,), centre.dtype)
    for offset, edge_mask in ((1, upper_mask), (-1, lower_mask), (NY, all_mask), (-NY, all_mask)):
        neighbour = shift_cells(centre, offset, edge_mask)
        neighbour_conduct = shift_cells(conduct, offset, edge_mask)
        accumulated = accumulated + 0.5 * (conduct + neighbour_conduct) * (centre - neighbour)
    return accumulated


def local_by_slots(source_chaos_terms, mean_conductivity, mode_shapes, coupling, slot_term, bounds):
    slot_count = source_chaos_terms.shape[0]
    conductivity = jnp.concatenate(
        [mean_conductivity[None], mean_conductivity[None] * mode_shapes], axis=0
    )
    conduct_padded = with_halo(conductivity, (("space", 1),), 1)
    matrices = mixing_matrices(coupling, slot_term)
    first_own = lax.axis_index("chaos") * slot_count
    own_rows = lax.dynamic_slice_in_dim(matrices, first_own, slot_count, 1)
    own_terms = lax.dynamic_slice_in_dim(slot_term, first_own, slot_count, 0)
    occupied = (own_terms >= 0).astype(jnp.float32)[:, None, None]
    lower_bound = bounds[0]
    upper_bound = bounds[1]
    midpoint = 0.5 * (upper_bound + lower_bound)
    half_span = 0.5 * (upper_bound - lower_bound)
    sigma_one = midpoint / half_span
    rho_now = 1.0 / sigma_one
    residual = source_chaos_terms * occupied
    solution_field = jnp.zeros_like(residual)
    direction = residual / midpoint
    for iteration in range(ITERS):
        solution_field = solution_field + direction
        fields = jnp.einsum(
            "ksr,rzc->kszc",
            own_rows,
            lax.all_gather(direction, "chaos", axis=0, tiled=True),
            precision=full_precision,
        )
        field_padded = with_halo(fields, (("space", 2),), 1)
        diffused = diffuse(field_padded, conduct_padded[:, None])
        residual = residual - jnp.sum(diffused, axis=0)
        if iteration + 1 < ITERS:
            rho_next = 1.0 / (2.0 * sigma_one - rho_now)
            direction = rho_next * rho_now * direction + 2.0 * rho_next / half_span * residual
            rho_now = rho_next
    return (solution_field, residual)


OWN_TILES = 2
FOLDED = OWN_TILES + ITERS


def block_of(device, spaces):
    chaos, space = divmod(device, spaces)
    return chaos * spaces + (space if chaos % 2 == 0 else spaces - 1 - space)


def lane_masks(rows):
    lane = lax.broadcasted_iota(jnp.int32, (rows, LANES), 1)
    return lane < NY, lane % NY > 0, lane % NY < NY - 1


def plane_sums(tiles, masks):
    low_half, has_left, has_right = masks
    zero = jnp.zeros(tiles[0].shape, jnp.float32)
    swapped = [pltpu.roll(tile, NY, 1) for tile in tiles]
    sums = []
    for t, tile in enumerate(tiles[:-1]):
        if t == 0:
            across = swapped[0] + jnp.where(low_half, swapped[2], swapped[1])
        elif t == 1:
            across = swapped[1] + jnp.where(low_half, swapped[0], swapped[2])
        elif t == 2:
            across = swapped[3] + jnp.where(low_half, swapped[1], swapped[0])
        else:
            across = swapped[t - 1] + swapped[t + 1]
        left = jnp.where(has_left, pltpu.roll(tile, 1, 1), zero)
        right = jnp.where(has_right, pltpu.roll(tile, LANES - 1, 1), zero)
        sums.append(across + (left + right))
    return sums


def neighbour_sums(ref, layer, count, masks):
    sums = plane_sums([ref[layer, t] for t in range(count)], masks)
    for other in (layer - 1, layer + 1):
        if 0 <= other < ref.shape[0]:
            sums = [total + ref[other, t] for t, total in enumerate(sums)]
    return sums


def split_stack(tiles, depth):
    wide = jnp.concatenate(tiles, axis=1)
    spare = depth // 2 - wide.shape[0]
    if spare:
        wide = jnp.concatenate([wide, jnp.zeros((spare, wide.shape[1]), wide.dtype)], axis=0)
    high = wide.astype(jnp.bfloat16)
    low = (wide - high.astype(jnp.float32)).astype(jnp.bfloat16)
    return jnp.concatenate([high, low], axis=0)


def lanes(t):
    return pl.ds(t * LANES, LANES)


def run_copies(copies):
    for copy in copies:
        copy.start()
    for copy in copies:
        copy.wait()


def scatter_kernel(blocks, in_ref, out_ref, sems):
    run_copies(
        [
            pltpu.make_async_copy(in_ref.at[:, block], out_ref.at[device], sems.at[device])
            for device, block in enumerate(blocks)
        ]
    )


def collect_kernel(blocks, in_ref, *rest):
    *outs, sems = rest
    run_copies(
        [
            pltpu.make_async_copy(
                in_ref.at[device, n], out_ref.at[:, block], sems.at[n, device]
            )
            for n, out_ref in enumerate(outs)
            for device, block in enumerate(blocks)
        ]
    )


def start_kernel(chaos, spaces, weight_ref, in_ref, residual_ref, up_ref, down_ref):
    layers, tiles, slots, _ = residual_ref.shape
    own = slots // chaos
    thick = layers // spaces
    pieces = tiles * thick
    half = layers // 2
    low_half = lane_masks(slots)[0]
    weight = weight_ref[...]
    for l in range(layers):
        i, z = divmod(l, thick)
        for t in range(tiles):
            first = t * thick + z
            residual_ref[l, t] = weight * jnp.concatenate(
                [
                    in_ref[pl.ds((c * spaces + i) * own * pieces + first, own, stride=pieces), :]
                    for c in range(chaos)
                ],
                axis=0,
            )
        up_ref[l] = residual_ref[l, 1]
        down_ref[l] = residual_ref[l, 0]
    for l in range(half):
        later = l + half
        up_ref[layers + l] = jnp.where(
            low_half, pltpu.roll(residual_ref[later, 0], NY, 1), residual_ref[l, 0]
        )
        down_ref[layers + l] = jnp.where(
            low_half, residual_ref[l, 1], pltpu.roll(residual_ref[later, 1], NY, 1)
        )


def coefficient_kernel(place, inside, mean_ref, modes_ref, a_ref, b_ref):
    modes, layers, _ = a_ref.shape
    columns = mean_ref.shape[-1] // LANES
    masks = lane_masks(layers)
    low_half = masks[0]
    layer = lax.broadcasted_iota(jnp.int32, (layers, LANES), 0)
    zero = jnp.zeros((layers, LANES), jnp.float32)
    weights = [inside[0], inside[0], None, None, inside[1], inside[1]]
    starts = []
    for u in range(6):
        column = jnp.clip(place[0] * OWN_TILES + (u - 2), 0, columns - 1)
        starts.append(pl.multiple_of(column * LANES, LANES))

    def folded(read):
        runs = []
        for start, weight in zip(starts, weights):
            run = read(pl.ds(start, LANES))
            runs.append(run if weight is None else run * weight)
        return [
            runs[2],
            runs[3],
            jnp.where(low_half, runs[4], runs[1]),
            jnp.where(low_half, runs[1], runs[4]),
            jnp.where(low_half, runs[5], runs[0]),
        ]

    spaces = mean_ref.shape[0]
    mean = folded(
        lambda part: jnp.concatenate([mean_ref[i, :, part] for i in range(spaces)], axis=0)
    )
    for k in range(modes):
        values = mean
        if k > 0:
            mode = folded(
                lambda part: jnp.concatenate(
                    [modes_ref[i, k - 1, :, part] for i in range(spaces)], axis=0
                )
            )
            values = [m * value for m, value in zip(mean, mode)]
        sums = plane_sums(values, masks)
        for t in range(FOLDED):
            a_ref[k, :, lanes(t)] = 0.5 * values[t]
        for t in range(FOLDED - 1):
            below = jnp.where(layer > 0, pltpu.roll(values[t], 1, 0), zero)
            above = jnp.where(layer < layers - 1, pltpu.roll(values[t], layers - 1, 0), zero)
            b_ref[k, :, lanes(t)] = 3.0 * values[t] + 0.5 * (sums[t] + (below + above))


def iterate_kernel(
    chaos,
    spaces,
    scales,
    inside,
    mix_ref,
    a_ref,
    b_ref,
    unweight_ref,
    start_ref,
    up_ref,
    down_ref,
    sent_ref,
    r_ref,
    d_ref,
    total_ref,
    edge_ref,
    x_ref,
):
    layers, _, slots, _ = start_ref.shape
    modes = a_ref.shape[0]
    own = slots // chaos
    thick = layers // spaces
    pieces = OWN_TILES * thick
    half = layers // 2
    masks = lane_masks(slots)
    low_half = masks[0]
    mix = mix_ref[...]
    depth = mix.shape[1]

    def send(field, l, t, value):
        i, z = divmod(l, thick)
        value = value * unweight_ref[...]
        for c in range(chaos):
            first = ((c * spaces + i) * 2 + field) * own * pieces + t * thick + z
            sent_ref[pl.ds(first, own, stride=pieces), :] = value[c * own : (c + 1) * own]

    for l in range(layers):
        below, above = up_ref[l], down_ref[l]
        far_below, far_above = up_ref[layers + l % half], down_ref[layers + l % half]
        if l < half:
            far = jnp.where(low_half, far_above, far_below)
        else:
            far = pltpu.roll(jnp.where(low_half, far_below, far_above), NY, 1)
        tiles = [
            start_ref[l, 0],
            start_ref[l, 1],
            jnp.where(low_half, above, below),
            jnp.where(low_half, below, above),
            far,
        ]
        for t, tile in enumerate(tiles):
            if t < FOLDED - 1:
                r_ref[l, t] = tile
            d_ref[l, t] = tile * scales[0]

    for step in range(ITERS):
        count = FOLDED - step
        full = count - 1
        for l in range(layers):
            direct = [d_ref[l, t] for t in range(count)]
            around = neighbour_sums(d_ref, l, count, masks)
            mixed = jnp.dot(
                mix, split_stack(direct + around, depth), preferred_element_type=jnp.float32
            )

            def part(k, n):
                return mixed[(k - 1) * slots : k * slots, n * LANES : (n + 1) * LANES]

            for t in range(count):
                a = a_ref[0, l : l + 1, lanes(t)]
                edge = a * direct[t]
                if t < full:
                    total = b_ref[0, l : l + 1, lanes(t)] * direct[t] - a * around[t]
                for k in range(1, modes):
                    a = a_ref[k, l : l + 1, lanes(t)]
                    edge = edge + a * part(k, t)
                    if t < full:
                        b = b_ref[k, l : l + 1, lanes(t)]
                        total = total + (b * part(k, t) - a * part(k, count + t))
                edge_ref[l, t] = edge
                if t < full:
                    total_ref[l, t] = total
        for l in range(layers):
            spread = neighbour_sums(edge_ref, l, count, masks)
            for t in range(full):
                diffused = total_ref[l, t] - spread[t]
                if t >= OWN_TILES:
                    first, second = inside[(t + 1) % 2], inside[t % 2]
                    diffused = diffused * jnp.where(low_half, first, second)
                residual = r_ref[l, t] - diffused
                if step == ITERS - 1:
                    send(1, l, t, residual)
                    continue
                r_ref[l, t] = residual
                old = d_ref[l, t]
                direction = scales[1 + 2 * step] * old + scales[2 + 2 * step] * residual
                d_ref[l, t] = direction
                if t < OWN_TILES:
                    value = (old if step == 0 else x_ref[l, t]) + direction
                    if step == ITERS - 2:
                        send(0, l, t, value)
                    else:
                        x_ref[l, t] = value


def call(kernel, outs, scalars, arrays, scratch=(), flops=0, copies=False):
    kind = pl.ANY if copies else pltpu.VMEM
    in_specs = [pl.BlockSpec(memory_space=pltpu.SMEM)] * len(scalars) + [
        pl.BlockSpec(memory_space=kind)
    ] * len(arrays)
    moved = sum(4 * x.size for x in arrays) + sum(4 * x.size for x in outs)
    return pl.pallas_call(
        kernel,
        out_shape=outs,
        in_specs=in_specs,
        out_specs=[pl.BlockSpec(memory_space=kind)] * len(outs),
        scratch_shapes=scratch,
        compiler_params=pltpu.CompilerParams(vmem_limit_bytes=40 * 1024 * 1024),
        cost_estimate=pl.CostEstimate(flops=flops, bytes_accessed=moved, transcendentals=0),
    )(*scalars, *arrays)


def coupling_tables(coupling, slot_term):
    bf16 = jnp.bfloat16
    slots = slot_term.shape[0]
    raising = (slot_term[None, None, :] == coupling[:, :, 0:1]).astype(bf16)
    lowering = (slot_term[None, None, :] == coupling[:, :, 1:2]).astype(bf16)
    weighted = raising * coupling[:, :, 2:3].astype(bf16)
    matrices = jnp.einsum(
        "kps,kpr->ksr", weighted, lowering, preferred_element_type=jnp.float32
    ) + jnp.einsum("kps,kpr->ksr", lowering, raising, preferred_element_type=jnp.float32)
    spare = -slots % 16
    matrices = jnp.pad(matrices.astype(bf16), ((0, 0), (0, 0), (0, spare)))
    matrices = matrices.reshape(-1, slots + spare)
    degree = jnp.sum(weighted.astype(jnp.float32), axis=1)
    factorial = jnp.where(degree > 2.5, 6.0, jnp.where(degree > 1.5, 2.0, 1.0))
    scale = jnp.sqrt(jnp.prod(factorial, axis=0))
    occupied = (slot_term >= 0).astype(jnp.float32)
    spread = jnp.ones((1, LANES), jnp.float32)
    return (
        jnp.concatenate([matrices, matrices], axis=1),
        (occupied * scale)[:, None] * spread,
        (occupied / scale)[:, None] * spread,
    )


def local_by_cells(source_chaos_terms, mean_conductivity, mode_shapes, coupling, slot_term, bounds):
    own, thick, cells = source_chaos_terms.shape
    chaos, spaces = lax.axis_size("chaos"), lax.axis_size("space")
    devices = chaos * spaces
    slots = own * chaos
    layers = thick * spaces
    columns = cells // LANES
    pieces = OWN_TILES * thick
    blocks = [block_of(device, spaces) for device in range(devices)]
    f32 = jnp.float32

    def shape(*sizes):
        return jax.ShapeDtypeStruct(sizes, f32)

    rows = source_chaos_terms.reshape(own, thick, columns, LANES)
    rows = jnp.transpose(rows, (0, 2, 1, 3)).reshape(own, devices, pieces, LANES)
    scattered = call(
        functools.partial(scatter_kernel, blocks),
        [shape(devices, own, pieces, LANES)],
        [],
        [rows],
        [pltpu.SemaphoreType.DMA((devices,))],
        copies=True,
    )[0]
    gathered = lax.all_to_all(scattered, BOTH, 0, 0, tiled=True).reshape(-1, LANES)

    mean = lax.all_gather(mean_conductivity, "space")
    modes = lax.all_gather(mode_shapes, "space")
    row, column = lax.axis_index("chaos"), lax.axis_index("space")
    block = row * spaces + jnp.where(row % 2 == 0, column, spaces - 1 - column)
    inside = jnp.stack([block > 0, block < devices - 1]).astype(f32)
    count = mode_shapes.shape[0] + 1
    a, b = call(
        coefficient_kernel,
        [shape(count, layers, FOLDED * LANES), shape(count, layers, (FOLDED - 1) * LANES)],
        [block[None], inside],
        [mean, modes],
    )

    mix, weight, unweight = coupling_tables(coupling, slot_term)
    midpoint = 0.5 * (bounds[1] + bounds[0])
    half_span = 0.5 * (bounds[1] - bounds[0])
    sigma_one = midpoint / half_span
    rho_now = 1.0 / sigma_one
    scales = [1.0 / midpoint]
    for _ in range(ITERS - 1):
        rho_next = 1.0 / (2.0 * sigma_one - rho_now)
        scales += [rho_next * rho_now, 2.0 * rho_next / half_span]
        rho_now = rho_next
    scales = jnp.stack(scales)

    message = shape(layers + layers // 2, slots, LANES)
    start, up, down = call(
        functools.partial(start_kernel, chaos, spaces),
        [shape(layers, OWN_TILES, slots, LANES), message, message],
        [],
        [weight, gathered],
    )
    place = {n: device for device, n in enumerate(blocks)}
    upward = [(place[n], place[n + 1]) for n in range(devices - 1)]
    downward = [(place[n + 1], place[n]) for n in range(devices - 1)]
    from_below = lax.ppermute(up, BOTH, upward)
    from_above = lax.ppermute(down, BOTH, downward)

    def held(tiles):
        return pltpu.VMEM((layers, tiles, slots, LANES), f32)

    sent = call(
        functools.partial(iterate_kernel, chaos, spaces),
        [shape(devices * 2 * own * pieces, LANES)],
        [scales, inside],
        [mix, a, b, unweight, start, from_below, from_above],
        [held(FOLDED - 1), held(FOLDED), held(FOLDED - 1), held(FOLDED), held(OWN_TILES)],
        flops=10000000000,
    )[0]
    sent = sent.reshape(devices, 2, own, pieces, LANES)
    received = lax.all_to_all(sent, BOTH, 0, 0, tiled=True)
    outs = call(
        functools.partial(collect_kernel, blocks),
        [shape(own, devices, pieces, LANES)] * 2,
        [],
        [received],
        [pltpu.SemaphoreType.DMA((2, devices))],
        copies=True,
    )
    return tuple(
        jnp.transpose(out.reshape(own, columns, thick, LANES), (0, 2, 1, 3)).reshape(
            own, thick, cells
        )
        for out in outs
    )


def local(source_chaos_terms, mean_conductivity, mode_shapes, coupling, slot_term, bounds):
    own, thick, cells = source_chaos_terms.shape
    chaos, spaces = lax.axis_size("chaos"), lax.axis_size("space")
    fits = (
        thick * spaces == 8
        and cells == chaos * spaces * OWN_TILES * LANES
        and (own * chaos) % 8 == 0
    )
    plan = local_by_cells if fits else local_by_slots
    return plan(
        source_chaos_terms, mean_conductivity, mode_shapes, coupling, slot_term, bounds
    )


def solution(mesh):
    in_specs = (
        P(("groups", "chaos"), "space", None),
        P("space", None),
        P(None, "space", None),
        P(),
        P(),
        P("groups"),
    )
    out_specs = (P(("groups", "chaos"), "space", None), P(("groups", "chaos"), "space", None))
    return jax.shard_map(local, mesh=mesh, in_specs=in_specs, out_specs=out_specs, check_vma=False)
```

profile of v0, /device:TPU:1, one launch (start us, length us, event | category | flops | bytes accessed | tf_op | source)
XLA Modules:
  0.0 108.2 jit_solution(11842932419748442512)
XLA Ops:
  0.6 0.0 copy-start
  0.6 1.1 %copy-done = f32[22,2,4096]{2,1,0:T(2,128)S(1)} copy-done((f32[22,2,4096]{2,1,0:T(2,128)S(1)}, f32[22,2,4096]{2,1,0:T(2,128)}, u32[]{:S(2)}) %copy-start) | copy-done | bytes 720920
  1.7 0.0 copy-start.4
  1.7 0.0 copy-start.3
  1.7 0.0 copy-start.2
  1.7 1.0 shard_map.78
  2.7 0.0 copy-start.1
  2.7 7.3 %all-to-all-start = ((f32[16,22,4,128]{3,2,1,0:T(4,128)}), f32[16,22,4,128]{3,2,1,0:T(4,128)S(1)}, u32[]{:S(2)}, u32[]{:S(2)}) async-start(f32[16,22,4,128]{3,2,1,0:T(4,128)} %shard_map.78), calls=%async_computation | async-start | bytes 1441792 | tf_op jit(solution)/shard_map/all_to_all | solution.py:449
  10.1 0.0 copy-done.4
  10.1 0.6 fusion.17
  10.7 0.0 copy-done.3
  10.7 0.0 copy-done.2
  10.7 0.1 convert_reduce_fusion
  10.9 0.4 fusion.2
  11.3 0.4 fusion
  11.8 15.7 %all-to-all-done = f32[16,22,4,128]{3,2,1,0:T(4,128)S(1)} async-done(((f32[16,22,4,128]{3,2,1,0:T(4,128)}), f32[16,22,4,128]{3,2,1,0:T(4,128)S(1)}, u32[]{:S(2)}, u32[]{:S(2)}) %all-to-all-start) | async-done | bytes 720928 | tf_op jit(solution)/shard_map/all_to_all | solution.py:449
  27.5 0.1 mul.68.weight_ref
  27.6 0.2 shard_map.79
  27.8 2.8 %collective-permute-start = (f32[12,88,128]{2,1,0:T(8,128)S(1)}, f32[12,88,128]{2,1,0:T(8,128)S(1)}, u32[]{:S(2)}, u32[]{:S(2)}) collective-permute-start(f32[12,88,128]{2,1,0:T(8,128)S(1)} %get-tuple-element.12), channel_id=1, source_target_pairs={{0,1},{1,2},{2,3},{3,7},{7,6},{6,5},{5,4},{4,8},{8,9},{9,10},{10,1... | collective-permute-start | bytes 1622024 | tf_op jit(solution)/shard_map/ppermute | solution.py:486
  30.6 1.9 %collective-permute-start.1 = (f32[12,88,128]{2,1,0:T(8,128)S(1)}, f32[12,88,128]{2,1,0:T(8,128)S(1)}, u32[]{:S(2)}, u32[]{:S(2)}) collective-permute-start(f32[12,88,128]{2,1,0:T(8,128)S(1)} %get-tuple-element.13), channel_id=1, source_target_pairs={{1,0},{2,1},{3,2},{7,3},{6,7},{5,6},{4,5},{8,4},{9,8},{10,9},{11,1... | collective-permute-start | bytes 1622024 | tf_op jit(solution)/shard_map/ppermute | solution.py:487
  32.5 0.0 copy-done.1
  32.5 10.8 %all-gather.2.mean_ref = f32[4,2,4096]{2,1,0:T(2,128)S(1)} all-gather(f32[1,2,4096]{2,1,0:T(2,128)S(1)} %bitcast.41), channel_id=2, replica_groups=mesh['groups'=2,'chaos'=4,'space'=4] {'space'}, dimensions={0}, use_global_device_ids=true | all-gather | bytes 163840 | tf_op jit(solution)/shard_map/all_gather | solution.py:451
  46.2 0.1 add_convert_fusion.inside
  46.3 8.9 %all-gather.1 = f32[24,2,4096]{2,1,0:T(2,128)S(1)} all-gather(f32[6,2,4096]{2,1,0:T(2,128)} %param.8), channel_id=3, replica_groups=mesh['groups'=2,'chaos'=4,'space'=4] {'space'}, dimensions={0}, use_global_device_ids=true | all-gather | bytes 983040 | tf_op jit(solution)/shard_map/all_gather | solution.py:452
  55.2 0.7 shard_map.77
  55.9 0.1 stack.32.scales
  56.0 0.1 pad_maximum_fusion.mix_ref
  56.2 0.0 collective-permute-done.up_ref
  56.2 0.0 collective-permute-done.1.down_ref
  56.2 0.1 mul.66.unweight_ref
  56.3 13.1 %shard_map.80 = f32[2816,128]{1,0:T(8,128)S(1)} custom-call(f32[5]{0:T(128)S(1)} %stack.32.scales, f32[2]{0:T(128)S(1)} %add_convert_fusion.inside, bf16[528,192]{1,0:T(8,128)(2,1)S(1)} %pad_maximum_fusion.mix_ref, f32[7,8,640]{2,1,0:T(8,128)S(1)} %get-tuple-element.9.a_ref, f32[7,8,512]{2,1,0:T(8,128)S(1)} %get-tuple-element.10.b_ref, ...), custom_call_target="tpu_custom_call" | custom-call | flops 10000000000 | bytes 3952640 | tf_op jit(solution)/shard_map/pallas_call | solution.py:390
  69.4 37.5 %all_to_all.10.in_ref = f32[16,2,22,4,128]{4,3,2,1,0:T(4,128)S(1)} all-to-all(f32[16,2,22,4,128]{4,3,2,1,0:T(4,128)S(1)} %bitcast.38), channel_id=1, replica_groups=mesh['groups'=2,'chaos'=4,'space'=4] {'chaos','space'}, dimensions={0} | all-to-all | bytes 2883584 | tf_op jit(solution)/shard_map/all_to_all | solution.py:501
  106.9 1.4 %shard_map.81 = (f32[22,16,4,128]{3,2,1,0:T(4,128)}, f32[22,16,4,128]{3,2,1,0:T(4,128)}) custom-call(f32[16,2,22,4,128]{4,3,2,1,0:T(4,128)S(1)} %all_to_all.10.in_ref), custom_call_target="tpu_custom_call" | custom-call | bytes 2883584 | tf_op jit(solution)/shard_map/pallas_call | solution.py:390
  (6 shorter events, 0.1 us)
Async XLA Ops:
  0.6 1.1 %copy-start = (f32[22,2,4096]{2,1,0:T(2,128)S(1)}, f32[22,2,4096]{2,1,0:T(2,128)}, u32[]{:S(2)}) copy-start(f32[22,2,4096]{2,1,0:T(2,128)} %param.6) | copy-start | bytes 2162692
  1.7 8.3 %copy-start.4 = (f32[2]{0:T(128)S(1)}, f32[2]{0:T(128)}, u32[]{:S(2)}) copy-start(f32[2]{0:T(128)} %param.11) | copy-start | bytes 28
  1.7 9.0 %copy-start.3 = (s32[6,28,3]{1,2,0:T(4,128)S(1)}, s32[6,28,3]{1,2,0:T(4,128)}, u32[]{:S(2)}) copy-start(s32[6,28,3]{1,2,0:T(4,128)} %param.9) | copy-start | bytes 6052
  1.7 9.0 %copy-start.2 = (s32[88]{0:T(128)S(1)}, s32[88]{0:T(128)}, u32[]{:S(2)}) copy-start(s32[88]{0:T(128)} %param.10) | copy-start | bytes 1060
  2.7 29.8 %copy-start.1 = (f32[2,4096]{1,0:T(2,128)S(1)}, f32[2,4096]{1,0:T(2,128)}, u32[]{:S(2)}) copy-start(f32[2,4096]{1,0:T(2,128)} %param.7) | copy-start | bytes 98308
  2.7 24.7 %all-to-all-start = ((f32[16,22,4,128]{3,2,1,0:T(4,128)}), f32[16,22,4,128]{3,2,1,0:T(4,128)S(1)}, u32[]{:S(2)}, u32[]{:S(2)}) async-start(f32[16,22,4,128]{3,2,1,0:T(4,128)} %shard_map.78), calls=%async_computation | async-start | bytes 1441792 | tf_op jit(solution)/shard_map/all_to_all | solution.py:449
  27.8 28.4 %collective-permute-start = (f32[12,88,128]{2,1,0:T(8,128)S(1)}, f32[12,88,128]{2,1,0:T(8,128)S(1)}, u32[]{:S(2)}, u32[]{:S(2)}) collective-permute-start(f32[12,88,128]{2,1,0:T(8,128)S(1)} %get-tuple-element.12), channel_id=1, source_target_pairs={{0,1},{1,2},{2,3},{3,7},{7,6},{6,5},{5,4},{4,8},{8,9},{9,10},{10,1... | collective-permute-start | bytes 1622024 | tf_op jit(solution)/shard_map/ppermute | solution.py:486
  30.6 25.6 %collective-permute-start.1 = (f32[12,88,128]{2,1,0:T(8,128)S(1)}, f32[12,88,128]{2,1,0:T(8,128)S(1)}, u32[]{:S(2)}, u32[]{:S(2)}) collective-permute-start(f32[12,88,128]{2,1,0:T(8,128)S(1)} %get-tuple-element.13), channel_id=1, source_target_pairs={{1,0},{2,1},{3,2},{7,3},{6,7},{5,6},{4,5},{8,4},{9,8},{10,9},{11,1... | collective-permute-start | bytes 1622024 | tf_op jit(solution)/shard_map/ppermute | solution.py:487
where the time goes:
time: 109 us; the launch traced here: 108 us
  blocking collectives  57.2 us (52%)
  Pallas kernels  16.4 us (15%)
  waiting for transfers between devices  15.7 us (14%)
  starting transfers between devices  12 us (11%)
  between operations  3.65 us (3%)
  local copies, waits for them, and re-layouts  2 us (2%)
    all_to_all x1, blocking collectives, local_by_cells(): received = lax.all_to_all(sent, BOTH, 0, 0, tiled=True)  37.5 us
    pallas_call x5, Pallas kernels, call(): pl.pallas_call(kernel, out_shape=outs, in_specs=in_specs, out_specs=[pl.B...  16.4 us
    all_to_all x1, waiting for transfers between devices, local_by_cells(): lax.all_to_all(scattered, BOTH, 0, 0, tiled=True).reshape(-1, LANES)  15.7 us
    all_gather x1, blocking collectives, local_by_cells(): mean = lax.all_gather(mean_conductivity, 'space')  10.8 us
    all_gather x1, blocking collectives, local_by_cells(): modes = lax.all_gather(mode_shapes, 'space')  8.92 us
    all_to_all x1, starting transfers between devices, local_by_cells(): lax.all_to_all(scattered, BOTH, 0, 0, tiled=True).reshape(-1, LANES)  7.33 us
    ppermute x1, starting transfers between devices, local_by_cells(): from_below = lax.ppermute(up, BOTH, upward)  2.78 us
  transfers between devices with their start and end apart: 3, of which 1 were waited for; matrix products, arithmetic and copies ran while one was open for 2% of the time, Pallas kernels for 1%

commit v1 on v0

--- a/solution.py
+++ b/solution.py
@@ -174,13 +174,31 @@
         copy.wait()
 
 
-def scatter_kernel(blocks, in_ref, out_ref, sems):
-    run_copies(
-        [
-            pltpu.make_async_copy(in_ref.at[:, block], out_ref.at[device], sems.at[device])
-            for device, block in enumerate(blocks)
-        ]
-    )
+def scatter_kernel(blocks, chaos_index, in_ref, mean_ref, modes_ref, out_ref, sems):
+    own, devices, pieces, _ = in_ref.shape
+    modes = modes_ref.shape[0] // (devices * pieces)
+    copies = [
+        pltpu.make_async_copy(
+            in_ref.at[:, block], out_ref.at[device, pl.ds(0, own)], sems.at[device]
+        )
+        for device, block in enumerate(blocks)
+    ]
+    for copy in copies:
+        copy.start()
+    for device, block in enumerate(blocks):
+        row = block * pieces + chaos_index[0]
+        values = modes_ref[pl.ds(row, modes, stride=devices * pieces), :]
+        out_ref[device, own] = values[:pieces]
+        out_ref[device, own + 1] = jnp.concatenate(
+            [
+                values[pieces:],
+                mean_ref[pl.ds(row, 1), :],
+                jnp.zeros((2 * pieces - modes - 1, LANES), jnp.float32),
+            ],
+            axis=0,
+        )
+    for copy in copies:
+        copy.wait()
 
 
 def collect_kernel(blocks, in_ref, *rest):
@@ -196,83 +214,60 @@
     )
 
 
-def start_kernel(chaos, spaces, weight_ref, in_ref, residual_ref, up_ref, down_ref):
+def start_kernel(chaos, spaces, modes, weight_ref, in_ref, residual_ref, a_ref, up_ref, down_ref):
     layers, tiles, slots, _ = residual_ref.shape
     own = slots // chaos
     thick = layers // spaces
     pieces = tiles * thick
+    block = (own + 2) * pieces
     half = layers // 2
     low_half = lane_masks(slots)[0]
     weight = weight_ref[...]
+
+    def put(ref, place, value):
+        ref[pl.ds(place * slots, slots), :] = value
+
     for l in range(layers):
         i, z = divmod(l, thick)
         for t in range(tiles):
             first = t * thick + z
             residual_ref[l, t] = weight * jnp.concatenate(
                 [
-                    in_ref[pl.ds((c * spaces + i) * own * pieces + first, own, stride=pieces), :]
+                    in_ref[pl.ds((c * spaces + i) * block + first, own, stride=pieces), :]
                     for c in range(chaos)
                 ],
                 axis=0,
             )
-        up_ref[l] = residual_ref[l, 1]
-        down_ref[l] = residual_ref[l, 0]
+        put(up_ref, l, residual_ref[l, 1])
+        put(down_ref, l, residual_ref[l, 0])
     for l in range(half):
         later = l + half
-        up_ref[layers + l] = jnp.where(
-            low_half, pltpu.roll(residual_ref[later, 0], NY, 1), residual_ref[l, 0]
-        )
-        down_ref[layers + l] = jnp.where(
-            low_half, residual_ref[l, 1], pltpu.roll(residual_ref[later, 1], NY, 1)
-        )
-
-
-def coefficient_kernel(place, inside, mean_ref, modes_ref, a_ref, b_ref):
-    modes, layers, _ = a_ref.shape
-    columns = mean_ref.shape[-1] // LANES
-    masks = lane_masks(layers)
-    low_half = masks[0]
-    layer = lax.broadcasted_iota(jnp.int32, (layers, LANES), 0)
-    zero = jnp.zeros((layers, LANES), jnp.float32)
-    weights = [inside[0], inside[0], None, None, inside[1], inside[1]]
-    starts = []
-    for u in range(6):
-        column = jnp.clip(place[0] * OWN_TILES + (u - 2), 0, columns - 1)
-        starts.append(pl.multiple_of(column * LANES, LANES))
-
-    def folded(read):
-        runs = []
-        for start, weight in zip(starts, weights):
-            run = read(pl.ds(start, LANES))
-            runs.append(run if weight is None else run * weight)
-        return [
-            runs[2],
-            runs[3],
-            jnp.where(low_half, runs[4], runs[1]),
-            jnp.where(low_half, runs[1], runs[4]),
-            jnp.where(low_half, runs[5], runs[0]),
-        ]
-
-    spaces = mean_ref.shape[0]
-    mean = folded(
-        lambda part: jnp.concatenate([mean_ref[i, :, part] for i in range(spaces)], axis=0)
-    )
-    for k in range(modes):
-        values = mean
-        if k > 0:
-            mode = folded(
-                lambda part: jnp.concatenate(
-                    [modes_ref[i, k - 1, :, part] for i in range(spaces)], axis=0
-                )
-            )
-            values = [m * value for m, value in zip(mean, mode)]
-        sums = plane_sums(values, masks)
-        for t in range(FOLDED):
-            a_ref[k, :, lanes(t)] = 0.5 * values[t]
-        for t in range(FOLDED - 1):
-            below = jnp.where(layer > 0, pltpu.roll(values[t], 1, 0), zero)
-            above = jnp.where(layer < layers - 1, pltpu.roll(values[t], layers - 1, 0), zero)
-            b_ref[k, :, lanes(t)] = 3.0 * values[t] + 0.5 * (sums[t] + (below + above))
+        put(
+            up_ref,
+            layers + l,
+            jnp.where(low_half, pltpu.roll(residual_ref[later, 0], NY, 1), residual_ref[l, 0]),
+        )
+        put(
+            down_ref,
+            layers + l,
+            jnp.where(low_half, residual_ref[l, 1], pltpu.roll(residual_ref[later, 1], NY, 1)),
+        )
+
+    for t in range(tiles):
+        for z in range(thick):
+            for k in range(modes):
+                first = (t * thick + z) * spaces * block + own * pieces
+                first += k - 1 if k > 0 else modes - 1
+                a_ref[k, t, pl.ds(z, spaces, stride=thick), :] = in_ref[
+                    pl.ds(first, spaces, stride=block), :
+                ]
+        mean = 0.5 * a_ref[0, t]
+        for k in range(modes):
+            value = mean if k == 0 else mean * a_ref[k, t]
+            a_ref[k, t] = value
+            rows = pl.ds((layers + half) * slots + (k * tiles + t) * layers, layers)
+            up_ref[rows, :] = value
+            down_ref[rows, :] = value
 
 
 def iterate_kernel(
@@ -281,13 +276,14 @@
     scales,
     inside,
     mix_ref,
-    a_ref,
-    b_ref,
+    own_a_ref,
     unweight_ref,
     start_ref,
     up_ref,
     down_ref,
     sent_ref,
+    a_ref,
+    b_ref,
     r_ref,
     d_ref,
     total_ref,
@@ -295,7 +291,7 @@
     x_ref,
 ):
     layers, _, slots, _ = start_ref.shape
-    modes = a_ref.shape[0]
+    modes = own_a_ref.shape[0]
     own = slots // chaos
     thick = layers // spaces
     pieces = OWN_TILES * thick
@@ -312,9 +308,40 @@
             first = ((c * spaces + i) * 2 + field) * own * pieces + t * thick + z
             sent_ref[pl.ds(first, own, stride=pieces), :] = value[c * own : (c + 1) * own]
 
+    layer = lax.broadcasted_iota(jnp.int32, (layers, LANES), 0)
+    zero = jnp.zeros((layers, LANES), jnp.float32)
+    narrow_masks = lane_masks(layers)
+    low = narrow_masks[0]
+    for k in range(modes):
+        below, above = [
+            [
+                ref[pl.ds((layers + half) * slots + (k * OWN_TILES + t) * layers, layers), :]
+                for t in range(OWN_TILES)
+            ]
+            for ref in (up_ref, down_ref)
+        ]
+        values = [
+            own_a_ref[k, 0],
+            own_a_ref[k, 1],
+            jnp.where(low, above[0], below[1]),
+            jnp.where(low, below[1], above[0]),
+            jnp.where(low, above[1], below[0]),
+        ]
+        sums = plane_sums(values, narrow_masks)
+        for t in range(FOLDED):
+            a_ref[k, :, lanes(t)] = values[t]
+        for t in range(FOLDED - 1):
+            under = jnp.where(layer > 0, pltpu.roll(values[t], 1, 0), zero)
+            over = jnp.where(layer < layers - 1, pltpu.roll(values[t], layers - 1, 0), zero)
+            b_ref[k, :, lanes(t)] = 6.0 * values[t] + (sums[t] + (under + over))
+
+    def message(ref, place):
+        return ref[pl.ds(place * slots, slots), :]
+
     for l in range(layers):
-        below, above = up_ref[l], down_ref[l]
-        far_below, far_above = up_ref[layers + l % half], down_ref[layers + l % half]
+        below, above = message(up_ref, l), message(down_ref, l)
+        far_below = message(up_ref, layers + l % half)
+        far_above = message(down_ref, layers + l % half)
         if l < half:
             far = jnp.where(low_half, far_above, far_below)
         else:
@@ -342,7 +369,13 @@
             )
 
             def part(k, n):
-                return mixed[(k - 1) * slots : k * slots, n * LANES : (n + 1) * LANES]
+                return jnp.concatenate(
+                    [
+                        mixed[row : row + 8, n * LANES : (n + 1) * LANES]
+                        for row in range((k - 1) * 8, (modes - 1) * slots, (modes - 1) * 8)
+                    ],
+                    axis=0,
+                )
 
             for t in range(count):
                 a = a_ref[0, l : l + 1, lanes(t)]
@@ -381,17 +414,17 @@
                         x_ref[l, t] = value
 
 
-def call(kernel, outs, scalars, arrays, scratch=(), flops=0, copies=False):
-    kind = pl.ANY if copies else pltpu.VMEM
+def call(kernel, outs, scalars, arrays, scratch=(), flops=0, in_kinds=None, out_kind=pltpu.VMEM):
+    kinds = in_kinds or [pltpu.VMEM] * len(arrays)
     in_specs = [pl.BlockSpec(memory_space=pltpu.SMEM)] * len(scalars) + [
-        pl.BlockSpec(memory_space=kind)
-    ] * len(arrays)
+        pl.BlockSpec(memory_space=kind) for kind in kinds
+    ]
     moved = sum(4 * x.size for x in arrays) + sum(4 * x.size for x in outs)
     return pl.pallas_call(
         kernel,
         out_shape=outs,
         in_specs=in_specs,
-        out_specs=[pl.BlockSpec(memory_space=kind)] * len(outs),
+        out_specs=[pl.BlockSpec(memory_space=out_kind)] * len(outs),
         scratch_shapes=scratch,
         compiler_params=pltpu.CompilerParams(vmem_limit_bytes=40 * 1024 * 1024),
         cost_estimate=pl.CostEstimate(flops=flops, bytes_accessed=moved, transcendentals=0),
@@ -409,6 +442,7 @@
     ) + jnp.einsum("kps,kpr->ksr", lowering, raising, preferred_element_type=jnp.float32)
     spare = -slots % 16
     matrices = jnp.pad(matrices.astype(bf16), ((0, 0), (0, 0), (0, spare)))
+    matrices = matrices.reshape(-1, slots // 8, 8, slots + spare).transpose(1, 0, 2, 3)
     matrices = matrices.reshape(-1, slots + spare)
     degree = jnp.sum(weighted.astype(jnp.float32), axis=1)
     factorial = jnp.where(degree > 2.5, 6.0, jnp.where(degree > 1.5, 2.0, 1.0))
@@ -436,30 +470,28 @@
     def shape(*sizes):
         return jax.ShapeDtypeStruct(sizes, f32)
 
-    rows = source_chaos_terms.reshape(own, thick, columns, LANES)
-    rows = jnp.transpose(rows, (0, 2, 1, 3)).reshape(own, devices, pieces, LANES)
-    scattered = call(
-        functools.partial(scatter_kernel, blocks),
-        [shape(devices, own, pieces, LANES)],
-        [],
-        [rows],
-        [pltpu.SemaphoreType.DMA((devices,))],
-        copies=True,
-    )[0]
-    gathered = lax.all_to_all(scattered, BOTH, 0, 0, tiled=True).reshape(-1, LANES)
-
-    mean = lax.all_gather(mean_conductivity, "space")
-    modes = lax.all_gather(mode_shapes, "space")
+    def by_blocks(field):
+        lead = field.shape[:-2]
+        tiled = field.reshape(*lead, thick, columns, LANES)
+        return jnp.swapaxes(tiled, -3, -2)
+
     row, column = lax.axis_index("chaos"), lax.axis_index("space")
     block = row * spaces + jnp.where(row % 2 == 0, column, spaces - 1 - column)
     inside = jnp.stack([block > 0, block < devices - 1]).astype(f32)
-    count = mode_shapes.shape[0] + 1
-    a, b = call(
-        coefficient_kernel,
-        [shape(count, layers, FOLDED * LANES), shape(count, layers, (FOLDED - 1) * LANES)],
-        [block[None], inside],
-        [mean, modes],
-    )
+    modes = mode_shapes.shape[0] + 1
+    scattered = call(
+        functools.partial(scatter_kernel, blocks),
+        [shape(devices, own + 2, pieces, LANES)],
+        [row[None]],
+        [
+            by_blocks(source_chaos_terms).reshape(own, devices, pieces, LANES),
+            by_blocks(mean_conductivity).reshape(-1, LANES),
+            by_blocks(mode_shapes).reshape(-1, LANES),
+        ],
+        [pltpu.SemaphoreType.DMA((devices,))],
+        in_kinds=[pltpu.HBM, pltpu.VMEM, pltpu.VMEM],
+    )[0]
+    gathered = lax.all_to_all(scattered, BOTH, 0, 0, tiled=True).reshape(-1, LANES)
 
     mix, weight, unweight = coupling_tables(coupling, slot_term)
     midpoint = 0.5 * (bounds[1] + bounds[0])
@@ -473,10 +505,15 @@
         rho_now = rho_next
     scales = jnp.stack(scales)
 
-    message = shape(layers + layers // 2, slots, LANES)
-    start, up, down = call(
-        functools.partial(start_kernel, chaos, spaces),
-        [shape(layers, OWN_TILES, slots, LANES), message, message],
+    message = shape((layers + layers // 2) * slots + modes * OWN_TILES * layers, LANES)
+    start, own_a, up, down = call(
+        functools.partial(start_kernel, chaos, spaces, modes),
+        [
+            shape(layers, OWN_TILES, slots, LANES),
+            shape(modes, OWN_TILES, layers, LANES),
+            message,
+            message,
+        ],
         [],
         [weight, gathered],
     )
@@ -493,8 +530,16 @@
         functools.partial(iterate_kernel, chaos, spaces),
         [shape(devices * 2 * own * pieces, LANES)],
         [scales, inside],
-        [mix, a, b, unweight, start, from_below, from_above],
-        [held(FOLDED - 1), held(FOLDED), held(FOLDED - 1), held(FOLDED), held(OWN_TILES)],
+        [mix, own_a, unweight, start, from_below, from_above],
+        [
+            pltpu.VMEM((modes, layers, FOLDED * LANES), f32),
+            pltpu.VMEM((modes, layers, (FOLDED - 1) * LANES), f32),
+            held(FOLDED - 1),
+            held(FOLDED),
+            held(FOLDED - 1),
+            held(FOLDED),
+            held(OWN_TILES),
+        ],
         flops=10000000000,
     )[0]
     sent = sent.reshape(devices, 2, own, pieces, LANES)
@@ -505,7 +550,8 @@
         [],
         [received],
         [pltpu.SemaphoreType.DMA((2, devices))],
-        copies=True,
+        in_kinds=[pl.ANY],
+        out_kind=pltpu.HBM,
     )
     return tuple(
         jnp.transpose(out.reshape(own, columns, thick, LANES), (0, 2, 1, 3)).reshape(
@@ -522,6 +568,8 @@
         thick * spaces == 8
         and cells == chaos * spaces * OWN_TILES * LANES
         and (own * chaos) % 8 == 0
+        and chaos == OWN_TILES * thick
+        and chaos <= mode_shapes.shape[0] < 2 * chaos
     )
     plan = local_by_cells if fits else local_by_slots
     return plan(

time: 109 us -> 100 us (0.917)
  blocking collectives: 57.2 us -> 39.4 us
  waiting for transfers between devices: 15.7 us -> 23 us
  local copies, waits for them, and re-layouts: 2 us -> 3.68 us
    all_gather x2 -> x0, blocking collectives: 19.7 us -> none  [the longest x1 10.8 us: local_by_cells(): mean = lax.all_gather(mean_conductivity, 'space')]
    ppermute x1, waiting for transfers between devices: 0.01 us -> 4.4 us  [local_by_cells(): from_above = lax.ppermute(down, BOTH, downward)]
    all_to_all x1, waiting for transfers between devices: 15.7 us -> 17.9 us  [local_by_cells(): lax.all_to_all(scattered, BOTH, 0, 0, tiled=True).reshape(-1, LANES)]
    all_to_all x1, blocking collectives: 37.5 us -> 39.4 us  [local_by_cells(): received = lax.all_to_all(sent, BOTH, 0, 0, tiled=True)]
    unnamed x10 -> x12, local copies, waits for them, and re-layouts: 1.12 us -> 2.8 us
    pallas_call x5 -> x4, Pallas kernels: 16.4 us -> 16.6 us  [call(): pl.pallas_call(kernel, out_shape=outs, in_specs=in_specs, out_specs=[pl.B...]
  transfers between devices with their start and end apart: 3 -> 3, of which waited for: 1 -> 3; matrix products, arithmetic and copies ran while one was open for 2% -> 2% of each run, Pallas kernels for 1% -> 0%
where the time goes in v1:
time: 100 us; the launch traced here: 99.6 us
  blocking collectives  39.4 us (39%)
  waiting for transfers between devices  23 us (23%)
  Pallas kernels  16.6 us (17%)
  starting transfers between devices  12.1 us (12%)
  local copies, waits for them, and re-layouts  3.68 us (4%)
  between operations  3.66 us (4%)
    all_to_all x1, blocking collectives, local_by_cells(): received = lax.all_to_all(sent, BOTH, 0, 0, tiled=True)  39.4 us
    all_to_all x1, waiting for transfers between devices, local_by_cells(): lax.all_to_all(scattered, BOTH, 0, 0, tiled=True).reshape(-1, LANES)  17.9 us
    pallas_call x4, Pallas kernels, call(): pl.pallas_call(kernel, out_shape=outs, in_specs=in_specs, out_specs=[pl.B...  16.6 us
    all_to_all x1, starting transfers between devices, local_by_cells(): lax.all_to_all(scattered, BOTH, 0, 0, tiled=True).reshape(-1, LANES)  7.33 us
    ppermute x1, waiting for transfers between devices, local_by_cells(): from_above = lax.ppermute(down, BOTH, downward)  4.4 us
    ppermute x1, starting transfers between devices, local_by_cells(): from_below = lax.ppermute(up, BOTH, upward)  2.87 us
    unnamed x12, local copies, waits for them, and re-layouts  2.8 us
  transfers between devices with their start and end apart: 3, of which 3 were waited for; matrix products, arithmetic and copies ran while one was open for 2% of the time, Pallas kernels for 0%

profile of v1, /device:TPU:1, one launch (start us, length us, event | category | flops | bytes accessed | tf_op | source)
XLA Modules:
  0.0 99.6 jit_solution(2271950968427141075)
XLA Ops:
  0.6 0.0 copy-start
  0.6 1.1 %copy-done = f32[22,2,4096]{2,1,0:T(2,128)S(1)} copy-done((f32[22,2,4096]{2,1,0:T(2,128)S(1)}, f32[22,2,4096]{2,1,0:T(2,128)}, u32[]{:S(2)}) %copy-start) | copy-done | bytes 720920
  1.7 0.0 copy-start.1
  1.8 0.9 copy-done.1
  2.7 0.0 copy-start.2
  2.7 0.8 copy-done.2
  3.4 0.0 copy-start.4
  3.4 0.0 copy-start.3
  3.4 1.3 %shard_map.77 = f32[16,24,4,128]{3,2,1,0:T(4,128)} custom-call(s32[1]{0:T(128)} %bitcast.15.chaos_index, f32[22,16,4,128]{3,2,1,0:T(4,128)S(1)} %bitcast.50, f32[64,128]{1,0:T(8,128)S(1)} %bitcast.52, f32[384,128]{1,0:T(8,128)S(1)} %bitcast.51), custom_call_target="tpu_custom_call" | custom-call | bytes 1736704 | tf_op jit(solution)/shard_map/pallas_call | solution.py:423
  4.7 0.0 copy-start.5
  4.7 7.3 %all-to-all-start = ((f32[16,24,4,128]{3,2,1,0:T(4,128)}), f32[16,24,4,128]{3,2,1,0:T(4,128)S(1)}, u32[]{:S(2)}, u32[]{:S(2)}) async-start(f32[16,24,4,128]{3,2,1,0:T(4,128)} %shard_map.77), calls=%async_computation | async-start | bytes 1572864 | tf_op jit(solution)/shard_map/all_to_all | solution.py:494
  12.1 0.0 copy-done.4
  12.1 0.0 copy-done.3
  12.1 0.1 convert_reduce_fusion
  12.3 0.4 fusion.2
  12.7 17.9 %all-to-all-done = f32[16,24,4,128]{3,2,1,0:T(4,128)S(1)} async-done(((f32[16,24,4,128]{3,2,1,0:T(4,128)}), f32[16,24,4,128]{3,2,1,0:T(4,128)S(1)}, u32[]{:S(2)}, u32[]{:S(2)}) %all-to-all-start) | async-done | bytes 786464 | tf_op jit(solution)/shard_map/all_to_all | solution.py:494
  30.6 0.1 mul.67.weight_ref
  30.7 0.2 shard_map.78
  30.9 2.9 %collective-permute-start = (f32[1168,128]{1,0:T(8,128)S(1)}, f32[1168,128]{1,0:T(8,128)S(1)}, u32[]{:S(2)}, u32[]{:S(2)}) collective-permute-start(f32[1168,128]{1,0:T(8,128)S(1)} %get-tuple-element.10), channel_id=1, source_target_pairs={{0,1},{1,2},{2,3},{3,7},{7,6},{6,5},{5,4},{4,8},{8,9},{9,10},{10,1... | collective-permute-start | bytes 1794056 | tf_op jit(solution)/shard_map/ppermute | solution.py:523
  33.8 1.9 %collective-permute-start.1 = (f32[1168,128]{1,0:T(8,128)S(1)}, f32[1168,128]{1,0:T(8,128)S(1)}, u32[]{:S(2)}, u32[]{:S(2)}) collective-permute-start(f32[1168,128]{1,0:T(8,128)S(1)} %get-tuple-element.11), channel_id=1, source_target_pairs={{1,0},{2,1},{3,2},{7,3},{6,7},{5,6},{4,5},{8,4},{9,8},{10,9},{11,1... | collective-permute-start | bytes 1794056 | tf_op jit(solution)/shard_map/ppermute | solution.py:524
  35.7 0.0 copy-done.5
  35.7 0.6 fusion.17
  39.2 0.4 fusion
  39.7 0.1 stack.32.scales
  39.8 0.1 add_convert_fusion.inside
  39.9 0.1 pad_maximum_fusion.mix_ref
  40.0 0.7 collective-permute-done.up_ref
  40.7 4.4 %collective-permute-done.1.down_ref = f32[1168,128]{1,0:T(8,128)S(1)} collective-permute-done((f32[1168,128]{1,0:T(8,128)S(1)}, f32[1168,128]{1,0:T(8,128)S(1)}, u32[]{:S(2)}, u32[]{:S(2)}) %collective-permute-start.1) | collective-permute-done | bytes 598048 | tf_op jit(solution)/shard_map/ppermute | solution.py:524
  45.1 0.1 mul.68.unweight_ref
  45.2 13.8 %shard_map.79 = f32[2816,128]{1,0:T(8,128)S(1)} custom-call(f32[5]{0:T(128)S(1)} %stack.32.scales, f32[2]{0:T(128)S(1)} %add_convert_fusion.inside, bf16[528,192]{1,0:T(8,128)(2,1)S(1)} %pad_maximum_fusion.mix_ref, f32[7,2,8,128]{3,2,1,0:T(8,128)S(1)} %get-tuple-element.8.own_a_ref, f32[88,128]{1,0:T(8,128)S(1)} %mul.68.unweight_ref, ...), custom_call_target="tpu_custom_call" | custom-call | flops 10000000000 | bytes 3866624 | tf_op jit(solution)/shard_map/pallas_call | solution.py:423
  58.9 39.4 %all_to_all.10.in_ref = f32[16,2,22,4,128]{4,3,2,1,0:T(4,128)S(1)} all-to-all(f32[16,2,22,4,128]{4,3,2,1,0:T(4,128)S(1)} %bitcast.49), channel_id=1, replica_groups=mesh['groups'=2,'chaos'=4,'space'=4] {'chaos','space'}, dimensions={0} | all-to-all | bytes 2883584 | tf_op jit(solution)/shard_map/all_to_all | solution.py:546
  98.3 1.4 %shard_map.80 = (f32[22,16,4,128]{3,2,1,0:T(4,128)}, f32[22,16,4,128]{3,2,1,0:T(4,128)}) custom-call(f32[16,2,22,4,128]{4,3,2,1,0:T(4,128)S(1)} %all_to_all.10.in_ref), custom_call_target="tpu_custom_call" | custom-call | bytes 2883584 | tf_op jit(solution)/shard_map/pallas_call | solution.py:423
  (7 shorter events, 0.1 us)
Async XLA Ops:
  0.6 1.1 %copy-start = (f32[22,2,4096]{2,1,0:T(2,128)S(1)}, f32[22,2,4096]{2,1,0:T(2,128)}, u32[]{:S(2)}) copy-start(f32[22,2,4096]{2,1,0:T(2,128)} %param.6) | copy-start | bytes 2162692
  1.7 0.9 copy-start.1
  2.7 0.8 copy-start.2
  3.4 8.6 %copy-start.4 = (s32[6,28,3]{1,2,0:T(4,128)S(1)}, s32[6,28,3]{1,2,0:T(4,128)}, u32[]{:S(2)}) copy-start(s32[6,28,3]{1,2,0:T(4,128)} %param.9) | copy-start | bytes 6052
  3.4 8.7 %copy-start.3 = (s32[88]{0:T(128)S(1)}, s32[88]{0:T(128)}, u32[]{:S(2)}) copy-start(s32[88]{0:T(128)} %param.10) | copy-start | bytes 1060
  4.7 31.0 %copy-start.5 = (f32[2]{0:T(128)S(1)}, f32[2]{0:T(128)}, u32[]{:S(2)}) copy-start(f32[2]{0:T(128)} %param.11) | copy-start | bytes 28
  4.7 25.9 %all-to-all-start = ((f32[16,24,4,128]{3,2,1,0:T(4,128)}), f32[16,24,4,128]{3,2,1,0:T(4,128)S(1)}, u32[]{:S(2)}, u32[]{:S(2)}) async-start(f32[16,24,4,128]{3,2,1,0:T(4,128)} %shard_map.77), calls=%async_computation | async-start | bytes 1572864 | tf_op jit(solution)/shard_map/all_to_all | solution.py:494
  30.9 9.8 %collective-permute-start = (f32[1168,128]{1,0:T(8,128)S(1)}, f32[1168,128]{1,0:T(8,128)S(1)}, u32[]{:S(2)}, u32[]{:S(2)}) collective-permute-start(f32[1168,128]{1,0:T(8,128)S(1)} %get-tuple-element.10), channel_id=1, source_target_pairs={{0,1},{1,2},{2,3},{3,7},{7,6},{6,5},{5,4},{4,8},{8,9},{9,10},{10,1... | collective-permute-start | bytes 1794056 | tf_op jit(solution)/shard_map/ppermute | solution.py:523
  33.8 11.3 %collective-permute-start.1 = (f32[1168,128]{1,0:T(8,128)S(1)}, f32[1168,128]{1,0:T(8,128)S(1)}, u32[]{:S(2)}, u32[]{:S(2)}) collective-permute-start(f32[1168,128]{1,0:T(8,128)S(1)} %get-tuple-element.11), channel_id=1, source_target_pairs={{1,0},{2,1},{3,2},{7,3},{6,7},{5,6},{4,5},{8,4},{9,8},{10,9},{11,1... | collective-permute-start | bytes 1794056 | tf_op jit(solution)/shard_map/ppermute | solution.py:524

commit v2 on v1

--- a/solution.py
+++ b/solution.py
@@ -167,51 +167,53 @@
     return pl.ds(t * LANES, LANES)
 
 
-def run_copies(copies):
+def scatter_kernel(
+    blocks, chaos_index, in_ref, mean_ref, modes_ref, out_ref, mean_held, modes_held, sems
+):
+    own, devices, pieces, _ = in_ref.shape
+    modes = modes_ref.shape[0] // (devices * pieces)
+    small = [
+        pltpu.make_async_copy(mean_ref, mean_held, sems.at[devices]),
+        pltpu.make_async_copy(modes_ref, modes_held, sems.at[devices + 1]),
+    ]
+    copies = [
+        pltpu.make_async_copy(
+            in_ref.at[:, block], out_ref.at[device, pl.ds(0, own)], sems.at[device]
+        )
+        for device, block in enumerate(blocks)
+    ]
+    for copy in small + copies:
+        copy.start()
+    for copy in small:
+        copy.wait()
+    for device, block in enumerate(blocks):
+        row = block * pieces + chaos_index[0]
+        values = modes_held[pl.ds(row, modes, stride=devices * pieces), :]
+        out_ref[device, own] = values[:pieces]
+        out_ref[device, own + 1] = jnp.concatenate(
+            [
+                values[pieces:],
+                mean_held[pl.ds(row, 1), :],
+                jnp.zeros((2 * pieces - modes - 1, LANES), jnp.float32),
+            ],
+            axis=0,
+        )
+    for copy in copies:
+        copy.wait()
+
+
+def collect_kernel(blocks, *refs):
+    *arrays, sems = refs
+    fields = len(arrays) // 2
+    copies = [
+        pltpu.make_async_copy(in_ref.at[device], out_ref.at[:, block], sems.at[n, device])
+        for n, (in_ref, out_ref) in enumerate(zip(arrays[:fields], arrays[fields:]))
+        for device, block in enumerate(blocks)
+    ]
     for copy in copies:
         copy.start()
     for copy in copies:
         copy.wait()
-
-
-def scatter_kernel(blocks, chaos_index, in_ref, mean_ref, modes_ref, out_ref, sems):
-    own, devices, pieces, _ = in_ref.shape
-    modes = modes_ref.shape[0] // (devices * pieces)
-    copies = [
-        pltpu.make_async_copy(
-            in_ref.at[:, block], out_ref.at[device, pl.ds(0, own)], sems.at[device]
-        )
-        for device, block in enumerate(blocks)
-    ]
-    for copy in copies:
-        copy.start()
-    for device, block in enumerate(blocks):
-        row = block * pieces + chaos_index[0]
-        values = modes_ref[pl.ds(row, modes, stride=devices * pieces), :]
-        out_ref[device, own] = values[:pieces]
-        out_ref[device, own + 1] = jnp.concatenate(
-            [
-                values[pieces:],
-                mean_ref[pl.ds(row, 1), :],
-                jnp.zeros((2 * pieces - modes - 1, LANES), jnp.float32),
-            ],
-            axis=0,
-        )
-    for copy in copies:
-        copy.wait()
-
-
-def collect_kernel(blocks, in_ref, *rest):
-    *outs, sems = rest
-    run_copies(
-        [
-            pltpu.make_async_copy(
-                in_ref.at[device, n], out_ref.at[:, block], sems.at[n, device]
-            )
-            for n, out_ref in enumerate(outs)
-            for device, block in enumerate(blocks)
-        ]
-    )
 
 
 def start_kernel(chaos, spaces, modes, weight_ref, in_ref, residual_ref, a_ref, up_ref, down_ref):
@@ -270,7 +272,85 @@
             down_ref[rows, :] = value
 
 
-def iterate_kernel(
+def iterate(step, scales, inside, mix_ref, a_ref, b_ref, r_ref, d_ref, total_ref, edge_ref, x_ref, send):
+    layers, _, slots, _ = r_ref.shape
+    modes = a_ref.shape[0]
+    masks = lane_masks(slots)
+    low_half = masks[0]
+    mix = mix_ref[...]
+    depth = mix.shape[1]
+    count = FOLDED - step
+    full = count - 1
+    for l in range(layers):
+        direct = [d_ref[l, t] for t in range(count)]
+        around = neighbour_sums(d_ref, l, count, masks)
+        mixed = jnp.dot(
+            mix, split_stack(direct + around, depth), preferred_element_type=jnp.float32
+        )
+
+        def part(k, n):
+            return jnp.concatenate(
+                [
+                    mixed[row : row + 8, n * LANES : (n + 1) * LANES]
+                    for row in range((k - 1) * 8, (modes - 1) * slots, (modes - 1) * 8)
+                ],
+                axis=0,
+            )
+
+        for t in range(count):
+            a = a_ref[0, l : l + 1, lanes(t)]
+            edge = a * direct[t]
+            if t < full:
+                total = b_ref[0, l : l + 1, lanes(t)] * direct[t] - a * around[t]
+            for k in range(1, modes):
+                a = a_ref[k, l : l + 1, lanes(t)]
+                edge = edge + a * part(k, t)
+                if t < full:
+                    b = b_ref[k, l : l + 1, lanes(t)]
+                    total = total + (b * part(k, t) - a * part(k, count + t))
+            edge_ref[l, t] = edge
+            if t < full:
+                total_ref[l, t] = total
+    for l in range(layers):
+        spread = neighbour_sums(edge_ref, l, count, masks)
+        for t in range(full):
+            diffused = total_ref[l, t] - spread[t]
+            if t >= OWN_TILES:
+                first, second = inside[(t + 1) % 2], inside[t % 2]
+                diffused = diffused * jnp.where(low_half, first, second)
+            residual = r_ref[l, t] - diffused
+            if step == ITERS - 1:
+                send(l, t, residual)
+                continue
+            r_ref[l, t] = residual
+            old = d_ref[l, t]
+            direction = scales[1 + 2 * step] * old + scales[2 + 2 * step] * residual
+            d_ref[l, t] = direction
+            if t < OWN_TILES:
+                value = (old if step == 0 else x_ref[l, t]) + direction
+                if step == ITERS - 2:
+                    send(l, t, value)
+                else:
+                    x_ref[l, t] = value
+
+
+def sender(chaos, spaces, shape, unweight_ref, sent_ref):
+    layers, _, slots, _ = shape
+    own = slots // chaos
+    thick = layers // spaces
+    pieces = OWN_TILES * thick
+
+    def send(l, t, value):
+        i, z = divmod(l, thick)
+        value = value * unweight_ref[...]
+        for c in range(chaos):
+            first = (c * spaces + i) * own * pieces + t * thick + z
+            sent_ref[pl.ds(first, own, stride=pieces), :] = value[c * own : (c + 1) * own]
+
+    return send
+
+
+def first_kernel(
     chaos,
     spaces,
     scales,
@@ -292,21 +372,9 @@
 ):
     layers, _, slots, _ = start_ref.shape
     modes = own_a_ref.shape[0]
-    own = slots // chaos
-    thick = layers // spaces
-    pieces = OWN_TILES * thick
     half = layers // 2
-    masks = lane_masks(slots)
-    low_half = masks[0]
-    mix = mix_ref[...]
-    depth = mix.shape[1]
-
-    def send(field, l, t, value):
-        i, z = divmod(l, thick)
-        value = value * unweight_ref[...]
-        for c in range(chaos):
-            first = ((c * spaces + i) * 2 + field) * own * pieces + t * thick + z
-            sent_ref[pl.ds(first, own, stride=pieces), :] = value[c * own : (c + 1) * own]
+    low_half = lane_masks(slots)[0]
+    send = sender(chaos, spaces, start_ref.shape, unweight_ref, sent_ref)
 
     layer = lax.broadcasted_iota(jnp.int32, (layers, LANES), 0)
     zero = jnp.zeros((layers, LANES), jnp.float32)
@@ -358,66 +426,41 @@
                 r_ref[l, t] = tile
             d_ref[l, t] = tile * scales[0]
 
-    for step in range(ITERS):
-        count = FOLDED - step
-        full = count - 1
-        for l in range(layers):
-            direct = [d_ref[l, t] for t in range(count)]
-            around = neighbour_sums(d_ref, l, count, masks)
-            mixed = jnp.dot(
-                mix, split_stack(direct + around, depth), preferred_element_type=jnp.float32
-            )
-
-            def part(k, n):
-                return jnp.concatenate(
-                    [
-                        mixed[row : row + 8, n * LANES : (n + 1) * LANES]
-                        for row in range((k - 1) * 8, (modes - 1) * slots, (modes - 1) * 8)
-                    ],
-                    axis=0,
-                )
-
-            for t in range(count):
-                a = a_ref[0, l : l + 1, lanes(t)]
-                edge = a * direct[t]
-                if t < full:
-                    total = b_ref[0, l : l + 1, lanes(t)] * direct[t] - a * around[t]
-                for k in range(1, modes):
-                    a = a_ref[k, l : l + 1, lanes(t)]
-                    edge = edge + a * part(k, t)
-                    if t < full:
-                        b = b_ref[k, l : l + 1, lanes(t)]
-                        total = total + (b * part(k, t) - a * part(k, count + t))
-                edge_ref[l, t] = edge
-                if t < full:
-                    total_ref[l, t] = total
-        for l in range(layers):
-            spread = neighbour_sums(edge_ref, l, count, masks)
-            for t in range(full):
-                diffused = total_ref[l, t] - spread[t]
-                if t >= OWN_TILES:
-                    first, second = inside[(t + 1) % 2], inside[t % 2]
-                    diffused = diffused * jnp.where(low_half, first, second)
-                residual = r_ref[l, t] - diffused
-                if step == ITERS - 1:
-                    send(1, l, t, residual)
-                    continue
-                r_ref[l, t] = residual
-                old = d_ref[l, t]
-                direction = scales[1 + 2 * step] * old + scales[2 + 2 * step] * residual
-                d_ref[l, t] = direction
-                if t < OWN_TILES:
-                    value = (old if step == 0 else x_ref[l, t]) + direction
-                    if step == ITERS - 2:
-                        send(0, l, t, value)
-                    else:
-                        x_ref[l, t] = value
+    for step in range(ITERS - 1):
+        iterate(
+            step, scales, inside, mix_ref, a_ref, b_ref, r_ref, d_ref, total_ref, edge_ref, x_ref, send
+        )
+
+
+def last_kernel(
+    chaos,
+    spaces,
+    scales,
+    inside,
+    mix_ref,
+    unweight_ref,
+    a_ref,
+    b_ref,
+    r_ref,
+    d_ref,
+    sent_ref,
+    total_ref,
+    edge_ref,
+):
+    send = sender(chaos, spaces, r_ref.shape, unweight_ref, sent_ref)
+    iterate(
+        ITERS - 1, scales, inside, mix_ref, a_ref, b_ref, r_ref, d_ref, total_ref, edge_ref, None, send
+    )
 
 
 def call(kernel, outs, scalars, arrays, scratch=(), flops=0, in_kinds=None, out_kind=pltpu.VMEM):
     kinds = in_kinds or [pltpu.VMEM] * len(arrays)
     in_specs = [pl.BlockSpec(memory_space=pltpu.SMEM)] * len(scalars) + [
         pl.BlockSpec(memory_space=kind) for kind in kinds
+    ]
+    arrays = [
+        pltpu.with_memory_space_constraint(x, kind) if kind == pltpu.HBM else x
+        for x, kind in zip(arrays, kinds)
     ]
     moved = sum(4 * x.size for x in arrays) + sum(4 * x.size for x in outs)
     return pl.pallas_call(
@@ -488,8 +531,12 @@
             by_blocks(mean_conductivity).reshape(-1, LANES),
             by_blocks(mode_shapes).reshape(-1, LANES),
         ],
-        [pltpu.SemaphoreType.DMA((devices,))],
-        in_kinds=[pltpu.HBM, pltpu.VMEM, pltpu.VMEM],
+        [
+            pltpu.VMEM((devices * pieces, LANES), f32),
+            pltpu.VMEM(((modes - 1) * devices * pieces, LANES), f32),
+            pltpu.SemaphoreType.DMA((devices + 2,)),
+        ],
+        in_kinds=[pltpu.HBM] * 3,
     )[0]
     gathered = lax.all_to_all(scattered, BOTH, 0, 0, tiled=True).reshape(-1, LANES)
 
@@ -526,31 +573,39 @@
     def held(tiles):
         return pltpu.VMEM((layers, tiles, slots, LANES), f32)
 
-    sent = call(
-        functools.partial(iterate_kernel, chaos, spaces),
-        [shape(devices * 2 * own * pieces, LANES)],
+    sent, a, b, residual, direction = call(
+        functools.partial(first_kernel, chaos, spaces),
+        [
+            shape(devices * own * pieces, LANES),
+            shape(modes, layers, FOLDED * LANES),
+            shape(modes, layers, (FOLDED - 1) * LANES),
+            shape(layers, FOLDED - 1, slots, LANES),
+            shape(layers, FOLDED, slots, LANES),
+        ],
         [scales, inside],
         [mix, own_a, unweight, start, from_below, from_above],
-        [
-            pltpu.VMEM((modes, layers, FOLDED * LANES), f32),
-            pltpu.VMEM((modes, layers, (FOLDED - 1) * LANES), f32),
-            held(FOLDED - 1),
-            held(FOLDED),
-            held(FOLDED - 1),
-            held(FOLDED),
-            held(OWN_TILES),
-        ],
-        flops=10000000000,
+        [held(FOLDED - 1), held(FOLDED), held(OWN_TILES)],
+        flops=8000000000,
+    )
+    received = [lax.all_to_all(sent.reshape(devices, own, pieces, LANES), BOTH, 0, 0, tiled=True)]
+    sent = call(
+        functools.partial(last_kernel, chaos, spaces),
+        [shape(devices * own * pieces, LANES)],
+        [scales, inside],
+        [mix, unweight, a, b, residual, direction],
+        [held(OWN_TILES), held(OWN_TILES + 1)],
+        flops=3000000000,
     )[0]
-    sent = sent.reshape(devices, 2, own, pieces, LANES)
-    received = lax.all_to_all(sent, BOTH, 0, 0, tiled=True)
+    received.append(
+        lax.all_to_all(sent.reshape(devices, own, pieces, LANES), BOTH, 0, 0, tiled=True)
+    )
     outs = call(
         functools.partial(collect_kernel, blocks),
         [shape(own, devices, pieces, LANES)] * 2,
         [],
-        [received],
+        received,
         [pltpu.SemaphoreType.DMA((2, devices))],
-        in_kinds=[pl.ANY],
+        in_kinds=[pl.ANY] * 2,
         out_kind=pltpu.HBM,
     )
     return tuple(

time: 100 us -> 107 us (1.070)
  blocking collectives: 39.4 us -> 24.5 us
  waiting for transfers between devices: 23 us -> 34.2 us
  starting transfers between devices: 12.1 us -> 17.5 us
  Pallas kernels: 16.6 us -> 19.6 us
  local copies, waits for them, and re-layouts: 3.68 us -> 6.12 us
    all_to_all x1, blocking collectives: 39.4 us -> 24.5 us  [local_by_cells(): lax.all_to_all(sent.reshape(devices, own, pieces, LANES), BOTH, 0, 0, til...]
    all_to_all x0 -> x1, waiting for transfers between devices: none -> 11.2 us  [local_by_cells(): lax.all_to_all(sent.reshape(devices, own, pieces, LANES), BOTH, 0, 0, til...]
    all_to_all x0 -> x1, starting transfers between devices: none -> 5.4 us  [local_by_cells(): lax.all_to_all(sent.reshape(devices, own, pieces, LANES), BOTH, 0, 0, til...]
    pallas_call x4 -> x5, Pallas kernels: 16.6 us -> 19.6 us  [call(): pl.pallas_call(kernel, out_shape=outs, in_specs=in_specs, out_specs=[pl.B...]
    unnamed x12 -> x14, local copies, waits for them, and re-layouts: 2.8 us -> 5.2 us
  transfers between devices with their start and end apart: 3 -> 4, of which waited for: 3 -> 4; matrix products, arithmetic and copies ran while one was open for 2% -> 2% of each run, Pallas kernels for 0% -> 3%
where the time goes in v2:
time: 107 us
  waiting for transfers between devices  34.2 us (32%)
  blocking collectives  24.5 us (23%)
  Pallas kernels  19.6 us (18%)
  starting transfers between devices  17.5 us (16%)
  local copies, waits for them, and re-layouts  6.12 us (6%)
  between operations  3.8 us (4%)
    all_to_all x1, blocking collectives, local_by_cells(): lax.all_to_all(sent.reshape(devices, own, pieces, LANES), BOTH, 0, 0, til...  24.5 us
    pallas_call x5, Pallas kernels, call(): pl.pallas_call(kernel, out_shape=outs, in_specs=in_specs, out_specs=[pl.B...  19.6 us
    all_to_all x1, waiting for transfers between devices, local_by_cells(): lax.all_to_all(scattered, BOTH, 0, 0, tiled=True).reshape(-1, LANES)  17.9 us
    all_to_all x1, waiting for transfers between devices, local_by_cells(): lax.all_to_all(sent.reshape(devices, own, pieces, LANES), BOTH, 0, 0, til...  11.2 us
    all_to_all x1, starting transfers between devices, local_by_cells(): lax.all_to_all(scattered, BOTH, 0, 0, tiled=True).reshape(-1, LANES)  7.33 us
    all_to_all x1, starting transfers between devices, local_by_cells(): lax.all_to_all(sent.reshape(devices, own, pieces, LANES), BOTH, 0, 0, til...  5.4 us
    unnamed x14, local copies, waits for them, and re-layouts  5.2 us
    ppermute x1, waiting for transfers between devices, local_by_cells(): from_above = lax.ppermute(down, BOTH, downward)  4.08 us
  transfers between devices with their start and end apart: 4, of which 4 were waited for; matrix products, arithmetic and copies ran while one was open for 2% of the time, Pallas kernels for 3%

profile of v2, /device:TPU:1, one launch (start us, length us, event | category | flops | bytes accessed | tf_op | source)
XLA Modules:
  0.0 106.9 jit_solution(13691850077005539631)
XLA Ops:
  0.6 0.0 copy-start.5
  0.6 0.0 copy-start.4
  0.7 2.3 %shard_map.77 = f32[16,24,4,128]{3,2,1,0:T(4,128)} custom-call(s32[1]{0:T(128)} %bitcast.15.chaos_index, f32[22,16,4,128]{3,2,1,0:T(4,128)} %bitcast.51, f32[64,128]{1,0:T(8,128)} %bitcast.54, f32[384,128]{1,0:T(8,128)} %bitcast.53), custom_call_target="tpu_custom_call" | custom-call | bytes 1736704 | tf_op jit(solution)/shard_map/pallas_call | solution.py:466
  2.9 0.0 copy-start.6
  2.9 7.3 %all-to-all-start = ((f32[16,24,4,128]{3,2,1,0:T(4,128)}), f32[16,24,4,128]{3,2,1,0:T(4,128)S(1)}, u32[]{:S(2)}, u32[]{:S(2)}) async-start(f32[16,24,4,128]{3,2,1,0:T(4,128)} %shard_map.77), calls=%async_computation | async-start | bytes 1572864 | tf_op jit(solution)/shard_map/all_to_all | solution.py:541
  10.3 0.0 copy-done.5
  10.3 0.0 copy-done.4
  10.3 0.1 convert_reduce_fusion
  10.5 0.4 fusion.2
  10.9 17.9 %all-to-all-done = f32[16,24,4,128]{3,2,1,0:T(4,128)S(1)} async-done(((f32[16,24,4,128]{3,2,1,0:T(4,128)}), f32[16,24,4,128]{3,2,1,0:T(4,128)S(1)}, u32[]{:S(2)}, u32[]{:S(2)}) %all-to-all-start) | async-done | bytes 786464 | tf_op jit(solution)/shard_map/all_to_all | solution.py:541
  28.8 0.1 mul.67.weight_ref
  28.9 1.0 shard_map.78
  29.9 2.9 %collective-permute-start = (f32[1168,128]{1,0:T(8,128)}, f32[1168,128]{1,0:T(8,128)S(1)}, u32[]{:S(2)}, u32[]{:S(2)}) collective-permute-start(f32[1168,128]{1,0:T(8,128)} %get-tuple-element.15), channel_id=1, source_target_pairs={{0,1},{1,2},{2,3},{3,7},{7,6},{6,5},{5,4},{4,8},{8,9},{9,10},{10,1... | collective-permute-start | bytes 1794056 | tf_op jit(solution)/shard_map/ppermute | solution.py:570
  32.8 1.9 %collective-permute-start.1 = (f32[1168,128]{1,0:T(8,128)S(1)}, f32[1168,128]{1,0:T(8,128)S(1)}, u32[]{:S(2)}, u32[]{:S(2)}) collective-permute-start(f32[1168,128]{1,0:T(8,128)S(1)} %get-tuple-element.16), channel_id=1, source_target_pairs={{1,0},{2,1},{3,2},{7,3},{6,7},{5,6},{4,5},{8,4},{9,8},{10,9},{11,1... | collective-permute-start | bytes 1794056 | tf_op jit(solution)/shard_map/ppermute | solution.py:571
  34.7 0.0 copy-done.6
  34.7 0.6 fusion.17
  38.2 0.4 fusion
  38.7 0.1 stack.32.scales
  38.8 0.1 add_convert_fusion.inside
  38.8 0.1 pad_maximum_fusion.mix_ref
  39.0 1.0 collective-permute-done.up_ref
  40.0 4.1 %collective-permute-done.1.down_ref = f32[1168,128]{1,0:T(8,128)S(1)} collective-permute-done((f32[1168,128]{1,0:T(8,128)S(1)}, f32[1168,128]{1,0:T(8,128)S(1)}, u32[]{:S(2)}, u32[]{:S(2)}) %collective-permute-start.1) | collective-permute-done | bytes 598048 | tf_op jit(solution)/shard_map/ppermute | solution.py:571
  44.1 0.1 mul.68.unweight_ref
  44.1 11.6 %shard_map.79 = (f32[1408,128]{1,0:T(8,128)}, f32[7,8,640]{2,1,0:T(8,128)S(1)}, f32[7,8,512]{2,1,0:T(8,128)S(1)}, f32[8,4,88,128]{3,2,1,0:T(8,128)S(1)}, f32[8,5,88,128]{3,2,1,0:T(8,128)S(1)}) custom-call(f32[5]{0:T(128)S(1)} %stack.32.scales, f32[2]{0:T(128)S(1)} %add_convert_fusion.inside, bf16[528,192]{1,0:T(8,128)(2,1)S(1)} %pad_maximum_fusion.mix_ref, ...), custom_call_target="tpu_custom_call" | custom-call | flops 8000000000 | bytes 6647808 | tf_op jit(solution)/shard_map/pallas_call | solution.py:466
  55.7 0.0 copy-start
  55.7 1.2 %copy-done = f32[8,5,88,128]{3,2,1,0:T(8,128)} copy-done((f32[8,5,88,128]{3,2,1,0:T(8,128)}, f32[8,5,88,128]{3,2,1,0:T(8,128)S(1)}, u32[]{:S(2)}) %copy-start) | copy-done | bytes 1802264
  57.0 0.0 copy-start.2
  57.0 1.1 %copy-done.2 = f32[8,4,88,128]{3,2,1,0:T(8,128)} copy-done((f32[8,4,88,128]{3,2,1,0:T(8,128)}, f32[8,4,88,128]{3,2,1,0:T(8,128)S(1)}, u32[]{:S(2)}) %copy-start.2) | copy-done | bytes 1441816
  58.1 5.4 %all-to-all-start.1 = ((f32[16,22,4,128]{3,2,1,0:T(4,128)}), f32[16,22,4,128]{3,2,1,0:T(4,128)S(1)}, u32[]{:S(2)}, u32[]{:S(2)}) async-start(f32[16,22,4,128]{3,2,1,0:T(4,128)} %bitcast.26), calls=%async_computation.1 | async-start | bytes 1441792 | tf_op jit(solution)/shard_map/all_to_all | solution.py:590
  63.5 0.0 copy-start.1
  63.5 1.5 %copy-done.1 = f32[8,5,88,128]{3,2,1,0:T(8,128)S(1)} copy-done((f32[8,5,88,128]{3,2,1,0:T(8,128)S(1)}, f32[8,5,88,128]{3,2,1,0:T(8,128)}, u32[]{:S(2)}) %copy-start.1) | copy-done | bytes 1802264
  65.0 0.0 copy-start.3
  65.0 1.4 %copy-done.3 = f32[8,4,88,128]{3,2,1,0:T(8,128)S(1)} copy-done((f32[8,4,88,128]{3,2,1,0:T(8,128)S(1)}, f32[8,4,88,128]{3,2,1,0:T(8,128)}, u32[]{:S(2)}) %copy-start.3) | copy-done | bytes 1441816
  66.3 3.4 %shard_map.80 = f32[1408,128]{1,0:T(8,128)S(1)} custom-call(f32[5]{0:T(128)S(1)} %stack.32.scales, f32[2]{0:T(128)S(1)} %add_convert_fusion.inside, bf16[528,192]{1,0:T(8,128)(2,1)S(1)} %pad_maximum_fusion.mix_ref, f32[88,128]{1,0:T(8,128)S(1)} %mul.68.unweight_ref, f32[7,8,640]{2,1,0:T(8,128)S(1)} %get-tuple-element.18.a_ref, ...), custom_call_target="tpu_custom_call" | custom-call | flops 3000000000 | bytes 4673536 | tf_op jit(solution)/shard_map/pallas_call | solution.py:466
  69.7 11.2 %all-to-all-done.1.refs_0_ = f32[16,22,4,128]{3,2,1,0:T(4,128)S(1)} async-done(((f32[16,22,4,128]{3,2,1,0:T(4,128)}), f32[16,22,4,128]{3,2,1,0:T(4,128)S(1)}, u32[]{:S(2)}, u32[]{:S(2)}) %all-to-all-start.1) | async-done | bytes 720928 | tf_op jit(solution)/shard_map/all_to_all | solution.py:590
  80.9 24.5 %all_to_all.15.refs_1_ = f32[16,22,4,128]{3,2,1,0:T(4,128)S(1)} all-to-all(f32[16,22,4,128]{3,2,1,0:T(4,128)S(1)} %bitcast.50), channel_id=1, replica_groups=mesh['groups'=2,'chaos'=4,'space'=4] {'chaos','space'}, dimensions={0} | all-to-all | bytes 1441792 | tf_op jit(solution)/shard_map/all_to_all | solution.py:600
  105.4 1.4 %shard_map.81 = (f32[22,16,4,128]{3,2,1,0:T(4,128)}, f32[22,16,4,128]{3,2,1,0:T(4,128)}) custom-call(f32[16,22,4,128]{3,2,1,0:T(4,128)S(1)} %all-to-all-done.1.refs_0_, f32[16,22,4,128]{3,2,1,0:T(4,128)S(1)} %all_to_all.15.refs_1_), custom_call_target="tpu_custom_call" | custom-call | bytes 2883584 | tf_op jit(solution)/shard_map/pallas_call | solution.py:466
  (7 shorter events, 0.1 us)
Async XLA Ops:
  0.6 9.6 %copy-start.5 = (s32[6,28,3]{1,2,0:T(4,128)S(1)}, s32[6,28,3]{1,2,0:T(4,128)}, u32[]{:S(2)}) copy-start(s32[6,28,3]{1,2,0:T(4,128)} %param.9) | copy-start | bytes 6052
  0.6 9.7 %copy-start.4 = (s32[88]{0:T(128)S(1)}, s32[88]{0:T(128)}, u32[]{:S(2)}) copy-start(s32[88]{0:T(128)} %param.10) | copy-start | bytes 1060
  2.9 31.8 %copy-start.6 = (f32[2]{0:T(128)S(1)}, f32[2]{0:T(128)}, u32[]{:S(2)}) copy-start(f32[2]{0:T(128)} %param.11) | copy-start | bytes 28
  2.9 25.9 %all-to-all-start = ((f32[16,24,4,128]{3,2,1,0:T(4,128)}), f32[16,24,4,128]{3,2,1,0:T(4,128)S(1)}, u32[]{:S(2)}, u32[]{:S(2)}) async-start(f32[16,24,4,128]{3,2,1,0:T(4,128)} %shard_map.77), calls=%async_computation | async-start | bytes 1572864 | tf_op jit(solution)/shard_map/all_to_all | solution.py:541
  29.9 10.1 %collective-permute-start = (f32[1168,128]{1,0:T(8,128)}, f32[1168,128]{1,0:T(8,128)S(1)}, u32[]{:S(2)}, u32[]{:S(2)}) collective-permute-start(f32[1168,128]{1,0:T(8,128)} %get-tuple-element.15), channel_id=1, source_target_pairs={{0,1},{1,2},{2,3},{3,7},{7,6},{6,5},{5,4},{4,8},{8,9},{9,10},{10,1... | collective-permute-start | bytes 1794056 | tf_op jit(solution)/shard_map/ppermute | solution.py:570
  32.8 11.3 %collective-permute-start.1 = (f32[1168,128]{1,0:T(8,128)S(1)}, f32[1168,128]{1,0:T(8,128)S(1)}, u32[]{:S(2)}, u32[]{:S(2)}) collective-permute-start(f32[1168,128]{1,0:T(8,128)S(1)} %get-tuple-element.16), channel_id=1, source_target_pairs={{1,0},{2,1},{3,2},{7,3},{6,7},{5,6},{4,5},{8,4},{9,8},{10,9},{11,1... | collective-permute-start | bytes 1794056 | tf_op jit(solution)/shard_map/ppermute | solution.py:571
  55.7 1.2 %copy-start = (f32[8,5,88,128]{3,2,1,0:T(8,128)}, f32[8,5,88,128]{3,2,1,0:T(8,128)S(1)}, u32[]{:S(2)}) copy-start(f32[8,5,88,128]{3,2,1,0:T(8,128)S(1)} %get-tuple-element.21.d_ref) | copy-start | bytes 5406724
  57.0 1.1 %copy-start.2 = (f32[8,4,88,128]{3,2,1,0:T(8,128)}, f32[8,4,88,128]{3,2,1,0:T(8,128)S(1)}, u32[]{:S(2)}) copy-start(f32[8,4,88,128]{3,2,1,0:T(8,128)S(1)} %get-tuple-element.20.r_ref) | copy-start | bytes 4325380
  58.1 22.8 %all-to-all-start.1 = ((f32[16,22,4,128]{3,2,1,0:T(4,128)}), f32[16,22,4,128]{3,2,1,0:T(4,128)S(1)}, u32[]{:S(2)}, u32[]{:S(2)}) async-start(f32[16,22,4,128]{3,2,1,0:T(4,128)} %bitcast.26), calls=%async_computation.1 | async-start | bytes 1441792 | tf_op jit(solution)/shard_map/all_to_all | solution.py:590
  63.5 1.5 %copy-start.1 = (f32[8,5,88,128]{3,2,1,0:T(8,128)S(1)}, f32[8,5,88,128]{3,2,1,0:T(8,128)}, u32[]{:S(2)}) copy-start(f32[8,5,88,128]{3,2,1,0:T(8,128)} %copy-done) | copy-start | bytes 5406724
  65.0 1.4 %copy-start.3 = (f32[8,4,88,128]{3,2,1,0:T(8,128)S(1)}, f32[8,4,88,128]{3,2,1,0:T(8,128)}, u32[]{:S(2)}) copy-start(f32[8,4,88,128]{3,2,1,0:T(8,128)} %copy-done.2) | copy-start | bytes 4325380

commit v3 on v1

--- a/solution.py
+++ b/solution.py
@@ -125,12 +125,12 @@
     return lane < NY, lane % NY > 0, lane % NY < NY - 1
 
 
-def plane_sums(tiles, masks):
+def plane_sums(tiles, masks, first=0):
     low_half, has_left, has_right = masks
     zero = jnp.zeros(tiles[0].shape, jnp.float32)
     swapped = [pltpu.roll(tile, NY, 1) for tile in tiles]
     sums = []
-    for t, tile in enumerate(tiles[:-1]):
+    for t in range(first, len(tiles) - 1):
         if t == 0:
             across = swapped[0] + jnp.where(low_half, swapped[2], swapped[1])
         elif t == 1:
@@ -139,17 +139,17 @@
             across = swapped[3] + jnp.where(low_half, swapped[1], swapped[0])
         else:
             across = swapped[t - 1] + swapped[t + 1]
-        left = jnp.where(has_left, pltpu.roll(tile, 1, 1), zero)
-        right = jnp.where(has_right, pltpu.roll(tile, LANES - 1, 1), zero)
+        left = jnp.where(has_left, pltpu.roll(tiles[t], 1, 1), zero)
+        right = jnp.where(has_right, pltpu.roll(tiles[t], LANES - 1, 1), zero)
         sums.append(across + (left + right))
     return sums
 
 
-def neighbour_sums(ref, layer, count, masks):
-    sums = plane_sums([ref[layer, t] for t in range(count)], masks)
+def neighbour_sums(read, layer, layers, count, masks, first=0):
+    sums = plane_sums([read(layer, t) for t in range(count)], masks, first)
     for other in (layer - 1, layer + 1):
-        if 0 <= other < ref.shape[0]:
-            sums = [total + ref[other, t] for t, total in enumerate(sums)]
+        if 0 <= other < layers:
+            sums = [total + read(other, first + n) for n, total in enumerate(sums)]
     return sums
 
 
@@ -174,25 +174,33 @@
         copy.wait()
 
 
-def scatter_kernel(blocks, chaos_index, in_ref, mean_ref, modes_ref, out_ref, sems):
+def scatter_kernel(
+    blocks, chaos_index, in_ref, mean_ref, modes_ref, out_ref, mean_held, modes_held, sems
+):
     own, devices, pieces, _ = in_ref.shape
     modes = modes_ref.shape[0] // (devices * pieces)
+    small = [
+        pltpu.make_async_copy(mean_ref, mean_held, sems.at[devices]),
+        pltpu.make_async_copy(modes_ref, modes_held, sems.at[devices + 1]),
+    ]
     copies = [
         pltpu.make_async_copy(
             in_ref.at[:, block], out_ref.at[device, pl.ds(0, own)], sems.at[device]
         )
         for device, block in enumerate(blocks)
     ]
-    for copy in copies:
+    for copy in small + copies:
         copy.start()
+    for copy in small:
+        copy.wait()
     for device, block in enumerate(blocks):
         row = block * pieces + chaos_index[0]
-        values = modes_ref[pl.ds(row, modes, stride=devices * pieces), :]
+        values = modes_held[pl.ds(row, modes, stride=devices * pieces), :]
         out_ref[device, own] = values[:pieces]
         out_ref[device, own + 1] = jnp.concatenate(
             [
                 values[pieces:],
-                mean_ref[pl.ds(row, 1), :],
+                mean_held[pl.ds(row, 1), :],
                 jnp.zeros((2 * pieces - modes - 1, LANES), jnp.float32),
             ],
             axis=0,
@@ -214,7 +222,21 @@
     )
 
 
-def start_kernel(chaos, spaces, modes, weight_ref, in_ref, residual_ref, a_ref, up_ref, down_ref):
+def start_kernel(
+    chaos,
+    spaces,
+    modes,
+    odd,
+    scales,
+    mix_ref,
+    weight_ref,
+    in_ref,
+    residual_ref,
+    a_ref,
+    chip_ref,
+    core_ref,
+):
+    upward = odd[0] > 0
     layers, tiles, slots, _ = residual_ref.shape
     own = slots // chaos
     thick = layers // spaces
@@ -224,8 +246,9 @@
     low_half = lane_masks(slots)[0]
     weight = weight_ref[...]
 
-    def put(ref, place, value):
-        ref[pl.ds(place * slots, slots), :] = value
+    def put(rows, up, down):
+        chip_ref[rows, :] = jnp.where(upward, up, down)
+        core_ref[rows, :] = jnp.where(upward, down, up)
 
     for l in range(layers):
         i, z = divmod(l, thick)
@@ -238,18 +261,12 @@
                 ],
                 axis=0,
             )
-        put(up_ref, l, residual_ref[l, 1])
-        put(down_ref, l, residual_ref[l, 0])
+        put(pl.ds(l * slots, slots), residual_ref[l, 1], residual_ref[l, 0])
     for l in range(half):
         later = l + half
         put(
-            up_ref,
-            layers + l,
+            pl.ds((layers + l) * slots, slots),
             jnp.where(low_half, pltpu.roll(residual_ref[later, 0], NY, 1), residual_ref[l, 0]),
-        )
-        put(
-            down_ref,
-            layers + l,
             jnp.where(low_half, residual_ref[l, 1], pltpu.roll(residual_ref[later, 1], NY, 1)),
         )
 
@@ -266,8 +283,81 @@
             value = mean if k == 0 else mean * a_ref[k, t]
             a_ref[k, t] = value
             rows = pl.ds((layers + half) * slots + (k * tiles + t) * layers, layers)
-            up_ref[rows, :] = value
-            down_ref[rows, :] = value
+            put(rows, value, value)
+
+
+def mode_part(mixed, modes, k, n):
+    group = 8 * (modes - 1)
+    return jnp.concatenate(
+        [
+            mixed[row : row + 8, n * LANES : (n + 1) * LANES]
+            for row in range((k - 1) * 8, mixed.shape[0], group)
+        ],
+        axis=0,
+    )
+
+
+def layer_sum(values, layer):
+    layers = values.shape[0]
+    zero = jnp.zeros(values.shape, jnp.float32)
+    under = jnp.where(layer > 0, pltpu.roll(values, 1, 0), zero)
+    over = jnp.where(layer < layers - 1, pltpu.roll(values, layers - 1, 0), zero)
+    return under + over
+
+
+def weighted_tiles(mixed, modes, count, full, direct, around, a_of, b_of):
+    results = []
+    for t in range(count):
+        a = a_of(0, t)
+        edge = a * direct[t]
+        total = b_of(0, t) * direct[t] - a * around[t] if t < full else None
+        for k in range(1, modes):
+            a = a_of(k, t)
+            part = mode_part(mixed, modes, k, t)
+            edge = edge + a * part
+            if t < full:
+                beside = mode_part(mixed, modes, k, mixed.shape[1] // LANES - full + t)
+                total = total + (b_of(k, t) * part - a * beside)
+        results.append((total, edge))
+    return results
+
+
+def own_kernel(scales, mix_ref, own_a_ref, start_ref, total_ref, edge_ref, b_ref):
+    layers, tiles, slots, _ = start_ref.shape
+    modes = own_a_ref.shape[0]
+    masks = lane_masks(slots)
+    mix = mix_ref[...]
+    layer = lax.broadcasted_iota(jnp.int32, (layers, LANES), 0)
+    outside = jnp.zeros((layers, LANES), jnp.float32)
+    for k in range(modes):
+        values = [own_a_ref[k, t] for t in range(tiles)]
+        sums = plane_sums(values + [outside], lane_masks(layers))
+        for t in range(tiles):
+            b_ref[k, :, lanes(t)] = 6.0 * values[t] + (sums[t] + layer_sum(values[t], layer))
+    nothing = jnp.zeros((slots, LANES), jnp.float32)
+
+    def read(l, t):
+        return start_ref[l, t] * scales[0] if t < tiles else nothing
+
+    for l in range(layers):
+        direct = [read(l, t) for t in range(tiles)]
+        around = neighbour_sums(read, l, layers, tiles + 1, masks)
+        mixed = jnp.dot(
+            mix, split_stack(direct + around, mix.shape[1]), preferred_element_type=jnp.float32
+        )
+        results = weighted_tiles(
+            mixed,
+            modes,
+            tiles,
+            tiles,
+            direct,
+            around,
+            lambda k, t: own_a_ref[k, t, l : l + 1, :],
+            lambda k, t: b_ref[k, l : l + 1, lanes(t)],
+        )
+        for t, (total, edge) in enumerate(results):
+            total_ref[l, t] = total
+            edge_ref[l, t] = edge
 
 
 def iterate_kernel(
@@ -275,15 +365,19 @@
     spaces,
     scales,
     inside,
+    odd,
     mix_ref,
     own_a_ref,
     unweight_ref,
     start_ref,
-    up_ref,
-    down_ref,
+    own_total_ref,
+    own_edge_ref,
+    chip_ref,
+    core_ref,
     sent_ref,
     a_ref,
     b_ref,
+    face_ref,
     r_ref,
     d_ref,
     total_ref,
@@ -300,6 +394,11 @@
     low_half = masks[0]
     mix = mix_ref[...]
     depth = mix.shape[1]
+    upward = odd[0] > 0
+
+    def message(start, size):
+        chip, core = chip_ref[pl.ds(start, size), :], core_ref[pl.ds(start, size), :]
+        return jnp.where(upward, core, chip), jnp.where(upward, chip, core)
 
     def send(field, l, t, value):
         i, z = divmod(l, thick)
@@ -309,17 +408,11 @@
             sent_ref[pl.ds(first, own, stride=pieces), :] = value[c * own : (c + 1) * own]
 
     layer = lax.broadcasted_iota(jnp.int32, (layers, LANES), 0)
-    zero = jnp.zeros((layers, LANES), jnp.float32)
     narrow_masks = lane_masks(layers)
     low = narrow_masks[0]
     for k in range(modes):
-        below, above = [
-            [
-                ref[pl.ds((layers + half) * slots + (k * OWN_TILES + t) * layers, layers), :]
-                for t in range(OWN_TILES)
-            ]
-            for ref in (up_ref, down_ref)
-        ]
+        places = [(layers + half) * slots + (k * OWN_TILES + t) * layers for t in range(OWN_TILES)]
+        below, above = zip(*[message(place, layers) for place in places])
         values = [
             own_a_ref[k, 0],
             own_a_ref[k, 1],
@@ -331,17 +424,13 @@
         for t in range(FOLDED):
             a_ref[k, :, lanes(t)] = values[t]
         for t in range(FOLDED - 1):
-            under = jnp.where(layer > 0, pltpu.roll(values[t], 1, 0), zero)
-            over = jnp.where(layer < layers - 1, pltpu.roll(values[t], layers - 1, 0), zero)
-            b_ref[k, :, lanes(t)] = 6.0 * values[t] + (sums[t] + (under + over))
-
-    def message(ref, place):
-        return ref[pl.ds(place * slots, slots), :]
+            b_ref[k, :, lanes(t)] = 6.0 * values[t] + (sums[t] + layer_sum(values[t], layer))
+        face_ref[k, :, lanes(0)] = jnp.where(low, values[0], values[1])
+        face_ref[k, :, lanes(1)] = pltpu.roll(values[2], NY, 1)
 
     for l in range(layers):
-        below, above = message(up_ref, l), message(down_ref, l)
-        far_below = message(up_ref, layers + l % half)
-        far_above = message(down_ref, layers + l % half)
+        below, above = message(l * slots, slots)
+        far_below, far_above = message((layers + l % half) * slots, slots)
         if l < half:
             far = jnp.where(low_half, far_above, far_below)
         else:
@@ -358,46 +447,60 @@
                 r_ref[l, t] = tile
             d_ref[l, t] = tile * scales[0]
 
+    def read(l, t):
+        return d_ref[l, t]
+
+    zero = jnp.zeros((slots, LANES), jnp.float32)
     for step in range(ITERS):
         count = FOLDED - step
         full = count - 1
+        first = OWN_TILES if step == 0 else 0
         for l in range(layers):
-            direct = [d_ref[l, t] for t in range(count)]
-            around = neighbour_sums(d_ref, l, count, masks)
+            direct = [d_ref[l, t] for t in range(first, count)]
+            around = neighbour_sums(read, l, layers, count, masks, first)
+            extra = []
+            if step == 0:
+                extra = [jnp.where(low_half, d_ref[l, 0], d_ref[l, 1])]
             mixed = jnp.dot(
-                mix, split_stack(direct + around, depth), preferred_element_type=jnp.float32
+                mix, split_stack(direct + extra + around, depth), preferred_element_type=jnp.float32
             )
-
-            def part(k, n):
-                return jnp.concatenate(
-                    [
-                        mixed[row : row + 8, n * LANES : (n + 1) * LANES]
-                        for row in range((k - 1) * 8, (modes - 1) * slots, (modes - 1) * 8)
-                    ],
-                    axis=0,
-                )
-
-            for t in range(count):
-                a = a_ref[0, l : l + 1, lanes(t)]
-                edge = a * direct[t]
-                if t < full:
-                    total = b_ref[0, l : l + 1, lanes(t)] * direct[t] - a * around[t]
+            results = weighted_tiles(
+                mixed,
+                modes,
+                count - first,
+                full - first,
+                direct,
+                around,
+                lambda k, t: a_ref[k, l : l + 1, lanes(first + t)],
+                lambda k, t: b_ref[k, l : l + 1, lanes(first + t)],
+            )
+            for t, (total, edge) in enumerate(results):
+                edge_ref[l, first + t] = edge
+                if first + t < full:
+                    total_ref[l, first + t] = total
+            if step == 0:
+                own_face = face_ref[0, l : l + 1, lanes(0)]
+                other_face = face_ref[0, l : l + 1, lanes(1)]
+                part = other_face * extra[0] - own_face * pltpu.roll(direct[0], NY, 1)
                 for k in range(1, modes):
-                    a = a_ref[k, l : l + 1, lanes(t)]
-                    edge = edge + a * part(k, t)
-                    if t < full:
-                        b = b_ref[k, l : l + 1, lanes(t)]
-                        total = total + (b * part(k, t) - a * part(k, count + t))
-                edge_ref[l, t] = edge
-                if t < full:
-                    total_ref[l, t] = total
+                    own_face = face_ref[k, l : l + 1, lanes(0)]
+                    other_face = face_ref[k, l : l + 1, lanes(1)]
+                    own_mixed = mode_part(mixed, modes, k, len(direct))
+                    other_mixed = pltpu.roll(mode_part(mixed, modes, k, 0), NY, 1)
+                    part = part + (other_face * own_mixed - own_face * other_mixed)
+                total_ref[l, 0] = own_total_ref[l, 0] + jnp.where(low_half, part, zero)
+                total_ref[l, 1] = own_total_ref[l, 1] + jnp.where(low_half, zero, part)
+
+        def read_edge(l, t):
+            return own_edge_ref[l, t] if t < first else edge_ref[l, t]
+
         for l in range(layers):
-            spread = neighbour_sums(edge_ref, l, count, masks)
+            spread = neighbour_sums(read_edge, l, layers, count, masks)
             for t in range(full):
                 diffused = total_ref[l, t] - spread[t]
                 if t >= OWN_TILES:
-                    first, second = inside[(t + 1) % 2], inside[t % 2]
-                    diffused = diffused * jnp.where(low_half, first, second)
+                    lower, upper = inside[(t + 1) % 2], inside[t % 2]
+                    diffused = diffused * jnp.where(low_half, lower, upper)
                 residual = r_ref[l, t] - diffused
                 if step == ITERS - 1:
                     send(1, l, t, residual)
@@ -418,6 +521,10 @@
     kinds = in_kinds or [pltpu.VMEM] * len(arrays)
     in_specs = [pl.BlockSpec(memory_space=pltpu.SMEM)] * len(scalars) + [
         pl.BlockSpec(memory_space=kind) for kind in kinds
+    ]
+    arrays = [
+        pltpu.with_memory_space_constraint(x, kind) if kind == pltpu.HBM else x
+        for x, kind in zip(arrays, kinds)
     ]
     moved = sum(4 * x.size for x in arrays) + sum(4 * x.size for x in outs)
     return pl.pallas_call(
@@ -488,8 +595,12 @@
             by_blocks(mean_conductivity).reshape(-1, LANES),
             by_blocks(mode_shapes).reshape(-1, LANES),
         ],
-        [pltpu.SemaphoreType.DMA((devices,))],
-        in_kinds=[pltpu.HBM, pltpu.VMEM, pltpu.VMEM],
+        [
+            pltpu.VMEM((devices * pieces, LANES), f32),
+            pltpu.VMEM(((modes - 1) * devices * pieces, LANES), f32),
+            pltpu.SemaphoreType.DMA((devices + 2,)),
+        ],
+        in_kinds=[pltpu.HBM] * 3,
     )[0]
     gathered = lax.all_to_all(scattered, BOTH, 0, 0, tiled=True).reshape(-1, LANES)
 
@@ -506,7 +617,8 @@
     scales = jnp.stack(scales)
 
     message = shape((layers + layers // 2) * slots + modes * OWN_TILES * layers, LANES)
-    start, own_a, up, down = call(
+    odd = (block % 2)[None]
+    start, own_a, to_chip, to_core = call(
         functools.partial(start_kernel, chaos, spaces, modes),
         [
             shape(layers, OWN_TILES, slots, LANES),
@@ -514,14 +626,26 @@
             message,
             message,
         ],
-        [],
-        [weight, gathered],
+        [odd, scales],
+        [mix, weight, gathered],
     )
     place = {n: device for device, n in enumerate(blocks)}
-    upward = [(place[n], place[n + 1]) for n in range(devices - 1)]
-    downward = [(place[n + 1], place[n]) for n in range(devices - 1)]
-    from_below = lax.ppermute(up, BOTH, upward)
-    from_above = lax.ppermute(down, BOTH, downward)
+
+    def swap(field, lowest):
+        pairs = [(place[n], place[n + 1]) for n in range(lowest, devices - 1, 2)]
+        return lax.ppermute(field, BOTH, pairs + [(b, a) for a, b in pairs])
+
+    from_chip = swap(to_chip, 1)
+    from_core = swap(to_core, 0)
+    own_field = shape(layers, OWN_TILES, slots, LANES)
+    own_total, own_edge = call(
+        own_kernel,
+        [own_field, own_field],
+        [scales],
+        [mix, own_a, start],
+        [pltpu.VMEM((modes, layers, OWN_TILES * LANES), f32)],
+        flops=3000000000,
+    )
 
     def held(tiles):
         return pltpu.VMEM((layers, tiles, slots, LANES), f32)
@@ -529,11 +653,12 @@
     sent = call(
         functools.partial(iterate_kernel, chaos, spaces),
         [shape(devices * 2 * own * pieces, LANES)],
-        [scales, inside],
-        [mix, own_a, unweight, start, from_below, from_above],
+        [scales, inside, odd],
+        [mix, own_a, unweight, start, own_total, own_edge, from_chip, from_core],
         [
             pltpu.VMEM((modes, layers, FOLDED * LANES), f32),
             pltpu.VMEM((modes, layers, (FOLDED - 1) * LANES), f32),
+            pltpu.VMEM((modes, layers, 2 * LANES), f32),
             held(FOLDED - 1),
             held(FOLDED),
             held(FOLDED - 1),
@@ -568,6 +693,7 @@
         thick * spaces == 8
         and cells == chaos * spaces * OWN_TILES * LANES
         and (own * chaos) % 8 == 0
+        and spaces % 2 == 0
         and chaos == OWN_TILES * thick
         and chaos <= mode_shapes.shape[0] < 2 * chaos
     )

time: 100 us -> 94.9 us (0.949)
  waiting for transfers between devices: 23 us -> 19.6 us
  local copies, waits for them, and re-layouts: 3.68 us -> 0.9 us
  Pallas kernels: 16.6 us -> 19.1 us
  starting transfers between devices: 12.1 us -> 10.3 us
    all_to_all x1, waiting for transfers between devices: 17.9 us -> 13.7 us  [local_by_cells(): lax.all_to_all(scattered, BOTH, 0, 0, tiled=True).reshape(-1, LANES)]
    unnamed x12 -> x6, local copies, waits for them, and re-layouts: 2.8 us -> 0.01 us
    pallas_call x4 -> x5, Pallas kernels: 16.6 us -> 19.1 us  [call(): pl.pallas_call(kernel, out_shape=outs, in_specs=in_specs, out_specs=[pl.B...]
    ppermute x2, starting transfers between devices: 4.79 us -> 2.93 us  [swap(): return lax.ppermute(field, BOTH, pairs + [(b, a) for a, b in pairs])]
  transfers between devices with their start and end apart: 3 -> 3, of which waited for: 3 -> 2; matrix products, arithmetic and copies ran while one was open for 2% -> 2% of each run, Pallas kernels for 0% -> 3%
where the time goes in v3:
time: 94.9 us; the launch traced here: 94.6 us
  blocking collectives  39.8 us (42%)
  waiting for transfers between devices  19.6 us (21%)
  Pallas kernels  19.1 us (20%)
  starting transfers between devices  10.3 us (11%)
  between operations  3.68 us (4%)
    all_to_all x1, blocking collectives, local_by_cells(): received = lax.all_to_all(sent, BOTH, 0, 0, tiled=True)  39.8 us
    pallas_call x5, Pallas kernels, call(): pl.pallas_call(kernel, out_shape=outs, in_specs=in_specs, out_specs=[pl.B...  19.1 us
    all_to_all x1, waiting for transfers between devices, local_by_cells(): lax.all_to_all(scattered, BOTH, 0, 0, tiled=True).reshape(-1, LANES)  13.7 us
    all_to_all x1, starting transfers between devices, local_by_cells(): lax.all_to_all(scattered, BOTH, 0, 0, tiled=True).reshape(-1, LANES)  7.33 us
    ppermute x2, waiting for transfers between devices, swap(): return lax.ppermute(field, BOTH, pairs + [(b, a) for a, b in pairs])  5.95 us
    ppermute x2, starting transfers between devices, swap(): return lax.ppermute(field, BOTH, pairs + [(b, a) for a, b in pairs])  2.93 us
  transfers between devices with their start and end apart: 3, of which 2 were waited for; matrix products, arithmetic and copies ran while one was open for 2% of the time, Pallas kernels for 3%

profile of v3, /device:TPU:1, one launch (start us, length us, event | category | flops | bytes accessed | tf_op | source)
XLA Modules:
  0.0 94.6 jit_solution(8191079755367900300)
XLA Ops:
  0.6 0.0 copy-start.1
  0.6 0.0 copy-start.2
  0.7 0.0 copy-start
  0.7 2.2 %shard_map.77 = f32[16,24,4,128]{3,2,1,0:T(4,128)} custom-call(s32[1]{0:T(128)} %bitcast.16.chaos_index, f32[22,16,4,128]{3,2,1,0:T(4,128)} %bitcast.51, f32[64,128]{1,0:T(8,128)} %bitcast.54, f32[384,128]{1,0:T(8,128)} %bitcast.53), custom_call_target="tpu_custom_call" | custom-call | bytes 1736704 | tf_op jit(solution)/shard_map/pallas_call | solution.py:530
  2.9 7.3 %all-to-all-start = ((f32[16,24,4,128]{3,2,1,0:T(4,128)}), f32[16,24,4,128]{3,2,1,0:T(4,128)S(1)}, u32[]{:S(2)}, u32[]{:S(2)}) async-start(f32[16,24,4,128]{3,2,1,0:T(4,128)} %shard_map.77), calls=%async_computation | async-start | bytes 1572864 | tf_op jit(solution)/shard_map/all_to_all | solution.py:605
  10.3 0.0 copy-done.1
  10.3 0.0 copy-done.2
  10.3 0.6 fusion.17
  13.8 0.0 copy-done
  13.8 0.4 fusion.2
  14.2 0.4 fusion
  14.7 0.1 stack.32.scales
  14.8 0.1 convert_reduce_fusion
  15.0 0.1 pad_maximum_fusion.mix_ref
  15.1 13.7 %all-to-all-done = f32[16,24,4,128]{3,2,1,0:T(4,128)S(1)} async-done(((f32[16,24,4,128]{3,2,1,0:T(4,128)}), f32[16,24,4,128]{3,2,1,0:T(4,128)S(1)}, u32[]{:S(2)}, u32[]{:S(2)}) %all-to-all-start) | async-done | bytes 786464 | tf_op jit(solution)/shard_map/all_to_all | solution.py:605
  28.8 0.1 mul.67.weight_ref
  28.9 1.6 %shard_map.78 = (f32[8,2,88,128]{3,2,1,0:T(8,128)S(1)}, f32[7,2,8,128]{3,2,1,0:T(8,128)S(1)}, f32[1168,128]{1,0:T(8,128)}, f32[1168,128]{1,0:T(8,128)S(1)}) custom-call(s32[1]{0:T(128)} %bitcast.9.odd, f32[5]{0:T(128)S(1)} %stack.32.scales, bf16[528,192]{1,0:T(8,128)(2,1)S(1)} %pad_maximum_fusion.mix_ref, f32[88,128]{1,0:T(8,128)S(1)} %mul.67.weight_ref, ...), custom_call_target="tpu_custom_call" | custom-call | bytes 3211264 | tf_op jit(solution)/shard_map/pallas_call | solution.py:530
  30.4 2.9 %collective-permute-start = (f32[1168,128]{1,0:T(8,128)}, f32[1168,128]{1,0:T(8,128)S(1)}, u32[]{:S(2)}, u32[]{:S(2)}) collective-permute-start(f32[1168,128]{1,0:T(8,128)} %get-tuple-element.14), channel_id=1, source_target_pairs={{1,2},{3,7},{6,5},{4,8},{9,10},{11,15},{14,13},{2,1},{7,3},{5,6},{... | collective-permute-start | bytes 1794056 | tf_op jit(solution)/shard_map/ppermute | solution.py:636
  33.3 0.1 collective-permute-start.1
  33.4 0.1 add_convert_fusion.inside
  33.5 2.5 %shard_map.79 = (f32[8,2,88,128]{3,2,1,0:T(8,128)S(1)}, f32[8,2,88,128]{3,2,1,0:T(8,128)S(1)}) custom-call(f32[5]{0:T(128)S(1)} %stack.32.scales, bf16[528,192]{1,0:T(8,128)(2,1)S(1)} %pad_maximum_fusion.mix_ref, f32[7,2,8,128]{3,2,1,0:T(8,128)S(1)} %get-tuple-element.10.own_a_ref, f32[8,2,88,128]{3,2,1,0:T(8,128)S(1)} %get-tuple-element.11.start_ref), custom_call_target="tpu_custom_call" | custom-call | flops 3000000000 | bytes 2625536 | tf_op jit(solution)/shard_map/pallas_call | solution.py:530
  36.0 5.9 %collective-permute-done.chip_ref = f32[1168,128]{1,0:T(8,128)S(1)} collective-permute-done((f32[1168,128]{1,0:T(8,128)}, f32[1168,128]{1,0:T(8,128)S(1)}, u32[]{:S(2)}, u32[]{:S(2)}) %collective-permute-start) | collective-permute-done | bytes 598048 | tf_op jit(solution)/shard_map/ppermute | solution.py:636
  41.9 0.0 collective-permute-done.1.core_ref
  41.9 0.1 mul.68.unweight_ref
  42.0 11.4 %shard_map.80 = f32[2816,128]{1,0:T(8,128)S(1)} custom-call(f32[5]{0:T(128)S(1)} %stack.32.scales, f32[2]{0:T(128)S(1)} %add_convert_fusion.inside, s32[1]{0:T(128)} %bitcast.9.odd, bf16[528,192]{1,0:T(8,128)(2,1)S(1)} %pad_maximum_fusion.mix_ref, f32[7,2,8,128]{3,2,1,0:T(8,128)S(1)} %get-tuple-element.10.own_a_ref, f32[88,128]{1,0:T(8,128)S(1)} %mul.68.unweight_ref, ...), custom_call_target="tpu_custom_call" | custom-call | flops 10000000000 | bytes 5308416 | tf_op jit(solution)/shard_map/pallas_call | solution.py:530
  53.5 39.8 %all_to_all.10.in_ref = f32[16,2,22,4,128]{4,3,2,1,0:T(4,128)S(1)} all-to-all(f32[16,2,22,4,128]{4,3,2,1,0:T(4,128)S(1)} %bitcast.50), channel_id=1, replica_groups=mesh['groups'=2,'chaos'=4,'space'=4] {'chaos','space'}, dimensions={0} | all-to-all | bytes 2883584 | tf_op jit(solution)/shard_map/all_to_all | solution.py:671
  93.2 1.4 %shard_map.81 = (f32[22,16,4,128]{3,2,1,0:T(4,128)}, f32[22,16,4,128]{3,2,1,0:T(4,128)}) custom-call(f32[16,2,22,4,128]{4,3,2,1,0:T(4,128)S(1)} %all_to_all.10.in_ref), custom_call_target="tpu_custom_call" | custom-call | bytes 2883584 | tf_op jit(solution)/shard_map/pallas_call | solution.py:530
  (7 shorter events, 0.1 us)
Async XLA Ops:
  0.6 9.6 %copy-start.1 = (s32[6,28,3]{1,2,0:T(4,128)S(1)}, s32[6,28,3]{1,2,0:T(4,128)}, u32[]{:S(2)}) copy-start(s32[6,28,3]{1,2,0:T(4,128)} %param.9) | copy-start | bytes 6052
  0.6 9.6 %copy-start.2 = (f32[2]{0:T(128)S(1)}, f32[2]{0:T(128)}, u32[]{:S(2)}) copy-start(f32[2]{0:T(128)} %param.11) | copy-start | bytes 28
  0.7 13.1 %copy-start = (s32[88]{0:T(128)S(1)}, s32[88]{0:T(128)}, u32[]{:S(2)}) copy-start(s32[88]{0:T(128)} %param.10) | copy-start | bytes 1060
  2.9 25.9 %all-to-all-start = ((f32[16,24,4,128]{3,2,1,0:T(4,128)}), f32[16,24,4,128]{3,2,1,0:T(4,128)S(1)}, u32[]{:S(2)}, u32[]{:S(2)}) async-start(f32[16,24,4,128]{3,2,1,0:T(4,128)} %shard_map.77), calls=%async_computation | async-start | bytes 1572864 | tf_op jit(solution)/shard_map/all_to_all | solution.py:605
  30.4 11.5 %collective-permute-start = (f32[1168,128]{1,0:T(8,128)}, f32[1168,128]{1,0:T(8,128)S(1)}, u32[]{:S(2)}, u32[]{:S(2)}) collective-permute-start(f32[1168,128]{1,0:T(8,128)} %get-tuple-element.14), channel_id=1, source_target_pairs={{1,2},{3,7},{6,5},{4,8},{9,10},{11,15},{14,13},{2,1},{7,3},{5,6},{... | collective-permute-start | bytes 1794056 | tf_op jit(solution)/shard_map/ppermute | solution.py:636
  33.3 8.6 %collective-permute-start.1 = (f32[1168,128]{1,0:T(8,128)S(1)}, f32[1168,128]{1,0:T(8,128)S(1)}, u32[]{:S(2)}, u32[]{:S(2)}) collective-permute-start(f32[1168,128]{1,0:T(8,128)S(1)} %get-tuple-element.15), channel_id=1, source_target_pairs={{0,1},{2,3},{7,6},{5,4},{8,9},{10,11},{15,14},{13,12},{1,0},{3,2},... | collective-permute-start | bytes 1794056 | tf_op jit(solution)/shard_map/ppermute | solution.py:636

commit v4 on v3

--- a/solution.py
+++ b/solution.py
@@ -174,39 +174,87 @@
         copy.wait()
 
 
-def scatter_kernel(
-    blocks, chaos_index, in_ref, mean_ref, modes_ref, out_ref, mean_held, modes_held, sems
-):
-    own, devices, pieces, _ = in_ref.shape
-    modes = modes_ref.shape[0] // (devices * pieces)
-    small = [
-        pltpu.make_async_copy(mean_ref, mean_held, sems.at[devices]),
-        pltpu.make_async_copy(modes_ref, modes_held, sems.at[devices + 1]),
+def scatter_kernel(blocks, in_ref, out_ref, held_ref, sems):
+    own = in_ref.shape[0]
+    parts = sems.shape[0]
+    bounds = [own * n // parts for n in range(parts + 1)]
+    spans = [pl.ds(a, b - a) for a, b in zip(bounds[:-1], bounds[1:])]
+    copies = [
+        pltpu.make_async_copy(in_ref.at[span], held_ref.at[span], sems.at[n])
+        for n, span in enumerate(spans)
     ]
-    copies = [
-        pltpu.make_async_copy(
-            in_ref.at[:, block], out_ref.at[device, pl.ds(0, own)], sems.at[device]
-        )
-        for device, block in enumerate(blocks)
-    ]
-    for copy in small + copies:
+    for copy in copies:
         copy.start()
-    for copy in small:
+    for copy, span in zip(copies, spans):
         copy.wait()
-    for device, block in enumerate(blocks):
-        row = block * pieces + chaos_index[0]
-        values = modes_held[pl.ds(row, modes, stride=devices * pieces), :]
-        out_ref[device, own] = values[:pieces]
-        out_ref[device, own + 1] = jnp.concatenate(
-            [
-                values[pieces:],
-                mean_held[pl.ds(row, 1), :],
-                jnp.zeros((2 * pieces - modes - 1, LANES), jnp.float32),
-            ],
-            axis=0,
-        )
-    for copy in copies:
-        copy.wait()
+        for device, block in enumerate(blocks):
+            out_ref[device, span] = held_ref[span, block]
+
+
+def pick_kernel(targets, scales, mix_ref, mean_ref, modes_ref, *outs):
+    count, per_mode = mean_ref.shape[0], outs[0].shape[0] // (1 + modes_ref.shape[0] // mean_ref.shape[0])
+    side = per_mode // 3
+    last = count // side - 1
+    for n, out_ref in enumerate(outs):
+        block = targets[n]
+        lower = jnp.where(block > 0, 1.0, 0.0)
+        upper = jnp.where(block < last, 1.0, 0.0)
+        before = jnp.maximum(block - 1, 0) * side
+        after = jnp.minimum(block + 1, last) * side
+        for k in range(out_ref.shape[0] // per_mode):
+            ref, base = (mean_ref, 0) if k == 0 else (modes_ref, (k - 1) * count)
+            first = k * per_mode
+            out_ref[pl.ds(first, side), :] = ref[pl.ds(base + before, side), :] * lower
+            out_ref[pl.ds(first + side, side), :] = ref[pl.ds(base + block * side, side), :]
+            out_ref[pl.ds(first + 2 * side, side), :] = ref[pl.ds(base + after, side), :] * upper
+
+
+def layer_sum(values, layer):
+    layers = values.shape[0]
+    zero = jnp.zeros(values.shape, jnp.float32)
+    under = jnp.where(layer > 0, pltpu.roll(values, 1, 0), zero)
+    over = jnp.where(layer < layers - 1, pltpu.roll(values, layers - 1, 0), zero)
+    return under + over
+
+
+def coefficient_kernel(thick, sources, *refs):
+    *ins, a_ref, b_ref, own_b_ref, face_ref, held_ref = refs
+    modes, layers, _ = a_ref.shape
+    tiles = held_ref.shape[1]
+    layer = lax.broadcasted_iota(jnp.int32, (layers, LANES), 0)
+    masks = lane_masks(layers)
+    low_half = masks[0]
+    for n, in_ref in enumerate(ins):
+        for k in range(modes):
+            for u in range(tiles):
+                held_ref[k, u, pl.ds(sources[n] * thick, thick), :] = in_ref[
+                    pl.ds((k * tiles + u) * thick, thick), :
+                ]
+    mean = None
+    for k in range(modes):
+        runs = [held_ref[k, u] for u in range(tiles)]
+        values = [
+            runs[2],
+            runs[3],
+            jnp.where(low_half, runs[4], runs[1]),
+            jnp.where(low_half, runs[1], runs[4]),
+            jnp.where(low_half, runs[5], runs[0]),
+        ]
+        if k == 0:
+            values = mean = [0.5 * value for value in values]
+        else:
+            values = [m * value for m, value in zip(mean, values)]
+        sums = plane_sums(values, masks)
+        for t in range(FOLDED):
+            a_ref[k, :, lanes(t)] = values[t]
+        for t in range(FOLDED - 1):
+            b_ref[k, :, lanes(t)] = 6.0 * values[t] + (sums[t] + layer_sum(values[t], layer))
+        outside = jnp.zeros((layers, LANES), jnp.float32)
+        sums = plane_sums(values[:OWN_TILES] + [outside], masks)
+        for t in range(OWN_TILES):
+            own_b_ref[k, :, lanes(t)] = 6.0 * values[t] + (sums[t] + layer_sum(values[t], layer))
+        face_ref[k, :, lanes(0)] = jnp.where(low_half, values[0], values[1])
+        face_ref[k, :, lanes(1)] = pltpu.roll(values[2], NY, 1)
 
 
 def collect_kernel(blocks, in_ref, *rest):
@@ -222,68 +270,52 @@
     )
 
 
-def start_kernel(
-    chaos,
-    spaces,
-    modes,
-    odd,
-    scales,
-    mix_ref,
-    weight_ref,
-    in_ref,
-    residual_ref,
-    a_ref,
-    chip_ref,
-    core_ref,
-):
+def slot_parts(own, chaos):
+    whole = own // 8 * 8
+    parts = [(c, 0, whole, c * whole) for c in range(chaos)]
+    return parts + [
+        (c, whole, own - whole, chaos * whole + c * (own - whole)) for c in range(chaos)
+    ]
+
+
+def start_kernel(chaos, spaces, odd, a_ref, weight_ref, in_ref, residual_ref, chip_ref, core_ref):
     upward = odd[0] > 0
     layers, tiles, slots, _ = residual_ref.shape
     own = slots // chaos
     thick = layers // spaces
     pieces = tiles * thick
-    block = (own + 2) * pieces
     half = layers // 2
     low_half = lane_masks(slots)[0]
     weight = weight_ref[...]
 
-    def put(rows, up, down):
+    def put(place, up, down):
+        rows = pl.ds(place * slots, slots)
         chip_ref[rows, :] = jnp.where(upward, up, down)
         core_ref[rows, :] = jnp.where(upward, down, up)
 
     for l in range(layers):
         i, z = divmod(l, thick)
         for t in range(tiles):
-            first = t * thick + z
-            residual_ref[l, t] = weight * jnp.concatenate(
-                [
-                    in_ref[pl.ds((c * spaces + i) * block + first, own, stride=pieces), :]
-                    for c in range(chaos)
-                ],
-                axis=0,
-            )
-        put(pl.ds(l * slots, slots), residual_ref[l, 1], residual_ref[l, 0])
+            rows = [
+                in_ref[
+                    pl.ds(
+                        ((c * spaces + i) * own + slot) * pieces + t * thick + z,
+                        number,
+                        stride=pieces,
+                    ),
+                    :,
+                ]
+                for c, slot, number, _ in slot_parts(own, chaos)
+            ]
+            residual_ref[l, t] = weight * jnp.concatenate(rows, axis=0)
+        put(l, residual_ref[l, 1], residual_ref[l, 0])
     for l in range(half):
         later = l + half
         put(
-            pl.ds((layers + l) * slots, slots),
+            layers + l,
             jnp.where(low_half, pltpu.roll(residual_ref[later, 0], NY, 1), residual_ref[l, 0]),
             jnp.where(low_half, residual_ref[l, 1], pltpu.roll(residual_ref[later, 1], NY, 1)),
         )
-
-    for t in range(tiles):
-        for z in range(thick):
-            for k in range(modes):
-                first = (t * thick + z) * spaces * block + own * pieces
-                first += k - 1 if k > 0 else modes - 1
-                a_ref[k, t, pl.ds(z, spaces, stride=thick), :] = in_ref[
-                    pl.ds(first, spaces, stride=block), :
-                ]
-        mean = 0.5 * a_ref[0, t]
-        for k in range(modes):
-            value = mean if k == 0 else mean * a_ref[k, t]
-            a_ref[k, t] = value
-            rows = pl.ds((layers + half) * slots + (k * tiles + t) * layers, layers)
-            put(rows, value, value)
 
 
 def mode_part(mixed, modes, k, n):
@@ -297,43 +329,28 @@
     )
 
 
-def layer_sum(values, layer):
-    layers = values.shape[0]
-    zero = jnp.zeros(values.shape, jnp.float32)
-    under = jnp.where(layer > 0, pltpu.roll(values, 1, 0), zero)
-    over = jnp.where(layer < layers - 1, pltpu.roll(values, layers - 1, 0), zero)
-    return under + over
-
-
-def weighted_tiles(mixed, modes, count, full, direct, around, a_of, b_of):
+def weighted_tiles(mixed, modes, place, beside, direct, around, a_of, b_of):
     results = []
-    for t in range(count):
+    for t, tile in enumerate(direct):
+        full = t < len(around)
         a = a_of(0, t)
-        edge = a * direct[t]
-        total = b_of(0, t) * direct[t] - a * around[t] if t < full else None
+        edge = a * tile
+        total = b_of(0, t) * tile - a * around[t] if full else None
         for k in range(1, modes):
             a = a_of(k, t)
-            part = mode_part(mixed, modes, k, t)
+            part = mode_part(mixed, modes, k, place + t)
             edge = edge + a * part
-            if t < full:
-                beside = mode_part(mixed, modes, k, mixed.shape[1] // LANES - full + t)
-                total = total + (b_of(k, t) * part - a * beside)
+            if full:
+                total = total + (b_of(k, t) * part - a * mode_part(mixed, modes, k, beside + t))
         results.append((total, edge))
     return results
 
 
-def own_kernel(scales, mix_ref, own_a_ref, start_ref, total_ref, edge_ref, b_ref):
+def own_kernel(scales, mix_ref, a_ref, b_ref, start_ref, total_ref, edge_ref):
     layers, tiles, slots, _ = start_ref.shape
-    modes = own_a_ref.shape[0]
+    modes = a_ref.shape[0]
     masks = lane_masks(slots)
     mix = mix_ref[...]
-    layer = lax.broadcasted_iota(jnp.int32, (layers, LANES), 0)
-    outside = jnp.zeros((layers, LANES), jnp.float32)
-    for k in range(modes):
-        values = [own_a_ref[k, t] for t in range(tiles)]
-        sums = plane_sums(values + [outside], lane_masks(layers))
-        for t in range(tiles):
-            b_ref[k, :, lanes(t)] = 6.0 * values[t] + (sums[t] + layer_sum(values[t], layer))
     nothing = jnp.zeros((slots, LANES), jnp.float32)
 
     def read(l, t):
@@ -348,11 +365,11 @@
         results = weighted_tiles(
             mixed,
             modes,
-            tiles,
+            0,
             tiles,
             direct,
             around,
-            lambda k, t: own_a_ref[k, t, l : l + 1, :],
+            lambda k, t: a_ref[k, l : l + 1, lanes(t)],
             lambda k, t: b_ref[k, l : l + 1, lanes(t)],
         )
         for t, (total, edge) in enumerate(results):
@@ -367,7 +384,9 @@
     inside,
     odd,
     mix_ref,
-    own_a_ref,
+    a_ref,
+    b_ref,
+    face_ref,
     unweight_ref,
     start_ref,
     own_total_ref,
@@ -375,9 +394,6 @@
     chip_ref,
     core_ref,
     sent_ref,
-    a_ref,
-    b_ref,
-    face_ref,
     r_ref,
     d_ref,
     total_ref,
@@ -385,7 +401,7 @@
     x_ref,
 ):
     layers, _, slots, _ = start_ref.shape
-    modes = own_a_ref.shape[0]
+    modes = a_ref.shape[0]
     own = slots // chaos
     thick = layers // spaces
     pieces = OWN_TILES * thick
@@ -403,30 +419,9 @@
     def send(field, l, t, value):
         i, z = divmod(l, thick)
         value = value * unweight_ref[...]
-        for c in range(chaos):
-            first = ((c * spaces + i) * 2 + field) * own * pieces + t * thick + z
-            sent_ref[pl.ds(first, own, stride=pieces), :] = value[c * own : (c + 1) * own]
-
-    layer = lax.broadcasted_iota(jnp.int32, (layers, LANES), 0)
-    narrow_masks = lane_masks(layers)
-    low = narrow_masks[0]
-    for k in range(modes):
-        places = [(layers + half) * slots + (k * OWN_TILES + t) * layers for t in range(OWN_TILES)]
-        below, above = zip(*[message(place, layers) for place in places])
-        values = [
-            own_a_ref[k, 0],
-            own_a_ref[k, 1],
-            jnp.where(low, above[0], below[1]),
-            jnp.where(low, below[1], above[0]),
-            jnp.where(low, above[1], below[0]),
-        ]
-        sums = plane_sums(values, narrow_masks)
-        for t in range(FOLDED):
-            a_ref[k, :, lanes(t)] = values[t]
-        for t in range(FOLDED - 1):
-            b_ref[k, :, lanes(t)] = 6.0 * values[t] + (sums[t] + layer_sum(values[t], layer))
-        face_ref[k, :, lanes(0)] = jnp.where(low, values[0], values[1])
-        face_ref[k, :, lanes(1)] = pltpu.roll(values[2], NY, 1)
+        for c, slot, number, row in slot_parts(own, chaos):
+            first = (((c * spaces + i) * 2 + field) * own + slot) * pieces + t * thick + z
+            sent_ref[pl.ds(first, number, stride=pieces), :] = value[row : row + number]
 
     for l in range(layers):
         below, above = message(l * slots, slots)
@@ -455,38 +450,45 @@
         count = FOLDED - step
         full = count - 1
         first = OWN_TILES if step == 0 else 0
-        for l in range(layers):
-            direct = [d_ref[l, t] for t in range(first, count)]
-            around = neighbour_sums(read, l, layers, count, masks, first)
-            extra = []
-            if step == 0:
-                extra = [jnp.where(low_half, d_ref[l, 0], d_ref[l, 1])]
+        group = 1 if step == 0 else 2
+        for lowest in range(0, layers, group):
+            gathered, stacked = [], []
+            for l in range(lowest, lowest + group):
+                direct = [d_ref[l, t] for t in range(first, count)]
+                around = neighbour_sums(read, l, layers, count, masks, first)
+                extra = []
+                if step == 0:
+                    extra = [jnp.where(low_half, d_ref[l, 0], d_ref[l, 1])]
+                gathered.append((l, len(stacked), direct, extra, around))
+                stacked += direct + extra + around
             mixed = jnp.dot(
-                mix, split_stack(direct + extra + around, depth), preferred_element_type=jnp.float32
+                mix, split_stack(stacked, depth), preferred_element_type=jnp.float32
             )
-            results = weighted_tiles(
-                mixed,
-                modes,
-                count - first,
-                full - first,
-                direct,
-                around,
-                lambda k, t: a_ref[k, l : l + 1, lanes(first + t)],
-                lambda k, t: b_ref[k, l : l + 1, lanes(first + t)],
-            )
-            for t, (total, edge) in enumerate(results):
-                edge_ref[l, first + t] = edge
-                if first + t < full:
-                    total_ref[l, first + t] = total
-            if step == 0:
+            for l, place, direct, extra, around in gathered:
+                results = weighted_tiles(
+                    mixed,
+                    modes,
+                    place,
+                    place + len(direct) + len(extra),
+                    direct,
+                    around,
+                    lambda k, t: a_ref[k, l : l + 1, lanes(first + t)],
+                    lambda k, t: b_ref[k, l : l + 1, lanes(first + t)],
+                )
+                for t, (total, edge) in enumerate(results):
+                    edge_ref[l, first + t] = edge
+                    if first + t < full:
+                        total_ref[l, first + t] = total
+                if not extra:
+                    continue
                 own_face = face_ref[0, l : l + 1, lanes(0)]
                 other_face = face_ref[0, l : l + 1, lanes(1)]
                 part = other_face * extra[0] - own_face * pltpu.roll(direct[0], NY, 1)
                 for k in range(1, modes):
                     own_face = face_ref[k, l : l + 1, lanes(0)]
                     other_face = face_ref[k, l : l + 1, lanes(1)]
-                    own_mixed = mode_part(mixed, modes, k, len(direct))
-                    other_mixed = pltpu.roll(mode_part(mixed, modes, k, 0), NY, 1)
+                    own_mixed = mode_part(mixed, modes, k, place + len(direct))
+                    other_mixed = pltpu.roll(mode_part(mixed, modes, k, place), NY, 1)
                     part = part + (other_face * own_mixed - own_face * other_mixed)
                 total_ref[l, 0] = own_total_ref[l, 0] + jnp.where(low_half, part, zero)
                 total_ref[l, 1] = own_total_ref[l, 1] + jnp.where(low_half, zero, part)
@@ -538,9 +540,16 @@
     )(*scalars, *arrays)
 
 
-def coupling_tables(coupling, slot_term):
+def coupling_tables(coupling, slot_term, chaos):
     bf16 = jnp.bfloat16
     slots = slot_term.shape[0]
+    by_source = slot_term.reshape(chaos, -1)
+    slot_term = jnp.concatenate(
+        [
+            by_source[c, slot : slot + number]
+            for c, slot, number, _ in slot_parts(slots // chaos, chaos)
+        ]
+    )
     raising = (slot_term[None, None, :] == coupling[:, :, 0:1]).astype(bf16)
     lowering = (slot_term[None, None, :] == coupling[:, :, 1:2]).astype(bf16)
     weighted = raising * coupling[:, :, 2:3].astype(bf16)
@@ -577,34 +586,7 @@
     def shape(*sizes):
         return jax.ShapeDtypeStruct(sizes, f32)
 
-    def by_blocks(field):
-        lead = field.shape[:-2]
-        tiled = field.reshape(*lead, thick, columns, LANES)
-        return jnp.swapaxes(tiled, -3, -2)
-
-    row, column = lax.axis_index("chaos"), lax.axis_index("space")
-    block = row * spaces + jnp.where(row % 2 == 0, column, spaces - 1 - column)
-    inside = jnp.stack([block > 0, block < devices - 1]).astype(f32)
-    modes = mode_shapes.shape[0] + 1
-    scattered = call(
-        functools.partial(scatter_kernel, blocks),
-        [shape(devices, own + 2, pieces, LANES)],
-        [row[None]],
-        [
-            by_blocks(source_chaos_terms).reshape(own, devices, pieces, LANES),
-            by_blocks(mean_conductivity).reshape(-1, LANES),
-            by_blocks(mode_shapes).reshape(-1, LANES),
-        ],
-        [
-            pltpu.VMEM((devices * pieces, LANES), f32),
-            pltpu.VMEM(((modes - 1) * devices * pieces, LANES), f32),
-            pltpu.SemaphoreType.DMA((devices + 2,)),
-        ],
-        in_kinds=[pltpu.HBM] * 3,
-    )[0]
-    gathered = lax.all_to_all(scattered, BOTH, 0, 0, tiled=True).reshape(-1, LANES)
-
-    mix, weight, unweight = coupling_tables(coupling, slot_term)
+    mix, weight, unweight = coupling_tables(coupling, slot_term, chaos)
     midpoint = 0.5 * (bounds[1] + bounds[0])
     half_span = 0.5 * (bounds[1] - bounds[0])
     sigma_one = midpoint / half_span
@@ -616,18 +598,58 @@
         rho_now = rho_next
     scales = jnp.stack(scales)
 
-    message = shape((layers + layers // 2) * slots + modes * OWN_TILES * layers, LANES)
+    def by_columns(field):
+        tiled = field.reshape(*field.shape[:-2], thick, columns, LANES)
+        return jnp.swapaxes(tiled, -3, -2)
+
+    scattered = call(
+        functools.partial(scatter_kernel, blocks),
+        [shape(devices, own, pieces, LANES)],
+        [],
+        [by_columns(source_chaos_terms).reshape(own, devices, pieces, LANES)],
+        [pltpu.VMEM((own, devices, pieces, LANES), f32), pltpu.SemaphoreType.DMA((2,))],
+        in_kinds=[pltpu.HBM],
+    )[0]
+    gathered = lax.all_to_all(scattered, BOTH, 0, 0, tiled=True).reshape(-1, LANES)
+
+    row, column = lax.axis_index("chaos"), lax.axis_index("space")
+
+    def block_at(space):
+        return row * spaces + jnp.where(row % 2 == 0, space, spaces - 1 - space)
+
+    block = block_at(column)
+    inside = jnp.stack([block > 0, block < devices - 1]).astype(f32)
     odd = (block % 2)[None]
-    start, own_a, to_chip, to_core = call(
-        functools.partial(start_kernel, chaos, spaces, modes),
+    modes = mode_shapes.shape[0] + 1
+    steps = jnp.arange(spaces)
+    picked = call(
+        pick_kernel,
+        [shape(modes * 3 * pieces, LANES)] * spaces,
+        [block_at((column + steps) % spaces), scales],
         [
-            shape(layers, OWN_TILES, slots, LANES),
-            shape(modes, OWN_TILES, layers, LANES),
-            message,
-            message,
+            mix,
+            by_columns(mean_conductivity).reshape(-1, LANES),
+            by_columns(mode_shapes).reshape(-1, LANES),
         ],
-        [odd, scales],
-        [mix, weight, gathered],
+    )
+    picked = [picked[0]] + [
+        lax.ppermute(picked[n], "space", [(i, (i + n) % spaces) for i in range(spaces)])
+        for n in range(1, spaces)
+    ]
+    a, b, own_b, face = call(
+        functools.partial(coefficient_kernel, thick),
+        [shape(modes, layers, tiles * LANES) for tiles in (FOLDED, FOLDED - 1, OWN_TILES, 2)],
+        [(column - steps) % spaces],
+        picked,
+        [pltpu.VMEM((modes, 3 * OWN_TILES, layers, LANES), f32)],
+    )
+
+    message = shape((layers + layers // 2) * slots, LANES)
+    start, to_chip, to_core = call(
+        functools.partial(start_kernel, chaos, spaces),
+        [shape(layers, OWN_TILES, slots, LANES), message, message],
+        [odd],
+        [a, weight, gathered],
     )
     place = {n: device for device, n in enumerate(blocks)}
 
@@ -642,8 +664,7 @@
         own_kernel,
         [own_field, own_field],
         [scales],
-        [mix, own_a, start],
-        [pltpu.VMEM((modes, layers, OWN_TILES * LANES), f32)],
+        [mix, a, own_b, start],
         flops=3000000000,
     )
 
@@ -654,11 +675,8 @@
         functools.partial(iterate_kernel, chaos, spaces),
         [shape(devices * 2 * own * pieces, LANES)],
         [scales, inside, odd],
-        [mix, own_a, unweight, start, own_total, own_edge, from_chip, from_core],
+        [mix, a, b, face, unweight, start, own_total, own_edge, from_chip, from_core],
         [
-            pltpu.VMEM((modes, layers, FOLDED * LANES), f32),
-            pltpu.VMEM((modes, layers, (FOLDED - 1) * LANES), f32),
-            pltpu.VMEM((modes, layers, 2 * LANES), f32),
             held(FOLDED - 1),
             held(FOLDED),
             held(FOLDED - 1),
@@ -694,8 +712,6 @@
         and cells == chaos * spaces * OWN_TILES * LANES
         and (own * chaos) % 8 == 0
         and spaces % 2 == 0
-        and chaos == OWN_TILES * thick
-        and chaos <= mode_shapes.shape[0] < 2 * chaos
     )
     plan = local_by_cells if fits else local_by_slots
     return plan(

time: 94.9 us -> 92.9 us (0.979)
  waiting for transfers between devices: 19.6 us -> 14.3 us
  starting transfers between devices: 10.3 us -> 12.7 us
    all_to_all x1, waiting for transfers between devices: 13.7 us -> 5.42 us  [local_by_cells(): lax.all_to_all(scattered, BOTH, 0, 0, tiled=True).reshape(-1, LANES)]
    ppermute x0 -> x3, waiting for transfers between devices: none -> 3.42 us  [local_by_cells(): lax.ppermute(picked[n], 'space', [(i, (i + n) % spaces) for i in range(sp...]
    ppermute x0 -> x3, starting transfers between devices: none -> 2.23 us  [local_by_cells(): lax.ppermute(picked[n], 'space', [(i, (i + n) % spaces) for i in range(sp...]
    pallas_call x5 -> x7, Pallas kernels: 19.1 us -> 20 us  [call(): pl.pallas_call(kernel, out_shape=outs, in_specs=in_specs, out_specs=[pl.B...]
  transfers between devices with their start and end apart: 3 -> 6, of which waited for: 2 -> 5; matrix products, arithmetic and copies ran while one was open for 2% -> 2% of each run, Pallas kernels for 3% -> 4%
where the time goes in v4:
time: 92.9 us; the launch traced here: 92.6 us
  blocking collectives  39.5 us (43%)
  Pallas kernels  20 us (22%)
  waiting for transfers between devices  14.3 us (15%)
  starting transfers between devices  12.7 us (14%)
  between operations  3.71 us (4%)
  local copies, waits for them, and re-layouts  1.12 us (1%)
    all_to_all x1, blocking collectives, local_by_cells(): received = lax.all_to_all(sent, BOTH, 0, 0, tiled=True)  39.5 us
    pallas_call x7, Pallas kernels, call(): pl.pallas_call(kernel, out_shape=outs, in_specs=in_specs, out_specs=[pl.B...  20 us
    all_to_all x1, starting transfers between devices, local_by_cells(): lax.all_to_all(scattered, BOTH, 0, 0, tiled=True).reshape(-1, LANES)  7.47 us
    ppermute x2, waiting for transfers between devices, swap(): return lax.ppermute(field, BOTH, pairs + [(b, a) for a, b in pairs])  5.46 us
    all_to_all x1, waiting for transfers between devices, local_by_cells(): lax.all_to_all(scattered, BOTH, 0, 0, tiled=True).reshape(-1, LANES)  5.42 us
    ppermute x3, waiting for transfers between devices, local_by_cells(): lax.ppermute(picked[n], 'space', [(i, (i + n) % spaces) for i in range(sp...  3.42 us
    ppermute x2, starting transfers between devices, swap(): return lax.ppermute(field, BOTH, pairs + [(b, a) for a, b in pairs])  3.02 us
    ppermute x3, starting transfers between devices, local_by_cells(): lax.ppermute(picked[n], 'space', [(i, (i + n) % spaces) for i in range(sp...  2.23 us
  transfers between devices with their start and end apart: 6, of which 5 were waited for; matrix products, arithmetic and copies ran while one was open for 2% of the time, Pallas kernels for 4%

profile of v4, /device:TPU:1, one launch (start us, length us, event | category | flops | bytes accessed | tf_op | source)
XLA Modules:
  0.0 92.6 jit_solution(16754486736023022398)
XLA Ops:
  0.6 0.0 copy-start.3
  0.6 0.0 copy-start.4
  0.7 0.0 copy-start.2
  0.7 2.0 %shard_map.79 = f32[16,22,4,128]{3,2,1,0:T(4,128)} custom-call(f32[22,16,4,128]{3,2,1,0:T(4,128)} %bitcast.68), custom_call_target="tpu_custom_call" | custom-call | bytes 1441792 | tf_op jit(solution)/shard_map/pallas_call | solution.py:532
  2.7 0.0 copy-start
  2.7 0.0 copy-start.1
  2.7 7.5 %all-to-all-start = ((f32[16,22,4,128]{3,2,1,0:T(4,128)}), f32[16,22,4,128]{3,2,1,0:T(4,128)S(1)}, u32[]{:S(2)}, u32[]{:S(2)}) async-start(f32[16,22,4,128]{3,2,1,0:T(4,128)} %shard_map.79), calls=%async_computation | async-start | bytes 1441792 | tf_op jit(solution)/shard_map/all_to_all | solution.py:613
  10.2 0.0 copy-done.3
  10.2 0.6 fusion.19
  13.4 0.0 copy-done.4
  13.4 0.1 reshape.177
  13.5 0.1 slice_bitcast_fusion
  13.6 0.0 copy-done.2
  13.7 0.1 concatenate.13
  13.8 0.4 fusion.2
  14.2 0.4 fusion
  14.7 0.1 stack.32.scales
  14.8 0.1 pad_maximum_fusion.mix_ref
  14.9 0.0 copy-done
  15.0 0.0 copy-done.1
  15.0 0.6 shard_map.77
  15.6 1.7 %collective-permute-start = (f32[84,128]{1,0:T(8,128)S(1)}, f32[84,128]{1,0:T(8,128)S(1)}, u32[]{:S(2)}, u32[]{:S(2)}) collective-permute-start(f32[84,128]{1,0:T(8,128)S(1)} %get-tuple-element.18), channel_id=1, source_target_pairs={{0,1},{1,2},{2,3},{3,0},{4,5},{5,6},{6,7},{7,4},{8,9},{9,10},{10,1... | collective-permute-start | bytes 129032 | tf_op jit(solution)/shard_map/ppermute | solution.py:636
  17.3 0.0 collective-permute-start.1
  17.3 0.5 collective-permute-start.2
  17.8 0.1 convert_reduce_fusion
  18.0 0.6 collective-permute-done.refs_1_
  18.6 2.6 %collective-permute-done.1.refs_2_ = f32[84,128]{1,0:T(8,128)S(1)} collective-permute-done((f32[84,128]{1,0:T(8,128)S(1)}, f32[84,128]{1,0:T(8,128)S(1)}, u32[]{:S(2)}, u32[]{:S(2)}) %collective-permute-start.1) | collective-permute-done | bytes 43040 | tf_op jit(solution)/shard_map/ppermute | solution.py:636
  21.2 0.2 collective-permute-done.2.refs_3_
  21.4 0.8 shard_map.78
  22.2 5.4 %all-to-all-done = f32[16,22,4,128]{3,2,1,0:T(4,128)S(1)} async-done(((f32[16,22,4,128]{3,2,1,0:T(4,128)}), f32[16,22,4,128]{3,2,1,0:T(4,128)S(1)}, u32[]{:S(2)}, u32[]{:S(2)}) %all-to-all-start) | async-done | bytes 720928 | tf_op jit(solution)/shard_map/all_to_all | solution.py:613
  27.6 0.1 mul.69.weight_ref
  27.7 1.0 %shard_map.80 = (f32[8,2,88,128]{3,2,1,0:T(8,128)S(1)}, f32[1056,128]{1,0:T(8,128)}, f32[1056,128]{1,0:T(8,128)S(1)}) custom-call(s32[1]{0:T(128)} %bitcast.9.odd, f32[7,8,640]{2,1,0:T(8,128)S(1)} %get-tuple-element.21.a_ref, f32[88,128]{1,0:T(8,128)S(1)} %mul.69.weight_ref, f32[1408,128]{1,0:T(8,128)S(1)} %bitcast.64), custom_call_target="tpu_custom_call" | custom-call | bytes 2711552 | tf_op jit(solution)/shard_map/pallas_call | solution.py:532
  28.7 3.0 %collective-permute-start.3 = (f32[1056,128]{1,0:T(8,128)}, f32[1056,128]{1,0:T(8,128)S(1)}, u32[]{:S(2)}, u32[]{:S(2)}) collective-permute-start(f32[1056,128]{1,0:T(8,128)} %get-tuple-element.28), channel_id=1, source_target_pairs={{1,2},{3,7},{6,5},{4,8},{9,10},{11,15},{14,13},{2,1},{7,3},{5,6},{... | collective-permute-start | bytes 1622024 | tf_op jit(solution)/shard_map/ppermute | solution.py:658
  31.6 0.1 collective-permute-start.4
  31.7 0.1 add_convert_fusion.inside
  31.8 2.3 %shard_map.81 = (f32[8,2,88,128]{3,2,1,0:T(8,128)S(1)}, f32[8,2,88,128]{3,2,1,0:T(8,128)S(1)}) custom-call(f32[5]{0:T(128)S(1)} %stack.32.scales, bf16[528,192]{1,0:T(8,128)(2,1)S(1)} %pad_maximum_fusion.mix_ref, f32[7,8,640]{2,1,0:T(8,128)S(1)} %get-tuple-element.21.a_ref, f32[7,8,256]{2,1,0:T(8,128)S(1)} %get-tuple-element.25.b_ref, ...), custom_call_target="tpu_custom_call" | custom-call | flops 3000000000 | bytes 2768896 | tf_op jit(solution)/shard_map/pallas_call | solution.py:532
  34.1 5.5 %collective-permute-done.3.chip_ref = f32[1056,128]{1,0:T(8,128)S(1)} collective-permute-done((f32[1056,128]{1,0:T(8,128)}, f32[1056,128]{1,0:T(8,128)S(1)}, u32[]{:S(2)}, u32[]{:S(2)}) %collective-permute-start.3) | collective-permute-done | bytes 540704 | tf_op jit(solution)/shard_map/ppermute | solution.py:658
  39.6 0.0 collective-permute-done.4.core_ref
  39.6 0.1 mul.67.unweight_ref
  39.6 12.0 %shard_map.82 = f32[2816,128]{1,0:T(8,128)S(1)} custom-call(f32[5]{0:T(128)S(1)} %stack.32.scales, f32[2]{0:T(128)S(1)} %add_convert_fusion.inside, s32[1]{0:T(128)} %bitcast.9.odd, bf16[528,192]{1,0:T(8,128)(2,1)S(1)} %pad_maximum_fusion.mix_ref, f32[7,8,640]{2,1,0:T(8,128)S(1)} %get-tuple-element.21.a_ref, f32[7,8,512]{2,1,0:T(8,128)S(1)} %get-tuple-element.22.b_ref, ...), custom_call_target="tpu_custom_call" | custom-call | flops 10000000000 | bytes 5451776 | tf_op jit(solution)/shard_map/pallas_call | solution.py:532
  51.6 39.5 %all_to_all.10.in_ref = f32[16,2,22,4,128]{4,3,2,1,0:T(4,128)S(1)} all-to-all(f32[16,2,22,4,128]{4,3,2,1,0:T(4,128)S(1)} %bitcast.65), channel_id=1, replica_groups=mesh['groups'=2,'chaos'=4,'space'=4] {'chaos','space'}, dimensions={0} | all-to-all | bytes 2883584 | tf_op jit(solution)/shard_map/all_to_all | solution.py:689
  91.1 1.4 %shard_map.83 = (f32[22,16,4,128]{3,2,1,0:T(4,128)}, f32[22,16,4,128]{3,2,1,0:T(4,128)}) custom-call(f32[16,2,22,4,128]{4,3,2,1,0:T(4,128)S(1)} %all_to_all.10.in_ref), custom_call_target="tpu_custom_call" | custom-call | bytes 2883584 | tf_op jit(solution)/shard_map/pallas_call | solution.py:532
  (10 shorter events, 0.1 us)
Async XLA Ops:
  0.6 9.6 %copy-start.3 = (f32[2]{0:T(128)S(1)}, f32[2]{0:T(128)}, u32[]{:S(2)}) copy-start(f32[2]{0:T(128)} %param.11) | copy-start | bytes 28
  0.6 12.7 %copy-start.4 = (s32[88]{0:T(128)S(1)}, s32[88]{0:T(128)}, u32[]{:S(2)}) copy-start(s32[88]{0:T(128)} %param.10) | copy-start | bytes 1060
  0.7 13.0 %copy-start.2 = (s32[6,28,3]{1,2,0:T(4,128)S(1)}, s32[6,28,3]{1,2,0:T(4,128)}, u32[]{:S(2)}) copy-start(s32[6,28,3]{1,2,0:T(4,128)} %param.9) | copy-start | bytes 6052
  2.7 12.2 %copy-start = (f32[6,2,4096]{2,1,0:T(2,128)S(1)}, f32[6,2,4096]{2,1,0:T(2,128)}, u32[]{:S(2)}) copy-start(f32[6,2,4096]{2,1,0:T(2,128)} %param.8) | copy-start | bytes 589828
  2.7 12.2 %copy-start.1 = (f32[2,4096]{1,0:T(2,128)S(1)}, f32[2,4096]{1,0:T(2,128)}, u32[]{:S(2)}) copy-start(f32[2,4096]{1,0:T(2,128)} %param.7) | copy-start | bytes 98308
  2.7 24.9 %all-to-all-start = ((f32[16,22,4,128]{3,2,1,0:T(4,128)}), f32[16,22,4,128]{3,2,1,0:T(4,128)S(1)}, u32[]{:S(2)}, u32[]{:S(2)}) async-start(f32[16,22,4,128]{3,2,1,0:T(4,128)} %shard_map.79), calls=%async_computation | async-start | bytes 1441792 | tf_op jit(solution)/shard_map/all_to_all | solution.py:613
  15.6 3.1 %collective-permute-start = (f32[84,128]{1,0:T(8,128)S(1)}, f32[84,128]{1,0:T(8,128)S(1)}, u32[]{:S(2)}, u32[]{:S(2)}) collective-permute-start(f32[84,128]{1,0:T(8,128)S(1)} %get-tuple-element.18), channel_id=1, source_target_pairs={{0,1},{1,2},{2,3},{3,0},{4,5},{5,6},{6,7},{7,4},{8,9},{9,10},{10,1... | collective-permute-start | bytes 129032 | tf_op jit(solution)/shard_map/ppermute | solution.py:636
  17.3 3.9 %collective-permute-start.1 = (f32[84,128]{1,0:T(8,128)S(1)}, f32[84,128]{1,0:T(8,128)S(1)}, u32[]{:S(2)}, u32[]{:S(2)}) collective-permute-start(f32[84,128]{1,0:T(8,128)S(1)} %get-tuple-element.19), channel_id=1, source_target_pairs={{0,2},{1,3},{2,0},{3,1},{4,6},{5,7},{6,4},{7,5},{8,10},{9,11},{10,... | collective-permute-start | bytes 129032 | tf_op jit(solution)/shard_map/ppermute | solution.py:636
  17.3 4.2 %collective-permute-start.2 = (f32[84,128]{1,0:T(8,128)S(1)}, f32[84,128]{1,0:T(8,128)S(1)}, u32[]{:S(2)}, u32[]{:S(2)}) collective-permute-start(f32[84,128]{1,0:T(8,128)S(1)} %get-tuple-element.20), channel_id=1, source_target_pairs={{0,3},{1,0},{2,1},{3,2},{4,7},{5,4},{6,5},{7,6},{8,11},{9,8},{10,9... | collective-permute-start | bytes 129032 | tf_op jit(solution)/shard_map/ppermute | solution.py:636
  28.7 10.9 %collective-permute-start.3 = (f32[1056,128]{1,0:T(8,128)}, f32[1056,128]{1,0:T(8,128)S(1)}, u32[]{:S(2)}, u32[]{:S(2)}) collective-permute-start(f32[1056,128]{1,0:T(8,128)} %get-tuple-element.28), channel_id=1, source_target_pairs={{1,2},{3,7},{6,5},{4,8},{9,10},{11,15},{14,13},{2,1},{7,3},{5,6},{... | collective-permute-start | bytes 1622024 | tf_op jit(solution)/shard_map/ppermute | solution.py:658
  31.6 7.9 %collective-permute-start.4 = (f32[1056,128]{1,0:T(8,128)S(1)}, f32[1056,128]{1,0:T(8,128)S(1)}, u32[]{:S(2)}, u32[]{:S(2)}) collective-permute-start(f32[1056,128]{1,0:T(8,128)S(1)} %get-tuple-element.29), channel_id=1, source_target_pairs={{0,1},{2,3},{7,6},{5,4},{8,9},{10,11},{15,14},{13,12},{1,0},{3,2},... | collective-permute-start | bytes 1622024 | tf_op jit(solution)/shard_map/ppermute | solution.py:658

commit v5 on v4

--- a/solution.py
+++ b/solution.py
@@ -174,9 +174,12 @@
         copy.wait()
 
 
-def scatter_kernel(blocks, in_ref, out_ref, held_ref, sems):
+def scatter_kernel(targets, in_ref, terms_ref, *refs):
+    *outs, terms_out_ref, held_ref, sems = refs
     own = in_ref.shape[0]
-    parts = sems.shape[0]
+    parts = sems.shape[0] - 1
+    terms_copy = pltpu.make_async_copy(terms_ref, terms_out_ref, sems.at[parts])
+    terms_copy.start()
     bounds = [own * n // parts for n in range(parts + 1)]
     spans = [pl.ds(a, b - a) for a, b in zip(bounds[:-1], bounds[1:])]
     copies = [
@@ -187,8 +190,9 @@
         copy.start()
     for copy, span in zip(copies, spans):
         copy.wait()
-        for device, block in enumerate(blocks):
-            out_ref[device, span] = held_ref[span, block]
+        for n, out_ref in enumerate(outs):
+            out_ref[span] = held_ref[span, targets[n]]
+    terms_copy.wait()
 
 
 def pick_kernel(targets, scales, mix_ref, mean_ref, modes_ref, *outs):
@@ -257,17 +261,18 @@
         face_ref[k, :, lanes(1)] = pltpu.roll(values[2], NY, 1)
 
 
-def collect_kernel(blocks, in_ref, *rest):
-    *outs, sems = rest
-    run_copies(
-        [
-            pltpu.make_async_copy(
-                in_ref.at[device, n], out_ref.at[:, block], sems.at[n, device]
-            )
-            for n, out_ref in enumerate(outs)
-            for device, block in enumerate(blocks)
-        ]
-    )
+def collect_kernel(targets, *refs):
+    *arrays, first_ref, second_ref, sems = refs
+    half = len(arrays) // 2
+    copies = [
+        pltpu.make_async_copy(in_ref, out_ref.at[:, targets[n]], sems.at[f, n])
+        for f, out_ref in enumerate((first_ref, second_ref))
+        for n, in_ref in enumerate(arrays[f * half : (f + 1) * half])
+    ]
+    for copy in copies:
+        copy.start()
+    for copy in copies:
+        copy.wait()
 
 
 def slot_parts(own, chaos):
@@ -278,12 +283,33 @@
     ]
 
 
-def start_kernel(chaos, spaces, odd, a_ref, weight_ref, in_ref, residual_ref, chip_ref, core_ref):
+def partner_pieces(chaos_of, space_of, shape):
+    layers, tiles, slots, _ = shape
+    chaos, spaces = chaos_of.shape[0], space_of.shape[0]
+    own = slots // chaos
+    whole = own // 8 * 8
+    rest = own - whole
+    thick = layers // spaces
+    pieces = tiles * thick
+    for a in range(chaos):
+        c = chaos_of[a]
+        main = pl.ds(pl.multiple_of(c * whole, 8), whole)
+        tail = pl.ds(chaos * whole + c * rest, rest)
+        for b in range(spaces):
+            first = space_of[b] * thick
+            for t in range(tiles):
+                for z in range(thick):
+                    row = t * thick + z
+                    there = pl.ds(row, whole, stride=pieces)
+                    yield a * spaces + b, there, first + z, t, main
+                    there = pl.ds(whole * pieces + row, rest, stride=pieces)
+                    yield a * spaces + b, there, first + z, t, tail
+
+
+def start_kernel(odd, chaos_of, space_of, a_ref, weight_ref, *refs):
+    *ins, residual_ref, chip_ref, core_ref, raw_ref = refs
     upward = odd[0] > 0
     layers, tiles, slots, _ = residual_ref.shape
-    own = slots // chaos
-    thick = layers // spaces
-    pieces = tiles * thick
     half = layers // 2
     low_half = lane_masks(slots)[0]
     weight = weight_ref[...]
@@ -293,21 +319,11 @@
         chip_ref[rows, :] = jnp.where(upward, up, down)
         core_ref[rows, :] = jnp.where(upward, down, up)
 
+    for n, there, l, t, here in partner_pieces(chaos_of, space_of, residual_ref.shape):
+        raw_ref[l, t, here, :] = ins[n][there, :]
     for l in range(layers):
-        i, z = divmod(l, thick)
         for t in range(tiles):
-            rows = [
-                in_ref[
-                    pl.ds(
-                        ((c * spaces + i) * own + slot) * pieces + t * thick + z,
-                        number,
-                        stride=pieces,
-                    ),
-                    :,
-                ]
-                for c, slot, number, _ in slot_parts(own, chaos)
-            ]
-            residual_ref[l, t] = weight * jnp.concatenate(rows, axis=0)
+            residual_ref[l, t] = weight * raw_ref[l, t]
         put(l, residual_ref[l, 1], residual_ref[l, 0])
     for l in range(half):
         later = l + half
@@ -377,12 +393,98 @@
             edge_ref[l, t] = edge
 
 
-def iterate_kernel(
-    chaos,
-    spaces,
+def run_step(
+    step,
+    scales,
+    inside,
+    mix_ref,
+    a_ref,
+    b_ref,
+    r_ref,
+    d_ref,
+    total_ref,
+    edge_ref,
+    use,
+    face_ref=None,
+    own_total_ref=None,
+    own_edge_ref=None,
+):
+    layers, _, slots, _ = r_ref.shape
+    modes = a_ref.shape[0]
+    masks = lane_masks(slots)
+    low_half = masks[0]
+    mix = mix_ref[...]
+    depth = mix.shape[1]
+    zero = jnp.zeros((slots, LANES), jnp.float32)
+    count = FOLDED - step
+    full = count - 1
+    first = OWN_TILES if step == 0 else 0
+
+    def read(l, t):
+        return d_ref[l, t]
+
+    group = 1
+    for lowest in range(0, layers, group):
+        gathered, stacked = [], []
+        for l in range(lowest, lowest + group):
+            direct = [d_ref[l, t] for t in range(first, count)]
+            around = neighbour_sums(read, l, layers, count, masks, first)
+            extra = []
+            if step == 0:
+                extra = [jnp.where(low_half, d_ref[l, 0], d_ref[l, 1])]
+            gathered.append((l, len(stacked), direct, extra, around))
+            stacked += direct + extra + around
+        mixed = jnp.dot(
+            mix, split_stack(stacked, depth), preferred_element_type=jnp.float32
+        )
+        for l, place, direct, extra, around in gathered:
+            results = weighted_tiles(
+                mixed,
+                modes,
+                place,
+                place + len(direct) + len(extra),
+                direct,
+                around,
+                lambda k, t: a_ref[k, l : l + 1, lanes(first + t)],
+                lambda k, t: b_ref[k, l : l + 1, lanes(first + t)],
+            )
+            for t, (total, edge) in enumerate(results):
+                edge_ref[l, first + t] = edge
+                if first + t < full:
+                    total_ref[l, first + t] = total
+            if not extra:
+                continue
+            own_face = face_ref[0, l : l + 1, lanes(0)]
+            other_face = face_ref[0, l : l + 1, lanes(1)]
+            part = other_face * extra[0] - own_face * pltpu.roll(direct[0], NY, 1)
+            for k in range(1, modes):
+                own_face = face_ref[k, l : l + 1, lanes(0)]
+                other_face = face_ref[k, l : l + 1, lanes(1)]
+                own_mixed = mode_part(mixed, modes, k, place + len(direct))
+                other_mixed = pltpu.roll(mode_part(mixed, modes, k, place), NY, 1)
+                part = part + (other_face * own_mixed - own_face * other_mixed)
+            total_ref[l, 0] = own_total_ref[l, 0] + jnp.where(low_half, part, zero)
+            total_ref[l, 1] = own_total_ref[l, 1] + jnp.where(low_half, zero, part)
+
+    def read_edge(l, t):
+        return own_edge_ref[l, t] if t < first else edge_ref[l, t]
+
+    for l in range(layers):
+        spread = neighbour_sums(read_edge, l, layers, count, masks)
+        for t in range(full):
+            diffused = total_ref[l, t] - spread[t]
+            if t >= OWN_TILES:
+                lower, upper = inside[(t + 1) % 2], inside[t % 2]
+                diffused = diffused * jnp.where(low_half, lower, upper)
+            use(l, t, r_ref[l, t] - diffused)
+
+
+def first_kernel(
     scales,
     inside,
     odd,
+    chaos_of,
+    space_of,
     mix_ref,
     a_ref,
     b_ref,
@@ -393,35 +495,17 @@
     own_edge_ref,
     chip_ref,
     core_ref,
-    sent_ref,
-    r_ref,
-    d_ref,
-    total_ref,
-    edge_ref,
-    x_ref,
+    *refs,
 ):
+    *outs, left_r_ref, left_d_ref, r_ref, d_ref, total_ref, edge_ref, x_ref = refs
     layers, _, slots, _ = start_ref.shape
-    modes = a_ref.shape[0]
-    own = slots // chaos
-    thick = layers // spaces
-    pieces = OWN_TILES * thick
     half = layers // 2
-    masks = lane_masks(slots)
-    low_half = masks[0]
-    mix = mix_ref[...]
-    depth = mix.shape[1]
+    low_half = lane_masks(slots)[0]
     upward = odd[0] > 0
 
     def message(start, size):
         chip, core = chip_ref[pl.ds(start, size), :], core_ref[pl.ds(start, size), :]
         return jnp.where(upward, core, chip), jnp.where(upward, chip, core)
-
-    def send(field, l, t, value):
-        i, z = divmod(l, thick)
-        value = value * unweight_ref[...]
-        for c, slot, number, row in slot_parts(own, chaos):
-            first = (((c * spaces + i) * 2 + field) * own + slot) * pieces + t * thick + z
-            sent_ref[pl.ds(first, number, stride=pieces), :] = value[row : row + number]
 
     for l in range(layers):
         below, above = message(l * slots, slots)
@@ -442,85 +526,59 @@
                 r_ref[l, t] = tile
             d_ref[l, t] = tile * scales[0]
 
-    def read(l, t):
-        return d_ref[l, t]
-
-    zero = jnp.zeros((slots, LANES), jnp.float32)
-    for step in range(ITERS):
-        count = FOLDED - step
-        full = count - 1
-        first = OWN_TILES if step == 0 else 0
-        group = 1 if step == 0 else 2
-        for lowest in range(0, layers, group):
-            gathered, stacked = [], []
-            for l in range(lowest, lowest + group):
-                direct = [d_ref[l, t] for t in range(first, count)]
-                around = neighbour_sums(read, l, layers, count, masks, first)
-                extra = []
-                if step == 0:
-                    extra = [jnp.where(low_half, d_ref[l, 0], d_ref[l, 1])]
-                gathered.append((l, len(stacked), direct, extra, around))
-                stacked += direct + extra + around
-            mixed = jnp.dot(
-                mix, split_stack(stacked, depth), preferred_element_type=jnp.float32
-            )
-            for l, place, direct, extra, around in gathered:
-                results = weighted_tiles(
-                    mixed,
-                    modes,
-                    place,
-                    place + len(direct) + len(extra),
-                    direct,
-                    around,
-                    lambda k, t: a_ref[k, l : l + 1, lanes(first + t)],
-                    lambda k, t: b_ref[k, l : l + 1, lanes(first + t)],
-                )
-                for t, (total, edge) in enumerate(results):
-                    edge_ref[l, first + t] = edge
-                    if first + t < full:
-                        total_ref[l, first + t] = total
-                if not extra:
-                    continue
-                own_face = face_ref[0, l : l + 1, lanes(0)]
-                other_face = face_ref[0, l : l + 1, lanes(1)]
-                part = other_face * extra[0] - own_face * pltpu.roll(direct[0], NY, 1)
-                for k in range(1, modes):
-                    own_face = face_ref[k, l : l + 1, lanes(0)]
-                    other_face = face_ref[k, l : l + 1, lanes(1)]
-                    own_mixed = mode_part(mixed, modes, k, place + len(direct))
-                    other_mixed = pltpu.roll(mode_part(mixed, modes, k, place), NY, 1)
-                    part = part + (other_face * own_mixed - own_face * other_mixed)
-                total_ref[l, 0] = own_total_ref[l, 0] + jnp.where(low_half, part, zero)
-                total_ref[l, 1] = own_total_ref[l, 1] + jnp.where(low_half, zero, part)
-
-        def read_edge(l, t):
-            return own_edge_ref[l, t] if t < first else edge_ref[l, t]
-
-        for l in range(layers):
-            spread = neighbour_sums(read_edge, l, layers, count, masks)
-            for t in range(full):
-                diffused = total_ref[l, t] - spread[t]
-                if t >= OWN_TILES:
-                    lower, upper = inside[(t + 1) % 2], inside[t % 2]
-                    diffused = diffused * jnp.where(low_half, lower, upper)
-                residual = r_ref[l, t] - diffused
-                if step == ITERS - 1:
-                    send(1, l, t, residual)
-                    continue
+    for step in range(ITERS - 1):
+        ready = step == ITERS - 2
+
+        def use(l, t, residual):
+            if not ready:
                 r_ref[l, t] = residual
-                old = d_ref[l, t]
-                direction = scales[1 + 2 * step] * old + scales[2 + 2 * step] * residual
-                d_ref[l, t] = direction
-                if t < OWN_TILES:
-                    value = (old if step == 0 else x_ref[l, t]) + direction
-                    if step == ITERS - 2:
-                        send(0, l, t, value)
-                    else:
-                        x_ref[l, t] = value
+            elif t < OWN_TILES:
+                left_r_ref[l, t] = residual
+            old = d_ref[l, t]
+            direction = scales[1 + 2 * step] * old + scales[2 + 2 * step] * residual
+            (left_d_ref if ready else d_ref)[l, t] = direction
+            if t < OWN_TILES:
+                value = (old if step == 0 else x_ref[l, t]) + direction
+                x_ref[l, t] = value * unweight_ref[...] if ready else value
+
+        run_step(
+            step,
+            scales,
+            inside,
+            mix_ref,
+            a_ref,
+            b_ref,
+            r_ref,
+            d_ref,
+            total_ref,
+            edge_ref,
+            use,
+            face_ref,
+            own_total_ref,
+            own_edge_ref,
+        )
+    for n, there, l, t, here in partner_pieces(chaos_of, space_of, start_ref.shape):
+        outs[n][there, :] = x_ref[l, t, here, :]
+
+
+def last_kernel(
+    scales, inside, chaos_of, space_of, mix_ref, a_ref, b_ref, unweight_ref, r_ref, d_ref, *refs
+):
+    *outs, total_ref, edge_ref, left_ref = refs
+
+    def use(l, t, residual):
+        left_ref[l, t] = residual * unweight_ref[...]
+
+    run_step(
+        ITERS - 1, scales, inside, mix_ref, a_ref, b_ref, r_ref, d_ref, total_ref, edge_ref, use
+    )
+    for n, there, l, t, here in partner_pieces(chaos_of, space_of, r_ref.shape):
+        outs[n][there, :] = left_ref[l, t, here, :]
 
 
 def call(kernel, outs, scalars, arrays, scratch=(), flops=0, in_kinds=None, out_kind=pltpu.VMEM):
     kinds = in_kinds or [pltpu.VMEM] * len(arrays)
+    out_kinds = out_kind if isinstance(out_kind, list) else [out_kind] * len(outs)
     in_specs = [pl.BlockSpec(memory_space=pltpu.SMEM)] * len(scalars) + [
         pl.BlockSpec(memory_space=kind) for kind in kinds
     ]
@@ -533,9 +591,9 @@
         kernel,
         out_shape=outs,
         in_specs=in_specs,
-        out_specs=[pl.BlockSpec(memory_space=out_kind)] * len(outs),
+        out_specs=[pl.BlockSpec(memory_space=kind) for kind in out_kinds],
         scratch_shapes=scratch,
-        compiler_params=pltpu.CompilerParams(vmem_limit_bytes=40 * 1024 * 1024),
+        compiler_params=pltpu.CompilerParams(vmem_limit_bytes=24 * 1024 * 1024),
         cost_estimate=pl.CostEstimate(flops=flops, bytes_accessed=moved, transcendentals=0),
     )(*scalars, *arrays)
 
@@ -586,7 +644,6 @@
     def shape(*sizes):
         return jax.ShapeDtypeStruct(sizes, f32)
 
-    mix, weight, unweight = coupling_tables(coupling, slot_term, chaos)
     midpoint = 0.5 * (bounds[1] + bounds[0])
     half_span = 0.5 * (bounds[1] - bounds[0])
     sigma_one = midpoint / half_span
@@ -602,22 +659,47 @@
         tiled = field.reshape(*field.shape[:-2], thick, columns, LANES)
         return jnp.swapaxes(tiled, -3, -2)
 
-    scattered = call(
-        functools.partial(scatter_kernel, blocks),
-        [shape(devices, own, pieces, LANES)],
-        [],
-        [by_columns(source_chaos_terms).reshape(own, devices, pieces, LANES)],
-        [pltpu.VMEM((own, devices, pieces, LANES), f32), pltpu.SemaphoreType.DMA((2,))],
-        in_kinds=[pltpu.HBM],
-    )[0]
-    gathered = lax.all_to_all(scattered, BOTH, 0, 0, tiled=True).reshape(-1, LANES)
-
     row, column = lax.axis_index("chaos"), lax.axis_index("space")
 
-    def block_at(space):
-        return row * spaces + jnp.where(row % 2 == 0, space, spaces - 1 - space)
-
-    block = block_at(column)
+    def block_at(chaos_index, space):
+        return chaos_index * spaces + jnp.where(chaos_index % 2 == 0, space, spaces - 1 - space)
+
+    chaos_of = jnp.bitwise_xor(row, jnp.arange(chaos, dtype=jnp.int32))
+    space_of = jnp.bitwise_xor(column, jnp.arange(spaces, dtype=jnp.int32))
+    targets = block_at(chaos_of[:, None], space_of[None, :]).reshape(-1)
+
+    far = [(a, b) for b in range(spaces) for a in range(chaos // 2, chaos)]
+    near = [(a, b) for b in range(spaces) for a in range(chaos // 2) if a + b > 0]
+    order = []
+    while far or near:
+        order += far[:2] + near[:2 if len(near) > len(far) else 1]
+        far, near = far[2:], near[2 if len(near) > len(far) else 1 :]
+
+    def swap_all(fields):
+        received = list(fields)
+        for a, b in order:
+            pairs = [
+                (c * spaces + i, (c ^ a) * spaces + (i ^ b))
+                for c in range(chaos)
+                for i in range(spaces)
+            ]
+            received[a * spaces + b] = lax.ppermute(fields[a * spaces + b], BOTH, pairs)
+        return received
+
+    piece = shape(own, pieces, LANES)
+    *scattered, slot_term = call(
+        scatter_kernel,
+        [piece] * devices + [jax.ShapeDtypeStruct(slot_term.shape, slot_term.dtype)],
+        [targets],
+        [by_columns(source_chaos_terms).reshape(own, devices, pieces, LANES), slot_term],
+        [pltpu.VMEM((own, devices, pieces, LANES), f32), pltpu.SemaphoreType.DMA((3,))],
+        in_kinds=[pltpu.HBM] * 2,
+        out_kind=[pltpu.VMEM] * devices + [pltpu.HBM],
+    )
+    gathered = [field.reshape(-1, LANES) for field in swap_all(scattered)]
+    mix, weight, unweight = coupling_tables(coupling, slot_term, chaos)
+
+    block = block_at(row, column)
     inside = jnp.stack([block > 0, block < devices - 1]).astype(f32)
     odd = (block % 2)[None]
     modes = mode_shapes.shape[0] + 1
@@ -625,7 +707,7 @@
     picked = call(
         pick_kernel,
         [shape(modes * 3 * pieces, LANES)] * spaces,
-        [block_at((column + steps) % spaces), scales],
+        [block_at(row, (column + steps) % spaces), scales],
         [
             mix,
             by_columns(mean_conductivity).reshape(-1, LANES),
@@ -646,10 +728,11 @@
 
     message = shape((layers + layers // 2) * slots, LANES)
     start, to_chip, to_core = call(
-        functools.partial(start_kernel, chaos, spaces),
+        start_kernel,
         [shape(layers, OWN_TILES, slots, LANES), message, message],
-        [odd],
-        [a, weight, gathered],
+        [odd, chaos_of, space_of],
+        [a, weight, *gathered],
+        [pltpu.VMEM((layers, OWN_TILES, slots, LANES), f32)],
     )
     place = {n: device for device, n in enumerate(blocks)}
 
@@ -671,29 +754,33 @@
     def held(tiles):
         return pltpu.VMEM((layers, tiles, slots, LANES), f32)
 
+    flat = shape(own * pieces, LANES)
+    *sent, residual, direction = call(
+        first_kernel,
+        [flat] * devices
+        + [shape(layers, OWN_TILES, slots, LANES), shape(layers, OWN_TILES + 1, slots, LANES)],
+        [scales, inside, odd, chaos_of, space_of],
+        [mix, a, b, face, unweight, start, own_total, own_edge, from_chip, from_core],
+        [held(FOLDED - 1), held(FOLDED), held(FOLDED - 1), held(FOLDED), held(OWN_TILES)],
+        flops=8000000000,
+    )
+    received = swap_all([field.reshape(own, pieces, LANES) for field in sent])
     sent = call(
-        functools.partial(iterate_kernel, chaos, spaces),
-        [shape(devices * 2 * own * pieces, LANES)],
-        [scales, inside, odd],
-        [mix, a, b, face, unweight, start, own_total, own_edge, from_chip, from_core],
-        [
-            held(FOLDED - 1),
-            held(FOLDED),
-            held(FOLDED - 1),
-            held(FOLDED),
-            held(OWN_TILES),
-        ],
-        flops=10000000000,
-    )[0]
-    sent = sent.reshape(devices, 2, own, pieces, LANES)
-    received = lax.all_to_all(sent, BOTH, 0, 0, tiled=True)
+        last_kernel,
+        [flat] * devices,
+        [scales, inside, chaos_of, space_of],
+        [mix, a, b, unweight, residual, direction],
+        [held(OWN_TILES), held(OWN_TILES + 1), held(OWN_TILES)],
+        flops=3000000000,
+    )
+    received += swap_all([field.reshape(own, pieces, LANES) for field in sent])
     outs = call(
-        functools.partial(collect_kernel, blocks),
+        collect_kernel,
         [shape(own, devices, pieces, LANES)] * 2,
-        [],
-        [received],
+        [targets],
+        received,
         [pltpu.SemaphoreType.DMA((2, devices))],
-        in_kinds=[pl.ANY],
+        in_kinds=[pl.ANY] * len(received),
         out_kind=pltpu.HBM,
     )
     return tuple(
@@ -711,7 +798,8 @@
         thick * spaces == 8
         and cells == chaos * spaces * OWN_TILES * LANES
         and (own * chaos) % 8 == 0
-        and spaces % 2 == 0
+        and chaos & (chaos - 1) == 0
+        and spaces & (spaces - 1) == 0
     )
     plan = local_by_cells if fits else local_by_slots
     return plan(

time: 92.9 us -> 117 us (1.26)
  starting transfers between devices: 12.7 us -> 71.3 us
  blocking collectives: 39.5 us -> 0 us
  Pallas kernels: 20 us -> 21.9 us
  local copies, waits for them, and re-layouts: 1.12 us -> 2.77 us
    ppermute x0 -> x45, starting transfers between devices: none -> 66.9 us  [swap_all(): received[a * spaces + b] = lax.ppermute(fields[a * spaces + b], BOTH, pairs)]
    all_to_all x1 -> x0, blocking collectives: 39.5 us -> none  [local_by_cells(): received = lax.all_to_all(sent, BOTH, 0, 0, tiled=True)]
    ppermute x0 -> x45, waiting for transfers between devices: none -> 8.18 us  [swap_all(): received[a * spaces + b] = lax.ppermute(fields[a * spaces + b], BOTH, pairs)]
    all_to_all x1 -> x0, starting transfers between devices: 7.47 us -> none  [local_by_cells(): lax.all_to_all(scattered, BOTH, 0, 0, tiled=True).reshape(-1, LANES)]
    all_to_all x1 -> x0, waiting for transfers between devices: 5.42 us -> none  [local_by_cells(): lax.all_to_all(scattered, BOTH, 0, 0, tiled=True).reshape(-1, LANES)]
    ppermute x3, waiting for transfers between devices: 3.42 us -> 0.5 us  [local_by_cells(): lax.ppermute(picked[n], 'space', [(i, (i + n) % spaces) for i in range(sp...]
    pallas_call x7 -> x8, Pallas kernels: 20 us -> 21.9 us  [call(): pl.pallas_call(kernel, out_shape=outs, in_specs=in_specs, out_specs=[pl.B...]
  transfers between devices with their start and end apart: 6 -> 50, of which waited for: 5 -> 6; matrix products, arithmetic and copies ran while one was open for 2% -> 3% of each run, Pallas kernels for 4% -> 6%
where the time goes in v5:
time: 117 us; the launch traced here: 116 us
  starting transfers between devices  71.3 us (61%)
  Pallas kernels  21.9 us (19%)
  waiting for transfers between devices  14.5 us (12%)
  between operations  3.99 us (3%)
  local copies, waits for them, and re-layouts  2.77 us (2%)
    ppermute x45, starting transfers between devices, swap_all(): received[a * spaces + b] = lax.ppermute(fields[a * spaces + b], BOTH, pairs)  66.9 us
    pallas_call x8, Pallas kernels, call(): pl.pallas_call(kernel, out_shape=outs, in_specs=in_specs, out_specs=[pl.B...  21.9 us
    ppermute x45, waiting for transfers between devices, swap_all(): received[a * spaces + b] = lax.ppermute(fields[a * spaces + b], BOTH, pairs)  8.18 us
    ppermute x2, waiting for transfers between devices, swap(): return lax.ppermute(field, BOTH, pairs + [(b, a) for a, b in pairs])  5.77 us
    ppermute x2, starting transfers between devices, swap(): return lax.ppermute(field, BOTH, pairs + [(b, a) for a, b in pairs])  2.71 us
  transfers between devices with their start and end apart: 50, of which 6 were waited for; matrix products, arithmetic and copies ran while one was open for 3% of the time, Pallas kernels for 6%

profile of v5, /device:TPU:1, one launch (start us, length us, event | category | flops | bytes accessed | tf_op | source)
XLA Modules:
  0.0 115.9 jit_solution(15439813026850034306)
XLA Ops:
  0.8 0.1 add.66.targets
  0.9 1.8 %shard_map.77 = (f32[22,4,128]{2,1,0:T(4,128)S(1)}, f32[22,4,128]{2,1,0:T(4,128)S(1)}, f32[22,4,128]{2,1,0:T(4,128)S(1)}, f32[22,4,128]{2,1,0:T(4,128)S(1)}, f32...) custom-call(s32[16]{0:T(128)S(1)} %add.66.targets, ...), custom_call_target="tpu_custom_call" | custom-call | bytes 1442496 | tf_op jit(solution)/shard_map/pallas_call | solution.py:590
  2.6 0.1 collective-permute-start.3
  2.8 2.7 %collective-permute-start.4 = (f32[22,4,128]{2,1,0:T(4,128)S(1)}, f32[22,4,128]{2,1,0:T(4,128)S(1)}, u32[]{:S(2)}, u32[]{:S(2)}) collective-permute-start(f32[22,4,128]{2,1,0:T(4,128)S(1)} %get-tuple-element.78), channel_id=1, source_target_pairs={{0,2},{1,3},{2,0},{3,1},{4,6},{5,7},{6,4},{7,5},{8,10},{9,11},{10,... | collective-permute-start | bytes 135176 | tf_op jit(solution)/shard_map/ppermute | solution.py:686
  5.4 1.3 %fusion.21 = (f32[1]{0:T(128)}, f32[1]{0:T(128)}) fusion(f32[2]{0:T(128)} %param.11), kind=kLoop, calls=%fused_computation.56 | loop fusion | bytes 16 | tf_op jit(solution)/shard_map/slice | solution.py:647
  9.8 0.8 fusion.20
  10.7 0.4 fusion.2
  11.2 0.4 fusion
  11.7 0.1 pad_maximum_fusion.mix_ref
  11.8 0.1 stack.32.scales
  11.9 0.6 shard_map.78
  12.6 1.7 %collective-permute-start.1 = (f32[84,128]{1,0:T(8,128)S(1)}, f32[84,128]{1,0:T(8,128)S(1)}, u32[]{:S(2)}, u32[]{:S(2)}) collective-permute-start(f32[84,128]{1,0:T(8,128)S(1)} %get-tuple-element.71), channel_id=1, source_target_pairs={{0,2},{1,3},{2,0},{3,1},{4,6},{5,7},{6,4},{7,5},{8,10},{9,11},{10,... | collective-permute-start | bytes 129032 | tf_op jit(solution)/shard_map/ppermute | solution.py:718
  14.3 0.1 convert_reduce_fusion
  14.4 1.8 %collective-permute-start.5 = (f32[22,4,128]{2,1,0:T(4,128)S(1)}, f32[22,4,128]{2,1,0:T(4,128)S(1)}, u32[]{:S(2)}, u32[]{:S(2)}) collective-permute-start(f32[22,4,128]{2,1,0:T(4,128)S(1)} %get-tuple-element.79), channel_id=1, source_target_pairs={{0,3},{1,2},{2,1},{3,0},{4,7},{5,6},{6,5},{7,4},{8,11},{9,10},{10,... | collective-permute-start | bytes 135176 | tf_op jit(solution)/shard_map/ppermute | solution.py:686
  16.3 0.5 collective-permute-done.1.refs_2_
  16.8 1.3 %collective-permute-start.6 = (f32[22,4,128]{2,1,0:T(4,128)S(1)}, f32[22,4,128]{2,1,0:T(4,128)S(1)}, u32[]{:S(2)}, u32[]{:S(2)}) collective-permute-start(f32[22,4,128]{2,1,0:T(4,128)S(1)} %get-tuple-element.80), channel_id=1, source_target_pairs={{0,4},{1,5},{2,6},{3,7},{4,0},{5,1},{6,2},{7,3},{8,12},{9,13},{10,... | collective-permute-start | bytes 135176 | tf_op jit(solution)/shard_map/ppermute | solution.py:686
  18.1 0.9 collective-permute-start.7
  19.0 1.2 %collective-permute-start.8 = (f32[22,4,128]{2,1,0:T(4,128)S(1)}, f32[22,4,128]{2,1,0:T(4,128)S(1)}, u32[]{:S(2)}, u32[]{:S(2)}) collective-permute-start(f32[22,4,128]{2,1,0:T(4,128)S(1)} %get-tuple-element.82), channel_id=1, source_target_pairs={{0,6},{1,7},{2,4},{3,5},{4,2},{5,3},{6,0},{7,1},{8,14},{9,15},{10,... | collective-permute-start | bytes 135176 | tf_op jit(solution)/shard_map/ppermute | solution.py:686
  20.2 1.8 %collective-permute-start.9 = (f32[22,4,128]{2,1,0:T(4,128)S(1)}, f32[22,4,128]{2,1,0:T(4,128)S(1)}, u32[]{:S(2)}, u32[]{:S(2)}) collective-permute-start(f32[22,4,128]{2,1,0:T(4,128)S(1)} %get-tuple-element.83), channel_id=1, source_target_pairs={{0,7},{1,6},{2,5},{3,4},{4,3},{5,2},{6,1},{7,0},{8,15},{9,14},{10,... | collective-permute-start | bytes 135176 | tf_op jit(solution)/shard_map/ppermute | solution.py:686
  22.1 2.3 %collective-permute-start.10 = (f32[22,4,128]{2,1,0:T(4,128)S(1)}, f32[22,4,128]{2,1,0:T(4,128)S(1)}, u32[]{:S(2)}, u32[]{:S(2)}) collective-permute-start(f32[22,4,128]{2,1,0:T(4,128)S(1)} %get-tuple-element.84), channel_id=1, source_target_pairs={{0,8},{1,9},{2,10},{3,11},{4,12},{5,13},{6,14},{7,15},{8,0},{9,1},... | collective-permute-start | bytes 135176 | tf_op jit(solution)/shard_map/ppermute | solution.py:686
  24.4 2.2 %collective-permute-start.12 = (f32[22,4,128]{2,1,0:T(4,128)S(1)}, f32[22,4,128]{2,1,0:T(4,128)S(1)}, u32[]{:S(2)}, u32[]{:S(2)}) collective-permute-start(f32[22,4,128]{2,1,0:T(4,128)S(1)} %get-tuple-element.86), channel_id=1, source_target_pairs={{0,10},{1,11},{2,8},{3,9},{4,14},{5,15},{6,12},{7,13},{8,2},{9,3},... | collective-permute-start | bytes 135176 | tf_op jit(solution)/shard_map/ppermute | solution.py:686
  26.6 1.7 %collective-permute-start.13 = (f32[22,4,128]{2,1,0:T(4,128)S(1)}, f32[22,4,128]{2,1,0:T(4,128)S(1)}, u32[]{:S(2)}, u32[]{:S(2)}) collective-permute-start(f32[22,4,128]{2,1,0:T(4,128)S(1)} %get-tuple-element.87), channel_id=1, source_target_pairs={{0,11},{1,10},{2,9},{3,8},{4,15},{5,14},{6,13},{7,12},{8,3},{9,2},... | collective-permute-start | bytes 135176 | tf_op jit(solution)/shard_map/ppermute | solution.py:686
  28.3 2.5 %collective-permute-start.14 = (f32[22,4,128]{2,1,0:T(4,128)S(1)}, f32[22,4,128]{2,1,0:T(4,128)S(1)}, u32[]{:S(2)}, u32[]{:S(2)}) collective-permute-start(f32[22,4,128]{2,1,0:T(4,128)S(1)} %get-tuple-element.88), channel_id=1, source_target_pairs={{0,12},{1,13},{2,14},{3,15},{4,8},{5,9},{6,10},{7,11},{8,4},{9,5},... | collective-permute-start | bytes 135176 | tf_op jit(solution)/shard_map/ppermute | solution.py:686
  30.8 2.3 %collective-permute-start.15 = (f32[22,4,128]{2,1,0:T(4,128)S(1)}, f32[22,4,128]{2,1,0:T(4,128)S(1)}, u32[]{:S(2)}, u32[]{:S(2)}) collective-permute-start(f32[22,4,128]{2,1,0:T(4,128)S(1)} %get-tuple-element.89), channel_id=1, source_target_pairs={{0,13},{1,12},{2,15},{3,14},{4,9},{5,8},{6,11},{7,10},{8,5},{9,4},... | collective-permute-start | bytes 135176 | tf_op jit(solution)/shard_map/ppermute | solution.py:686
  33.0 1.6 %collective-permute-start.16 = (f32[22,4,128]{2,1,0:T(4,128)S(1)}, f32[22,4,128]{2,1,0:T(4,128)S(1)}, u32[]{:S(2)}, u32[]{:S(2)}) collective-permute-start(f32[22,4,128]{2,1,0:T(4,128)S(1)} %get-tuple-element.90), channel_id=1, source_target_pairs={{0,14},{1,15},{2,12},{3,13},{4,10},{5,11},{6,8},{7,9},{8,6},{9,7},... | collective-permute-start | bytes 135176 | tf_op jit(solution)/shard_map/ppermute | solution.py:686
  34.7 2.7 %collective-permute-start.17 = (f32[22,4,128]{2,1,0:T(4,128)S(1)}, f32[22,4,128]{2,1,0:T(4,128)S(1)}, u32[]{:S(2)}, u32[]{:S(2)}) collective-permute-start(f32[22,4,128]{2,1,0:T(4,128)S(1)} %get-tuple-element.91), channel_id=1, source_target_pairs={{0,15},{1,14},{2,13},{3,12},{4,11},{5,10},{6,9},{7,8},{8,7},{9,6},... | collective-permute-start | bytes 135176 | tf_op jit(solution)/shard_map/ppermute | solution.py:686
  37.3 0.8 shard_map.79
  38.1 0.5 collective-permute-done.16
  38.6 2.8 %collective-permute-done.17 = f32[22,4,128]{2,1,0:T(4,128)S(1)} collective-permute-done((f32[22,4,128]{2,1,0:T(4,128)S(1)}, f32[22,4,128]{2,1,0:T(4,128)S(1)}, u32[]{:S(2)}, u32[]{:S(2)}) %collective-permute-start.17) | collective-permute-done | bytes 45088 | tf_op jit(solution)/shard_map/ppermute | solution.py:686
  41.6 1.6 %shard_map.80 = (f32[8,2,88,128]{3,2,1,0:T(8,128)S(1)}, f32[1056,128]{1,0:T(8,128)}, f32[1056,128]{1,0:T(8,128)S(1)}) custom-call(s32[1]{0:T(128)} %bitcast.9.odd, s32[4]{0:T(128)S(1)} %iota_xor_fusion.1.chaos_of, s32[4]{0:T(128)S(1)} %get-tuple-element.150.space_of, f32[7,8,640]{2,1,0:T(8,128)S(1)} %get-tuple-element.73.a_ref, ...), custom_call_target="tpu_custom_call" | custom-call | bytes 2711552 | tf_op jit(solution)/shard_map/pallas_call | solution.py:590
  43.2 2.6 %collective-permute-start.18 = (f32[1056,128]{1,0:T(8,128)}, f32[1056,128]{1,0:T(8,128)S(1)}, u32[]{:S(2)}, u32[]{:S(2)}) collective-permute-start(f32[1056,128]{1,0:T(8,128)} %get-tuple-element.96), channel_id=1, source_target_pairs={{1,2},{3,7},{6,5},{4,8},{9,10},{11,15},{14,13},{2,1},{7,3},{5,6},{... | collective-permute-start | bytes 1622024 | tf_op jit(solution)/shard_map/ppermute | solution.py:741
  46.0 2.3 %shard_map.81 = (f32[8,2,88,128]{3,2,1,0:T(8,128)S(1)}, f32[8,2,88,128]{3,2,1,0:T(8,128)S(1)}) custom-call(f32[5]{0:T(128)S(1)} %stack.32.scales, bf16[528,192]{1,0:T(8,128)(2,1)S(1)} %pad_maximum_fusion.mix_ref, f32[7,8,640]{2,1,0:T(8,128)S(1)} %get-tuple-element.73.a_ref, f32[7,8,256]{2,1,0:T(8,128)S(1)} %get-tuple-element.93.b_ref, ...), custom_call_target="tpu_custom_call" | custom-call | flops 3000000000 | bytes 2768896 | tf_op jit(solution)/shard_map/pallas_call | solution.py:590
  48.3 5.8 %collective-permute-done.18.chip_ref = f32[1056,128]{1,0:T(8,128)S(1)} collective-permute-done((f32[1056,128]{1,0:T(8,128)}, f32[1056,128]{1,0:T(8,128)S(1)}, u32[]{:S(2)}, u32[]{:S(2)}) %collective-permute-start.18) | collective-permute-done | bytes 540704 | tf_op jit(solution)/shard_map/ppermute | solution.py:741
  54.1 9.3 %shard_map.82 = (f32[88,128]{1,0:T(8,128)S(1)}, f32[88,128]{1,0:T(8,128)S(1)}, f32[88,128]{1,0:T(8,128)S(1)}, f32[88,128]{1,0:T(8,128)S(1)}, f32[88,128]{1,0:T(8...) custom-call(f32[5]{0:T(128)S(1)} %stack.32.scales, ...), custom_call_target="tpu_custom_call" | custom-call | flops 8000000000 | bytes 6533120 | tf_op jit(solution)/shard_map/pallas_call | solution.py:590
  63.6 0.7 collective-permute-start.21
  64.3 1.4 %collective-permute-start.22 = (f32[22,4,128]{2,1,0:T(4,128)S(1)}, f32[22,4,128]{2,1,0:T(4,128)S(1)}, u32[]{:S(2)}, u32[]{:S(2)}) collective-permute-start(f32[22,4,128]{2,1,0:T(4,128)S(1)} %bitcast.157), channel_id=1, source_target_pairs={{0,3},{1,2},{2,1},{3,0},{4,7},{5,6},{6,5},{7,4},{8,11},{9,10},{10,... | collective-permute-start | bytes 135176 | tf_op jit(solution)/shard_map/ppermute | solution.py:686
  65.7 1.0 collective-permute-start.23
  66.7 0.5 collective-permute-start.24
  67.1 1.5 %collective-permute-start.25 = (f32[22,4,128]{2,1,0:T(4,128)S(1)}, f32[22,4,128]{2,1,0:T(4,128)S(1)}, u32[]{:S(2)}, u32[]{:S(2)}) collective-permute-start(f32[22,4,128]{2,1,0:T(4,128)S(1)} %bitcast.151), channel_id=1, source_target_pairs={{0,6},{1,7},{2,4},{3,5},{4,2},{5,3},{6,0},{7,1},{8,14},{9,15},{10,... | collective-permute-start | bytes 135176 | tf_op jit(solution)/shard_map/ppermute | solution.py:686
  68.6 1.5 %collective-permute-start.26 = (f32[22,4,128]{2,1,0:T(4,128)S(1)}, f32[22,4,128]{2,1,0:T(4,128)S(1)}, u32[]{:S(2)}, u32[]{:S(2)}) collective-permute-start(f32[22,4,128]{2,1,0:T(4,128)S(1)} %bitcast.149), channel_id=1, source_target_pairs={{0,7},{1,6},{2,5},{3,4},{4,3},{5,2},{6,1},{7,0},{8,15},{9,14},{10,... | collective-permute-start | bytes 135176 | tf_op jit(solution)/shard_map/ppermute | solution.py:686
  70.1 2.4 %collective-permute-start.27 = (f32[22,4,128]{2,1,0:T(4,128)S(1)}, f32[22,4,128]{2,1,0:T(4,128)S(1)}, u32[]{:S(2)}, u32[]{:S(2)}) collective-permute-start(f32[22,4,128]{2,1,0:T(4,128)S(1)} %bitcast.147), channel_id=1, source_target_pairs={{0,8},{1,9},{2,10},{3,11},{4,12},{5,13},{6,14},{7,15},{8,0},{9,1},... | collective-permute-start | bytes 135176 | tf_op jit(solution)/shard_map/ppermute | solution.py:686
  72.5 0.1 collective-permute-start.28
  72.7 2.3 %collective-permute-start.29 = (f32[22,4,128]{2,1,0:T(4,128)S(1)}, f32[22,4,128]{2,1,0:T(4,128)S(1)}, u32[]{:S(2)}, u32[]{:S(2)}) collective-permute-start(f32[22,4,128]{2,1,0:T(4,128)S(1)} %bitcast.143), channel_id=1, source_target_pairs={{0,10},{1,11},{2,8},{3,9},{4,14},{5,15},{6,12},{7,13},{8,2},{9,3},... | collective-permute-start | bytes 135176 | tf_op jit(solution)/shard_map/ppermute | solution.py:686
  75.0 1.5 %collective-permute-start.30 = (f32[22,4,128]{2,1,0:T(4,128)S(1)}, f32[22,4,128]{2,1,0:T(4,128)S(1)}, u32[]{:S(2)}, u32[]{:S(2)}) collective-permute-start(f32[22,4,128]{2,1,0:T(4,128)S(1)} %bitcast.137), channel_id=1, source_target_pairs={{0,11},{1,10},{2,9},{3,8},{4,15},{5,14},{6,13},{7,12},{8,3},{9,2},... | collective-permute-start | bytes 135176 | tf_op jit(solution)/shard_map/ppermute | solution.py:686
  76.5 2.0 %collective-permute-start.31 = (f32[22,4,128]{2,1,0:T(4,128)S(1)}, f32[22,4,128]{2,1,0:T(4,128)S(1)}, u32[]{:S(2)}, u32[]{:S(2)}) collective-permute-start(f32[22,4,128]{2,1,0:T(4,128)S(1)} %bitcast.134), channel_id=1, source_target_pairs={{0,12},{1,13},{2,14},{3,15},{4,8},{5,9},{6,10},{7,11},{8,4},{9,5},... | collective-permute-start | bytes 135176 | tf_op jit(solution)/shard_map/ppermute | solution.py:686
  78.5 1.2 %collective-permute-start.32 = (f32[22,4,128]{2,1,0:T(4,128)S(1)}, f32[22,4,128]{2,1,0:T(4,128)S(1)}, u32[]{:S(2)}, u32[]{:S(2)}) collective-permute-start(f32[22,4,128]{2,1,0:T(4,128)S(1)} %bitcast.132), channel_id=1, source_target_pairs={{0,13},{1,12},{2,15},{3,14},{4,9},{5,8},{6,11},{7,10},{8,5},{9,4},... | collective-permute-start | bytes 135176 | tf_op jit(solution)/shard_map/ppermute | solution.py:686
  79.8 2.4 %collective-permute-start.33 = (f32[22,4,128]{2,1,0:T(4,128)S(1)}, f32[22,4,128]{2,1,0:T(4,128)S(1)}, u32[]{:S(2)}, u32[]{:S(2)}) collective-permute-start(f32[22,4,128]{2,1,0:T(4,128)S(1)} %bitcast.131), channel_id=1, source_target_pairs={{0,14},{1,15},{2,12},{3,13},{4,10},{5,11},{6,8},{7,9},{8,6},{9,7},... | collective-permute-start | bytes 135176 | tf_op jit(solution)/shard_map/ppermute | solution.py:686
  82.1 2.4 %collective-permute-start.34 = (f32[22,4,128]{2,1,0:T(4,128)S(1)}, f32[22,4,128]{2,1,0:T(4,128)S(1)}, u32[]{:S(2)}, u32[]{:S(2)}) collective-permute-start(f32[22,4,128]{2,1,0:T(4,128)S(1)} %bitcast.130), channel_id=1, source_target_pairs={{0,15},{1,14},{2,13},{3,12},{4,11},{5,10},{6,9},{7,8},{8,7},{9,6},... | collective-permute-start | bytes 135176 | tf_op jit(solution)/shard_map/ppermute | solution.py:686
  84.5 3.6 %shard_map.83 = (f32[88,128]{1,0:T(8,128)S(1)}, f32[88,128]{1,0:T(8,128)S(1)}, f32[88,128]{1,0:T(8,128)S(1)}, f32[88,128]{1,0:T(8,128)S(1)}, f32[88,128]{1,0:T(8...) custom-call(f32[5]{0:T(128)S(1)} %stack.32.scales, ...), custom_call_target="tpu_custom_call" | custom-call | flops 3000000000 | bytes 3231744 | tf_op jit(solution)/shard_map/pallas_call | solution.py:590
  88.3 0.3 collective-permute-start.36
  88.6 1.8 %collective-permute-start.37 = (f32[22,4,128]{2,1,0:T(4,128)S(1)}, f32[22,4,128]{2,1,0:T(4,128)S(1)}, u32[]{:S(2)}, u32[]{:S(2)}) collective-permute-start(f32[22,4,128]{2,1,0:T(4,128)S(1)} %bitcast.152), channel_id=1, source_target_pairs={{0,3},{1,2},{2,1},{3,0},{4,7},{5,6},{6,5},{7,4},{8,11},{9,10},{10,... | collective-permute-start | bytes 135176 | tf_op jit(solution)/shard_map/ppermute | solution.py:686
  90.4 1.4 %collective-permute-start.39 = (f32[22,4,128]{2,1,0:T(4,128)S(1)}, f32[22,4,128]{2,1,0:T(4,128)S(1)}, u32[]{:S(2)}, u32[]{:S(2)}) collective-permute-start(f32[22,4,128]{2,1,0:T(4,128)S(1)} %bitcast.148), channel_id=1, source_target_pairs={{0,5},{1,4},{2,7},{3,6},{4,1},{5,0},{6,3},{7,2},{8,13},{9,12},{10,... | collective-permute-start | bytes 135176 | tf_op jit(solution)/shard_map/ppermute | solution.py:686
  91.9 2.9 %collective-permute-start.41 = (f32[22,4,128]{2,1,0:T(4,128)S(1)}, f32[22,4,128]{2,1,0:T(4,128)S(1)}, u32[]{:S(2)}, u32[]{:S(2)}) collective-permute-start(f32[22,4,128]{2,1,0:T(4,128)S(1)} %bitcast.144), channel_id=1, source_target_pairs={{0,7},{1,6},{2,5},{3,4},{4,3},{5,2},{6,1},{7,0},{8,15},{9,14},{10,... | collective-permute-start | bytes 135176 | tf_op jit(solution)/shard_map/ppermute | solution.py:686
  94.8 0.9 collective-permute-start.42
  95.8 1.4 %collective-permute-start.43 = (f32[22,4,128]{2,1,0:T(4,128)S(1)}, f32[22,4,128]{2,1,0:T(4,128)S(1)}, u32[]{:S(2)}, u32[]{:S(2)}) collective-permute-start(f32[22,4,128]{2,1,0:T(4,128)S(1)} %bitcast.141), channel_id=1, source_target_pairs={{0,9},{1,8},{2,11},{3,10},{4,13},{5,12},{6,15},{7,14},{8,1},{9,0},... | collective-permute-start | bytes 135176 | tf_op jit(solution)/shard_map/ppermute | solution.py:686
  97.2 1.5 %collective-permute-start.44 = (f32[22,4,128]{2,1,0:T(4,128)S(1)}, f32[22,4,128]{2,1,0:T(4,128)S(1)}, u32[]{:S(2)}, u32[]{:S(2)}) collective-permute-start(f32[22,4,128]{2,1,0:T(4,128)S(1)} %bitcast.140), channel_id=1, source_target_pairs={{0,10},{1,11},{2,8},{3,9},{4,14},{5,15},{6,12},{7,13},{8,2},{9,3},... | collective-permute-start | bytes 135176 | tf_op jit(solution)/shard_map/ppermute | solution.py:686
  98.7 2.4 %collective-permute-start.45 = (f32[22,4,128]{2,1,0:T(4,128)S(1)}, f32[22,4,128]{2,1,0:T(4,128)S(1)}, u32[]{:S(2)}, u32[]{:S(2)}) collective-permute-start(f32[22,4,128]{2,1,0:T(4,128)S(1)} %bitcast.139), channel_id=1, source_target_pairs={{0,11},{1,10},{2,9},{3,8},{4,15},{5,14},{6,13},{7,12},{8,3},{9,2},... | collective-permute-start | bytes 135176 | tf_op jit(solution)/shard_map/ppermute | solution.py:686
  101.0 2.0 %collective-permute-start.46 = (f32[22,4,128]{2,1,0:T(4,128)S(1)}, f32[22,4,128]{2,1,0:T(4,128)S(1)}, u32[]{:S(2)}, u32[]{:S(2)}) collective-permute-start(f32[22,4,128]{2,1,0:T(4,128)S(1)} %bitcast.138), channel_id=1, source_target_pairs={{0,12},{1,13},{2,14},{3,15},{4,8},{5,9},{6,10},{7,11},{8,4},{9,5},... | collective-permute-start | bytes 135176 | tf_op jit(solution)/shard_map/ppermute | solution.py:686
  103.0 1.2 %collective-permute-start.47 = (f32[22,4,128]{2,1,0:T(4,128)S(1)}, f32[22,4,128]{2,1,0:T(4,128)S(1)}, u32[]{:S(2)}, u32[]{:S(2)}) collective-permute-start(f32[22,4,128]{2,1,0:T(4,128)S(1)} %bitcast.136), channel_id=1, source_target_pairs={{0,13},{1,12},{2,15},{3,14},{4,9},{5,8},{6,11},{7,10},{8,5},{9,4},... | collective-permute-start | bytes 135176 | tf_op jit(solution)/shard_map/ppermute | solution.py:686
  104.3 2.6 %collective-permute-start.48 = (f32[22,4,128]{2,1,0:T(4,128)S(1)}, f32[22,4,128]{2,1,0:T(4,128)S(1)}, u32[]{:S(2)}, u32[]{:S(2)}) collective-permute-start(f32[22,4,128]{2,1,0:T(4,128)S(1)} %bitcast.135), channel_id=1, source_target_pairs={{0,14},{1,15},{2,12},{3,13},{4,10},{5,11},{6,8},{7,9},{8,6},{9,7},... | collective-permute-start | bytes 135176 | tf_op jit(solution)/shard_map/ppermute | solution.py:686
  106.9 2.2 %collective-permute-start.49 = (f32[22,4,128]{2,1,0:T(4,128)S(1)}, f32[22,4,128]{2,1,0:T(4,128)S(1)}, u32[]{:S(2)}, u32[]{:S(2)}) collective-permute-start(f32[22,4,128]{2,1,0:T(4,128)S(1)} %bitcast.133), channel_id=1, source_target_pairs={{0,15},{1,14},{2,13},{3,12},{4,11},{5,10},{6,9},{7,8},{8,7},{9,6},... | collective-permute-start | bytes 135176 | tf_op jit(solution)/shard_map/ppermute | solution.py:686
  109.1 0.9 collective-permute-done.48.refs_30_
  109.9 3.9 %collective-permute-done.49.refs_31_ = f32[22,4,128]{2,1,0:T(4,128)S(1)} collective-permute-done((f32[22,4,128]{2,1,0:T(4,128)S(1)}, f32[22,4,128]{2,1,0:T(4,128)S(1)}, u32[]{:S(2)}, u32[]{:S(2)}) %collective-permute-start.49) | collective-permute-done | bytes 45088 | tf_op jit(solution)/shard_map/ppermute | solution.py:686
  113.8 1.9 %shard_map.84 = (f32[22,16,4,128]{3,2,1,0:T(4,128)}, f32[22,16,4,128]{3,2,1,0:T(4,128)}) custom-call(s32[16]{0:T(128)S(1)} %add.66.targets, f32[22,4,128]{2,1,0:T(4,128)S(1)} %bitcast.114, f32[22,4,128]{2,1,0:T(4,128)S(1)} %collective-permute-done.20.refs_1_, f32[22,4,128]{2,1,0:T(4,128)S(1)} %collective-permute-done.21.refs_2_, ...), custom_call_target="tpu_custom_call" | custom-call | bytes 2883584 | tf_op jit(solution)/shard_map/pallas_call | solution.py:590
  (75 shorter events, 1.2 us)
Async XLA Ops:
  0.9 11.1 %copy-start = (f32[6,2,4096]{2,1,0:T(2,128)S(1)}, f32[6,2,4096]{2,1,0:T(2,128)}, u32[]{:S(2)}) copy-start(f32[6,2,4096]{2,1,0:T(2,128)} %param.8) | copy-start | bytes 589828
  0.9 11.1 %copy-start.1 = (f32[2,4096]{1,0:T(2,128)S(1)}, f32[2,4096]{1,0:T(2,128)}, u32[]{:S(2)}) copy-start(f32[2,4096]{1,0:T(2,128)} %param.7) | copy-start | bytes 98308
  2.6 16.4 %collective-permute-start.3 = (f32[22,4,128]{2,1,0:T(4,128)S(1)}, f32[22,4,128]{2,1,0:T(4,128)S(1)}, u32[]{:S(2)}, u32[]{:S(2)}) collective-permute-start(f32[22,4,128]{2,1,0:T(4,128)S(1)} %get-tuple-element.77), channel_id=1, source_target_pairs={{0,1},{1,0},{2,3},{3,2},{4,5},{5,4},{6,7},{7,6},{8,9},{9,8},{10,11... | collective-permute-start | bytes 135176 | tf_op jit(solution)/shard_map/ppermute | solution.py:686
  2.8 17.4 %collective-permute-start.4 = (f32[22,4,128]{2,1,0:T(4,128)S(1)}, f32[22,4,128]{2,1,0:T(4,128)S(1)}, u32[]{:S(2)}, u32[]{:S(2)}) collective-permute-start(f32[22,4,128]{2,1,0:T(4,128)S(1)} %get-tuple-element.78), channel_id=1, source_target_pairs={{0,2},{1,3},{2,0},{3,1},{4,6},{5,7},{6,4},{7,5},{8,10},{9,11},{10,... | collective-permute-start | bytes 135176 | tf_op jit(solution)/shard_map/ppermute | solution.py:686
  12.5 1.9 %collective-permute-start = (f32[84,128]{1,0:T(8,128)S(1)}, f32[84,128]{1,0:T(8,128)S(1)}, u32[]{:S(2)}, u32[]{:S(2)}) collective-permute-start(f32[84,128]{1,0:T(8,128)S(1)} %get-tuple-element.70), channel_id=1, source_target_pairs={{0,1},{1,2},{2,3},{3,0},{4,5},{5,6},{6,7},{7,4},{8,9},{9,10},{10,1... | collective-permute-start | bytes 129032 | tf_op jit(solution)/shard_map/ppermute | solution.py:718
  12.6 4.2 %collective-permute-start.1 = (f32[84,128]{1,0:T(8,128)S(1)}, f32[84,128]{1,0:T(8,128)S(1)}, u32[]{:S(2)}, u32[]{:S(2)}) collective-permute-start(f32[84,128]{1,0:T(8,128)S(1)} %get-tuple-element.71), channel_id=1, source_target_pairs={{0,2},{1,3},{2,0},{3,1},{4,6},{5,7},{6,4},{7,5},{8,10},{9,11},{10,... | collective-permute-start | bytes 129032 | tf_op jit(solution)/shard_map/ppermute | solution.py:718
  14.3 3.8 %collective-permute-start.2 = (f32[84,128]{1,0:T(8,128)S(1)}, f32[84,128]{1,0:T(8,128)S(1)}, u32[]{:S(2)}, u32[]{:S(2)}) collective-permute-start(f32[84,128]{1,0:T(8,128)S(1)} %get-tuple-element.72), channel_id=1, source_target_pairs={{0,3},{1,0},{2,1},{3,2},{4,7},{5,4},{6,5},{7,6},{8,11},{9,8},{10,9... | collective-permute-start | bytes 129032 | tf_op jit(solution)/shard_map/ppermute | solution.py:718
  14.4 7.6 %collective-permute-start.5 = (f32[22,4,128]{2,1,0:T(4,128)S(1)}, f32[22,4,128]{2,1,0:T(4,128)S(1)}, u32[]{:S(2)}, u32[]{:S(2)}) collective-permute-start(f32[22,4,128]{2,1,0:T(4,128)S(1)} %get-tuple-element.79), channel_id=1, source_target_pairs={{0,3},{1,2},{2,1},{3,0},{4,7},{5,6},{6,5},{7,4},{8,11},{9,10},{10,... | collective-permute-start | bytes 135176 | tf_op jit(solution)/shard_map/ppermute | solution.py:686
  16.8 7.6 %collective-permute-start.6 = (f32[22,4,128]{2,1,0:T(4,128)S(1)}, f32[22,4,128]{2,1,0:T(4,128)S(1)}, u32[]{:S(2)}, u32[]{:S(2)}) collective-permute-start(f32[22,4,128]{2,1,0:T(4,128)S(1)} %get-tuple-element.80), channel_id=1, source_target_pairs={{0,4},{1,5},{2,6},{3,7},{4,0},{5,1},{6,2},{7,3},{8,12},{9,13},{10,... | collective-permute-start | bytes 135176 | tf_op jit(solution)/shard_map/ppermute | solution.py:686
  18.1 6.4 %collective-permute-start.7 = (f32[22,4,128]{2,1,0:T(4,128)S(1)}, f32[22,4,128]{2,1,0:T(4,128)S(1)}, u32[]{:S(2)}, u32[]{:S(2)}) collective-permute-start(f32[22,4,128]{2,1,0:T(4,128)S(1)} %get-tuple-element.81), channel_id=1, source_target_pairs={{0,5},{1,4},{2,7},{3,6},{4,1},{5,0},{6,3},{7,2},{8,13},{9,12},{10,... | collective-permute-start | bytes 135176 | tf_op jit(solution)/shard_map/ppermute | solution.py:686
  19.0 7.6 %collective-permute-start.8 = (f32[22,4,128]{2,1,0:T(4,128)S(1)}, f32[22,4,128]{2,1,0:T(4,128)S(1)}, u32[]{:S(2)}, u32[]{:S(2)}) collective-permute-start(f32[22,4,128]{2,1,0:T(4,128)S(1)} %get-tuple-element.82), channel_id=1, source_target_pairs={{0,6},{1,7},{2,4},{3,5},{4,2},{5,3},{6,0},{7,1},{8,14},{9,15},{10,... | collective-permute-start | bytes 135176 | tf_op jit(solution)/shard_map/ppermute | solution.py:686
  20.2 8.1 %collective-permute-start.9 = (f32[22,4,128]{2,1,0:T(4,128)S(1)}, f32[22,4,128]{2,1,0:T(4,128)S(1)}, u32[]{:S(2)}, u32[]{:S(2)}) collective-permute-start(f32[22,4,128]{2,1,0:T(4,128)S(1)} %get-tuple-element.83), channel_id=1, source_target_pairs={{0,7},{1,6},{2,5},{3,4},{4,3},{5,2},{6,1},{7,0},{8,15},{9,14},{10,... | collective-permute-start | bytes 135176 | tf_op jit(solution)/shard_map/ppermute | solution.py:686
  22.1 8.7 %collective-permute-start.10 = (f32[22,4,128]{2,1,0:T(4,128)S(1)}, f32[22,4,128]{2,1,0:T(4,128)S(1)}, u32[]{:S(2)}, u32[]{:S(2)}) collective-permute-start(f32[22,4,128]{2,1,0:T(4,128)S(1)} %get-tuple-element.84), channel_id=1, source_target_pairs={{0,8},{1,9},{2,10},{3,11},{4,12},{5,13},{6,14},{7,15},{8,0},{9,1},... | collective-permute-start | bytes 135176 | tf_op jit(solution)/shard_map/ppermute | solution.py:686
  24.4 8.7 %collective-permute-start.11 = (f32[22,4,128]{2,1,0:T(4,128)S(1)}, f32[22,4,128]{2,1,0:T(4,128)S(1)}, u32[]{:S(2)}, u32[]{:S(2)}) collective-permute-start(f32[22,4,128]{2,1,0:T(4,128)S(1)} %get-tuple-element.85), channel_id=1, source_target_pairs={{0,9},{1,8},{2,11},{3,10},{4,13},{5,12},{6,15},{7,14},{8,1},{9,0},... | collective-permute-start | bytes 135176 | tf_op jit(solution)/shard_map/ppermute | solution.py:686
  24.4 10.2 %collective-permute-start.12 = (f32[22,4,128]{2,1,0:T(4,128)S(1)}, f32[22,4,128]{2,1,0:T(4,128)S(1)}, u32[]{:S(2)}, u32[]{:S(2)}) collective-permute-start(f32[22,4,128]{2,1,0:T(4,128)S(1)} %get-tuple-element.86), channel_id=1, source_target_pairs={{0,10},{1,11},{2,8},{3,9},{4,14},{5,15},{6,12},{7,13},{8,2},{9,3},... | collective-permute-start | bytes 135176 | tf_op jit(solution)/shard_map/ppermute | solution.py:686
  26.6 11.5 %collective-permute-start.13 = (f32[22,4,128]{2,1,0:T(4,128)S(1)}, f32[22,4,128]{2,1,0:T(4,128)S(1)}, u32[]{:S(2)}, u32[]{:S(2)}) collective-permute-start(f32[22,4,128]{2,1,0:T(4,128)S(1)} %get-tuple-element.87), channel_id=1, source_target_pairs={{0,11},{1,10},{2,9},{3,8},{4,15},{5,14},{6,13},{7,12},{8,3},{9,2},... | collective-permute-start | bytes 135176 | tf_op jit(solution)/shard_map/ppermute | solution.py:686
  28.3 9.8 %collective-permute-start.14 = (f32[22,4,128]{2,1,0:T(4,128)S(1)}, f32[22,4,128]{2,1,0:T(4,128)S(1)}, u32[]{:S(2)}, u32[]{:S(2)}) collective-permute-start(f32[22,4,128]{2,1,0:T(4,128)S(1)} %get-tuple-element.88), channel_id=1, source_target_pairs={{0,12},{1,13},{2,14},{3,15},{4,8},{5,9},{6,10},{7,11},{8,4},{9,5},... | collective-permute-start | bytes 135176 | tf_op jit(solution)/shard_map/ppermute | solution.py:686
  30.8 7.4 %collective-permute-start.15 = (f32[22,4,128]{2,1,0:T(4,128)S(1)}, f32[22,4,128]{2,1,0:T(4,128)S(1)}, u32[]{:S(2)}, u32[]{:S(2)}) collective-permute-start(f32[22,4,128]{2,1,0:T(4,128)S(1)} %get-tuple-element.89), channel_id=1, source_target_pairs={{0,13},{1,12},{2,15},{3,14},{4,9},{5,8},{6,11},{7,10},{8,5},{9,4},... | collective-permute-start | bytes 135176 | tf_op jit(solution)/shard_map/ppermute | solution.py:686
  33.0 5.6 %collective-permute-start.16 = (f32[22,4,128]{2,1,0:T(4,128)S(1)}, f32[22,4,128]{2,1,0:T(4,128)S(1)}, u32[]{:S(2)}, u32[]{:S(2)}) collective-permute-start(f32[22,4,128]{2,1,0:T(4,128)S(1)} %get-tuple-element.90), channel_id=1, source_target_pairs={{0,14},{1,15},{2,12},{3,13},{4,10},{5,11},{6,8},{7,9},{8,6},{9,7},... | collective-permute-start | bytes 135176 | tf_op jit(solution)/shard_map/ppermute | solution.py:686
  34.7 6.8 %collective-permute-start.17 = (f32[22,4,128]{2,1,0:T(4,128)S(1)}, f32[22,4,128]{2,1,0:T(4,128)S(1)}, u32[]{:S(2)}, u32[]{:S(2)}) collective-permute-start(f32[22,4,128]{2,1,0:T(4,128)S(1)} %get-tuple-element.91), channel_id=1, source_target_pairs={{0,15},{1,14},{2,13},{3,12},{4,11},{5,10},{6,9},{7,8},{8,7},{9,6},... | collective-permute-start | bytes 135176 | tf_op jit(solution)/shard_map/ppermute | solution.py:686
  43.2 10.9 %collective-permute-start.18 = (f32[1056,128]{1,0:T(8,128)}, f32[1056,128]{1,0:T(8,128)S(1)}, u32[]{:S(2)}, u32[]{:S(2)}) collective-permute-start(f32[1056,128]{1,0:T(8,128)} %get-tuple-element.96), channel_id=1, source_target_pairs={{1,2},{3,7},{6,5},{4,8},{9,10},{11,15},{14,13},{2,1},{7,3},{5,6},{... | collective-permute-start | bytes 1622024 | tf_op jit(solution)/shard_map/ppermute | solution.py:741
  45.8 8.2 %collective-permute-start.19 = (f32[1056,128]{1,0:T(8,128)S(1)}, f32[1056,128]{1,0:T(8,128)S(1)}, u32[]{:S(2)}, u32[]{:S(2)}) collective-permute-start(f32[1056,128]{1,0:T(8,128)S(1)} %get-tuple-element.97), channel_id=1, source_target_pairs={{0,1},{2,3},{7,6},{5,4},{8,9},{10,11},{15,14},{13,12},{1,0},{3,2},... | collective-permute-start | bytes 1622024 | tf_op jit(solution)/shard_map/ppermute | solution.py:741
  63.5 3.6 %collective-permute-start.20 = (f32[22,4,128]{2,1,0:T(4,128)S(1)}, f32[22,4,128]{2,1,0:T(4,128)S(1)}, u32[]{:S(2)}, u32[]{:S(2)}) collective-permute-start(f32[22,4,128]{2,1,0:T(4,128)S(1)} %bitcast.159), channel_id=1, source_target_pairs={{0,1},{1,0},{2,3},{3,2},{4,5},{5,4},{6,7},{7,6},{8,9},{9,8},{10,11... | collective-permute-start | bytes 135176 | tf_op jit(solution)/shard_map/ppermute | solution.py:686
  63.6 5.0 %collective-permute-start.21 = (f32[22,4,128]{2,1,0:T(4,128)S(1)}, f32[22,4,128]{2,1,0:T(4,128)S(1)}, u32[]{:S(2)}, u32[]{:S(2)}) collective-permute-start(f32[22,4,128]{2,1,0:T(4,128)S(1)} %bitcast.158), channel_id=1, source_target_pairs={{0,2},{1,3},{2,0},{3,1},{4,6},{5,7},{6,4},{7,5},{8,10},{9,11},{10,... | collective-permute-start | bytes 135176 | tf_op jit(solution)/shard_map/ppermute | solution.py:686
  64.3 5.9 %collective-permute-start.22 = (f32[22,4,128]{2,1,0:T(4,128)S(1)}, f32[22,4,128]{2,1,0:T(4,128)S(1)}, u32[]{:S(2)}, u32[]{:S(2)}) collective-permute-start(f32[22,4,128]{2,1,0:T(4,128)S(1)} %bitcast.157), channel_id=1, source_target_pairs={{0,3},{1,2},{2,1},{3,0},{4,7},{5,6},{6,5},{7,4},{8,11},{9,10},{10,... | collective-permute-start | bytes 135176 | tf_op jit(solution)/shard_map/ppermute | solution.py:686
  65.7 6.8 %collective-permute-start.23 = (f32[22,4,128]{2,1,0:T(4,128)S(1)}, f32[22,4,128]{2,1,0:T(4,128)S(1)}, u32[]{:S(2)}, u32[]{:S(2)}) collective-permute-start(f32[22,4,128]{2,1,0:T(4,128)S(1)} %bitcast.155), channel_id=1, source_target_pairs={{0,4},{1,5},{2,6},{3,7},{4,0},{5,1},{6,2},{7,3},{8,12},{9,13},{10,... | collective-permute-start | bytes 135176 | tf_op jit(solution)/shard_map/ppermute | solution.py:686
  66.7 6.0 %collective-permute-start.24 = (f32[22,4,128]{2,1,0:T(4,128)S(1)}, f32[22,4,128]{2,1,0:T(4,128)S(1)}, u32[]{:S(2)}, u32[]{:S(2)}) collective-permute-start(f32[22,4,128]{2,1,0:T(4,128)S(1)} %bitcast.153), channel_id=1, source_target_pairs={{0,5},{1,4},{2,7},{3,6},{4,1},{5,0},{6,3},{7,2},{8,13},{9,12},{10,... | collective-permute-start | bytes 135176 | tf_op jit(solution)/shard_map/ppermute | solution.py:686
  67.1 7.8 %collective-permute-start.25 = (f32[22,4,128]{2,1,0:T(4,128)S(1)}, f32[22,4,128]{2,1,0:T(4,128)S(1)}, u32[]{:S(2)}, u32[]{:S(2)}) collective-permute-start(f32[22,4,128]{2,1,0:T(4,128)S(1)} %bitcast.151), channel_id=1, source_target_pairs={{0,6},{1,7},{2,4},{3,5},{4,2},{5,3},{6,0},{7,1},{8,14},{9,15},{10,... | collective-permute-start | bytes 135176 | tf_op jit(solution)/shard_map/ppermute | solution.py:686
  68.6 7.9 %collective-permute-start.26 = (f32[22,4,128]{2,1,0:T(4,128)S(1)}, f32[22,4,128]{2,1,0:T(4,128)S(1)}, u32[]{:S(2)}, u32[]{:S(2)}) collective-permute-start(f32[22,4,128]{2,1,0:T(4,128)S(1)} %bitcast.149), channel_id=1, source_target_pairs={{0,7},{1,6},{2,5},{3,4},{4,3},{5,2},{6,1},{7,0},{8,15},{9,14},{10,... | collective-permute-start | bytes 135176 | tf_op jit(solution)/shard_map/ppermute | solution.py:686
  70.1 8.4 %collective-permute-start.27 = (f32[22,4,128]{2,1,0:T(4,128)S(1)}, f32[22,4,128]{2,1,0:T(4,128)S(1)}, u32[]{:S(2)}, u32[]{:S(2)}) collective-permute-start(f32[22,4,128]{2,1,0:T(4,128)S(1)} %bitcast.147), channel_id=1, source_target_pairs={{0,8},{1,9},{2,10},{3,11},{4,12},{5,13},{6,14},{7,15},{8,0},{9,1},... | collective-permute-start | bytes 135176 | tf_op jit(solution)/shard_map/ppermute | solution.py:686
  72.5 7.2 %collective-permute-start.28 = (f32[22,4,128]{2,1,0:T(4,128)S(1)}, f32[22,4,128]{2,1,0:T(4,128)S(1)}, u32[]{:S(2)}, u32[]{:S(2)}) collective-permute-start(f32[22,4,128]{2,1,0:T(4,128)S(1)} %bitcast.145), channel_id=1, source_target_pairs={{0,9},{1,8},{2,11},{3,10},{4,13},{5,12},{6,15},{7,14},{8,1},{9,0},... | collective-permute-start | bytes 135176 | tf_op jit(solution)/shard_map/ppermute | solution.py:686
  72.7 9.5 %collective-permute-start.29 = (f32[22,4,128]{2,1,0:T(4,128)S(1)}, f32[22,4,128]{2,1,0:T(4,128)S(1)}, u32[]{:S(2)}, u32[]{:S(2)}) collective-permute-start(f32[22,4,128]{2,1,0:T(4,128)S(1)} %bitcast.143), channel_id=1, source_target_pairs={{0,10},{1,11},{2,8},{3,9},{4,14},{5,15},{6,12},{7,13},{8,2},{9,3},... | collective-permute-start | bytes 135176 | tf_op jit(solution)/shard_map/ppermute | solution.py:686
  75.0 13.2 %collective-permute-start.30 = (f32[22,4,128]{2,1,0:T(4,128)S(1)}, f32[22,4,128]{2,1,0:T(4,128)S(1)}, u32[]{:S(2)}, u32[]{:S(2)}) collective-permute-start(f32[22,4,128]{2,1,0:T(4,128)S(1)} %bitcast.137), channel_id=1, source_target_pairs={{0,11},{1,10},{2,9},{3,8},{4,15},{5,14},{6,13},{7,12},{8,3},{9,2},... | collective-permute-start | bytes 135176 | tf_op jit(solution)/shard_map/ppermute | solution.py:686
  76.5 11.8 %collective-permute-start.31 = (f32[22,4,128]{2,1,0:T(4,128)S(1)}, f32[22,4,128]{2,1,0:T(4,128)S(1)}, u32[]{:S(2)}, u32[]{:S(2)}) collective-permute-start(f32[22,4,128]{2,1,0:T(4,128)S(1)} %bitcast.134), channel_id=1, source_target_pairs={{0,12},{1,13},{2,14},{3,15},{4,8},{5,9},{6,10},{7,11},{8,4},{9,5},... | collective-permute-start | bytes 135176 | tf_op jit(solution)/shard_map/ppermute | solution.py:686
  78.5 10.1 %collective-permute-start.32 = (f32[22,4,128]{2,1,0:T(4,128)S(1)}, f32[22,4,128]{2,1,0:T(4,128)S(1)}, u32[]{:S(2)}, u32[]{:S(2)}) collective-permute-start(f32[22,4,128]{2,1,0:T(4,128)S(1)} %bitcast.132), channel_id=1, source_target_pairs={{0,13},{1,12},{2,15},{3,14},{4,9},{5,8},{6,11},{7,10},{8,5},{9,4},... | collective-permute-start | bytes 135176 | tf_op jit(solution)/shard_map/ppermute | solution.py:686
  79.8 10.7 %collective-permute-start.33 = (f32[22,4,128]{2,1,0:T(4,128)S(1)}, f32[22,4,128]{2,1,0:T(4,128)S(1)}, u32[]{:S(2)}, u32[]{:S(2)}) collective-permute-start(f32[22,4,128]{2,1,0:T(4,128)S(1)} %bitcast.131), channel_id=1, source_target_pairs={{0,14},{1,15},{2,12},{3,13},{4,10},{5,11},{6,8},{7,9},{8,6},{9,7},... | collective-permute-start | bytes 135176 | tf_op jit(solution)/shard_map/ppermute | solution.py:686
  82.1 8.3 %collective-permute-start.34 = (f32[22,4,128]{2,1,0:T(4,128)S(1)}, f32[22,4,128]{2,1,0:T(4,128)S(1)}, u32[]{:S(2)}, u32[]{:S(2)}) collective-permute-start(f32[22,4,128]{2,1,0:T(4,128)S(1)} %bitcast.130), channel_id=1, source_target_pairs={{0,15},{1,14},{2,13},{3,12},{4,11},{5,10},{6,9},{7,8},{8,7},{9,6},... | collective-permute-start | bytes 135176 | tf_op jit(solution)/shard_map/ppermute | solution.py:686
  88.2 3.7 %collective-permute-start.35 = (f32[22,4,128]{2,1,0:T(4,128)S(1)}, f32[22,4,128]{2,1,0:T(4,128)S(1)}, u32[]{:S(2)}, u32[]{:S(2)}) collective-permute-start(f32[22,4,128]{2,1,0:T(4,128)S(1)} %bitcast.156), channel_id=1, source_target_pairs={{0,1},{1,0},{2,3},{3,2},{4,5},{5,4},{6,7},{7,6},{8,9},{9,8},{10,11... | collective-permute-start | bytes 135176 | tf_op jit(solution)/shard_map/ppermute | solution.py:686
  88.3 3.6 %collective-permute-start.36 = (f32[22,4,128]{2,1,0:T(4,128)S(1)}, f32[22,4,128]{2,1,0:T(4,128)S(1)}, u32[]{:S(2)}, u32[]{:S(2)}) collective-permute-start(f32[22,4,128]{2,1,0:T(4,128)S(1)} %bitcast.154), channel_id=1, source_target_pairs={{0,2},{1,3},{2,0},{3,1},{4,6},{5,7},{6,4},{7,5},{8,10},{9,11},{10,... | collective-permute-start | bytes 135176 | tf_op jit(solution)/shard_map/ppermute | solution.py:686
  88.6 6.2 %collective-permute-start.37 = (f32[22,4,128]{2,1,0:T(4,128)S(1)}, f32[22,4,128]{2,1,0:T(4,128)S(1)}, u32[]{:S(2)}, u32[]{:S(2)}) collective-permute-start(f32[22,4,128]{2,1,0:T(4,128)S(1)} %bitcast.152), channel_id=1, source_target_pairs={{0,3},{1,2},{2,1},{3,0},{4,7},{5,6},{6,5},{7,4},{8,11},{9,10},{10,... | collective-permute-start | bytes 135176 | tf_op jit(solution)/shard_map/ppermute | solution.py:686
  90.4 5.4 %collective-permute-start.38 = (f32[22,4,128]{2,1,0:T(4,128)S(1)}, f32[22,4,128]{2,1,0:T(4,128)S(1)}, u32[]{:S(2)}, u32[]{:S(2)}) collective-permute-start(f32[22,4,128]{2,1,0:T(4,128)S(1)} %bitcast.150), channel_id=1, source_target_pairs={{0,4},{1,5},{2,6},{3,7},{4,0},{5,1},{6,2},{7,3},{8,12},{9,13},{10,... | collective-permute-start | bytes 135176 | tf_op jit(solution)/shard_map/ppermute | solution.py:686
  90.4 6.7 %collective-permute-start.39 = (f32[22,4,128]{2,1,0:T(4,128)S(1)}, f32[22,4,128]{2,1,0:T(4,128)S(1)}, u32[]{:S(2)}, u32[]{:S(2)}) collective-permute-start(f32[22,4,128]{2,1,0:T(4,128)S(1)} %bitcast.148), channel_id=1, source_target_pairs={{0,5},{1,4},{2,7},{3,6},{4,1},{5,0},{6,3},{7,2},{8,13},{9,12},{10,... | collective-permute-start | bytes 135176 | tf_op jit(solution)/shard_map/ppermute | solution.py:686
  91.9 6.8 %collective-permute-start.40 = (f32[22,4,128]{2,1,0:T(4,128)S(1)}, f32[22,4,128]{2,1,0:T(4,128)S(1)}, u32[]{:S(2)}, u32[]{:S(2)}) collective-permute-start(f32[22,4,128]{2,1,0:T(4,128)S(1)} %bitcast.146), channel_id=1, source_target_pairs={{0,6},{1,7},{2,4},{3,5},{4,2},{5,3},{6,0},{7,1},{8,14},{9,15},{10,... | collective-permute-start | bytes 135176 | tf_op jit(solution)/shard_map/ppermute | solution.py:686
  91.9 9.1 %collective-permute-start.41 = (f32[22,4,128]{2,1,0:T(4,128)S(1)}, f32[22,4,128]{2,1,0:T(4,128)S(1)}, u32[]{:S(2)}, u32[]{:S(2)}) collective-permute-start(f32[22,4,128]{2,1,0:T(4,128)S(1)} %bitcast.144), channel_id=1, source_target_pairs={{0,7},{1,6},{2,5},{3,4},{4,3},{5,2},{6,1},{7,0},{8,15},{9,14},{10,... | collective-permute-start | bytes 135176 | tf_op jit(solution)/shard_map/ppermute | solution.py:686
  94.8 8.2 %collective-permute-start.42 = (f32[22,4,128]{2,1,0:T(4,128)S(1)}, f32[22,4,128]{2,1,0:T(4,128)S(1)}, u32[]{:S(2)}, u32[]{:S(2)}) collective-permute-start(f32[22,4,128]{2,1,0:T(4,128)S(1)} %bitcast.142), channel_id=1, source_target_pairs={{0,8},{1,9},{2,10},{3,11},{4,12},{5,13},{6,14},{7,15},{8,0},{9,1},... | collective-permute-start | bytes 135176 | tf_op jit(solution)/shard_map/ppermute | solution.py:686
  95.8 8.5 %collective-permute-start.43 = (f32[22,4,128]{2,1,0:T(4,128)S(1)}, f32[22,4,128]{2,1,0:T(4,128)S(1)}, u32[]{:S(2)}, u32[]{:S(2)}) collective-permute-start(f32[22,4,128]{2,1,0:T(4,128)S(1)} %bitcast.141), channel_id=1, source_target_pairs={{0,9},{1,8},{2,11},{3,10},{4,13},{5,12},{6,15},{7,14},{8,1},{9,0},... | collective-permute-start | bytes 135176 | tf_op jit(solution)/shard_map/ppermute | solution.py:686
  97.2 9.7 %collective-permute-start.44 = (f32[22,4,128]{2,1,0:T(4,128)S(1)}, f32[22,4,128]{2,1,0:T(4,128)S(1)}, u32[]{:S(2)}, u32[]{:S(2)}) collective-permute-start(f32[22,4,128]{2,1,0:T(4,128)S(1)} %bitcast.140), channel_id=1, source_target_pairs={{0,10},{1,11},{2,8},{3,9},{4,14},{5,15},{6,12},{7,13},{8,2},{9,3},... | collective-permute-start | bytes 135176 | tf_op jit(solution)/shard_map/ppermute | solution.py:686
  98.7 10.4 %collective-permute-start.45 = (f32[22,4,128]{2,1,0:T(4,128)S(1)}, f32[22,4,128]{2,1,0:T(4,128)S(1)}, u32[]{:S(2)}, u32[]{:S(2)}) collective-permute-start(f32[22,4,128]{2,1,0:T(4,128)S(1)} %bitcast.139), channel_id=1, source_target_pairs={{0,11},{1,10},{2,9},{3,8},{4,15},{5,14},{6,13},{7,12},{8,3},{9,2},... | collective-permute-start | bytes 135176 | tf_op jit(solution)/shard_map/ppermute | solution.py:686
  101.0 8.0 %collective-permute-start.46 = (f32[22,4,128]{2,1,0:T(4,128)S(1)}, f32[22,4,128]{2,1,0:T(4,128)S(1)}, u32[]{:S(2)}, u32[]{:S(2)}) collective-permute-start(f32[22,4,128]{2,1,0:T(4,128)S(1)} %bitcast.138), channel_id=1, source_target_pairs={{0,12},{1,13},{2,14},{3,15},{4,8},{5,9},{6,10},{7,11},{8,4},{9,5},... | collective-permute-start | bytes 135176 | tf_op jit(solution)/shard_map/ppermute | solution.py:686
  103.0 6.0 %collective-permute-start.47 = (f32[22,4,128]{2,1,0:T(4,128)S(1)}, f32[22,4,128]{2,1,0:T(4,128)S(1)}, u32[]{:S(2)}, u32[]{:S(2)}) collective-permute-start(f32[22,4,128]{2,1,0:T(4,128)S(1)} %bitcast.136), channel_id=1, source_target_pairs={{0,13},{1,12},{2,15},{3,14},{4,9},{5,8},{6,11},{7,10},{8,5},{9,4},... | collective-permute-start | bytes 135176 | tf_op jit(solution)/shard_map/ppermute | solution.py:686
  104.3 5.6 %collective-permute-start.48 = (f32[22,4,128]{2,1,0:T(4,128)S(1)}, f32[22,4,128]{2,1,0:T(4,128)S(1)}, u32[]{:S(2)}, u32[]{:S(2)}) collective-permute-start(f32[22,4,128]{2,1,0:T(4,128)S(1)} %bitcast.135), channel_id=1, source_target_pairs={{0,14},{1,15},{2,12},{3,13},{4,10},{5,11},{6,8},{7,9},{8,6},{9,7},... | collective-permute-start | bytes 135176 | tf_op jit(solution)/shard_map/ppermute | solution.py:686
  106.9 6.9 %collective-permute-start.49 = (f32[22,4,128]{2,1,0:T(4,128)S(1)}, f32[22,4,128]{2,1,0:T(4,128)S(1)}, u32[]{:S(2)}, u32[]{:S(2)}) collective-permute-start(f32[22,4,128]{2,1,0:T(4,128)S(1)} %bitcast.133), channel_id=1, source_target_pairs={{0,15},{1,14},{2,13},{3,12},{4,11},{5,10},{6,9},{7,8},{8,7},{9,6},... | collective-permute-start | bytes 135176 | tf_op jit(solution)/shard_map/ppermute | solution.py:686

commit v6 on v4

--- a/solution.py
+++ b/solution.py
@@ -450,7 +450,7 @@
         count = FOLDED - step
         full = count - 1
         first = OWN_TILES if step == 0 else 0
-        group = 1 if step == 0 else 2
+        group = 1
         for lowest in range(0, layers, group):
             gathered, stacked = [], []
             for l in range(lowest, lowest + group):
@@ -607,7 +607,7 @@
         [shape(devices, own, pieces, LANES)],
         [],
         [by_columns(source_chaos_terms).reshape(own, devices, pieces, LANES)],
-        [pltpu.VMEM((own, devices, pieces, LANES), f32), pltpu.SemaphoreType.DMA((2,))],
+        [pltpu.VMEM((own, devices, pieces, LANES), f32), pltpu.SemaphoreType.DMA((4,))],
         in_kinds=[pltpu.HBM],
     )[0]
     gathered = lax.all_to_all(scattered, BOTH, 0, 0, tiled=True).reshape(-1, LANES)

time: 92.9 us -> 92.9 us (level)
  no operation moved by 1% of the time
where the time goes in v6:
time: 92.9 us; the launch traced here: 92.6 us
  blocking collectives  39.5 us (43%)
  Pallas kernels  20 us (22%)
  waiting for transfers between devices  14.3 us (15%)
  starting transfers between devices  12.7 us (14%)
  between operations  3.71 us (4%)
  local copies, waits for them, and re-layouts  1.12 us (1%)
    all_to_all x1, blocking collectives, local_by_cells(): received = lax.all_to_all(sent, BOTH, 0, 0, tiled=True)  39.5 us
    pallas_call x7, Pallas kernels, call(): pl.pallas_call(kernel, out_shape=outs, in_specs=in_specs, out_specs=[pl.B...  20 us
    all_to_all x1, starting transfers between devices, local_by_cells(): lax.all_to_all(scattered, BOTH, 0, 0, tiled=True).reshape(-1, LANES)  7.47 us
    ppermute x2, waiting for transfers between devices, swap(): return lax.ppermute(field, BOTH, pairs + [(b, a) for a, b in pairs])  5.46 us
    all_to_all x1, waiting for transfers between devices, local_by_cells(): lax.all_to_all(scattered, BOTH, 0, 0, tiled=True).reshape(-1, LANES)  5.42 us
    ppermute x3, waiting for transfers between devices, local_by_cells(): lax.ppermute(picked[n], 'space', [(i, (i + n) % spaces) for i in range(sp...  3.42 us
    ppermute x2, starting transfers between devices, swap(): return lax.ppermute(field, BOTH, pairs + [(b, a) for a, b in pairs])  3.02 us
    ppermute x3, starting transfers between devices, local_by_cells(): lax.ppermute(picked[n], 'space', [(i, (i + n) % spaces) for i in range(sp...  2.23 us
  transfers between devices with their start and end apart: 6, of which 5 were waited for; matrix products, arithmetic and copies ran while one was open for 2% of the time, Pallas kernels for 4%

profile of v6, /device:TPU:1, one launch (start us, length us, event | category | flops | bytes accessed | tf_op | source)
XLA Modules:
  0.0 92.6 jit_solution(14213603779985757463)
XLA Ops:
  0.6 0.0 copy-start.3
  0.6 0.0 copy-start.4
  0.7 0.0 copy-start.2
  0.7 2.1 %shard_map.79 = f32[16,22,4,128]{3,2,1,0:T(4,128)} custom-call(f32[22,16,4,128]{3,2,1,0:T(4,128)} %bitcast.68), custom_call_target="tpu_custom_call" | custom-call | bytes 1441792 | tf_op jit(solution)/shard_map/pallas_call | solution.py:532
  2.8 0.0 copy-start
  2.8 0.0 copy-start.1
  2.8 7.5 %all-to-all-start = ((f32[16,22,4,128]{3,2,1,0:T(4,128)}), f32[16,22,4,128]{3,2,1,0:T(4,128)S(1)}, u32[]{:S(2)}, u32[]{:S(2)}) async-start(f32[16,22,4,128]{3,2,1,0:T(4,128)} %shard_map.79), calls=%async_computation | async-start | bytes 1441792 | tf_op jit(solution)/shard_map/all_to_all | solution.py:613
  10.3 0.0 copy-done.3
  10.3 0.6 fusion.19
  13.4 0.0 copy-done.4
  13.4 0.1 reshape.177
  13.5 0.1 slice_bitcast_fusion
  13.7 0.0 copy-done.2
  13.8 0.1 concatenate.13
  13.8 0.4 fusion.2
  14.3 0.4 fusion
  14.8 0.1 stack.32.scales
  14.9 0.1 pad_maximum_fusion.mix_ref
  15.0 0.0 copy-done
  15.0 0.0 copy-done.1
  15.0 0.6 shard_map.77
  15.7 1.7 %collective-permute-start = (f32[84,128]{1,0:T(8,128)S(1)}, f32[84,128]{1,0:T(8,128)S(1)}, u32[]{:S(2)}, u32[]{:S(2)}) collective-permute-start(f32[84,128]{1,0:T(8,128)S(1)} %get-tuple-element.18), channel_id=1, source_target_pairs={{0,1},{1,2},{2,3},{3,0},{4,5},{5,6},{6,7},{7,4},{8,9},{9,10},{10,1... | collective-permute-start | bytes 129032 | tf_op jit(solution)/shard_map/ppermute | solution.py:636
  17.3 0.0 collective-permute-start.1
  17.3 0.5 collective-permute-start.2
  17.9 0.1 convert_reduce_fusion
  18.1 0.6 collective-permute-done.refs_1_
  18.7 2.6 %collective-permute-done.1.refs_2_ = f32[84,128]{1,0:T(8,128)S(1)} collective-permute-done((f32[84,128]{1,0:T(8,128)S(1)}, f32[84,128]{1,0:T(8,128)S(1)}, u32[]{:S(2)}, u32[]{:S(2)}) %collective-permute-start.1) | collective-permute-done | bytes 43040 | tf_op jit(solution)/shard_map/ppermute | solution.py:636
  21.3 0.2 collective-permute-done.2.refs_3_
  21.5 0.8 shard_map.78
  22.3 5.4 %all-to-all-done = f32[16,22,4,128]{3,2,1,0:T(4,128)S(1)} async-done(((f32[16,22,4,128]{3,2,1,0:T(4,128)}), f32[16,22,4,128]{3,2,1,0:T(4,128)S(1)}, u32[]{:S(2)}, u32[]{:S(2)}) %all-to-all-start) | async-done | bytes 720928 | tf_op jit(solution)/shard_map/all_to_all | solution.py:613
  27.7 0.1 mul.69.weight_ref
  27.8 1.0 %shard_map.80 = (f32[8,2,88,128]{3,2,1,0:T(8,128)S(1)}, f32[1056,128]{1,0:T(8,128)}, f32[1056,128]{1,0:T(8,128)S(1)}) custom-call(s32[1]{0:T(128)} %bitcast.9.odd, f32[7,8,640]{2,1,0:T(8,128)S(1)} %get-tuple-element.21.a_ref, f32[88,128]{1,0:T(8,128)S(1)} %mul.69.weight_ref, f32[1408,128]{1,0:T(8,128)S(1)} %bitcast.64), custom_call_target="tpu_custom_call" | custom-call | bytes 2711552 | tf_op jit(solution)/shard_map/pallas_call | solution.py:532
  28.8 3.0 %collective-permute-start.3 = (f32[1056,128]{1,0:T(8,128)}, f32[1056,128]{1,0:T(8,128)S(1)}, u32[]{:S(2)}, u32[]{:S(2)}) collective-permute-start(f32[1056,128]{1,0:T(8,128)} %get-tuple-element.28), channel_id=1, source_target_pairs={{1,2},{3,7},{6,5},{4,8},{9,10},{11,15},{14,13},{2,1},{7,3},{5,6},{... | collective-permute-start | bytes 1622024 | tf_op jit(solution)/shard_map/ppermute | solution.py:658
  31.7 0.1 collective-permute-start.4
  31.8 0.1 add_convert_fusion.inside
  31.9 2.3 %shard_map.81 = (f32[8,2,88,128]{3,2,1,0:T(8,128)S(1)}, f32[8,2,88,128]{3,2,1,0:T(8,128)S(1)}) custom-call(f32[5]{0:T(128)S(1)} %stack.32.scales, bf16[528,192]{1,0:T(8,128)(2,1)S(1)} %pad_maximum_fusion.mix_ref, f32[7,8,640]{2,1,0:T(8,128)S(1)} %get-tuple-element.21.a_ref, f32[7,8,256]{2,1,0:T(8,128)S(1)} %get-tuple-element.25.b_ref, ...), custom_call_target="tpu_custom_call" | custom-call | flops 3000000000 | bytes 2768896 | tf_op jit(solution)/shard_map/pallas_call | solution.py:532
  34.2 5.5 %collective-permute-done.3.chip_ref = f32[1056,128]{1,0:T(8,128)S(1)} collective-permute-done((f32[1056,128]{1,0:T(8,128)}, f32[1056,128]{1,0:T(8,128)S(1)}, u32[]{:S(2)}, u32[]{:S(2)}) %collective-permute-start.3) | collective-permute-done | bytes 540704 | tf_op jit(solution)/shard_map/ppermute | solution.py:658
  39.6 0.0 collective-permute-done.4.core_ref
  39.6 0.1 mul.67.unweight_ref
  39.7 11.9 %shard_map.82 = f32[2816,128]{1,0:T(8,128)S(1)} custom-call(f32[5]{0:T(128)S(1)} %stack.32.scales, f32[2]{0:T(128)S(1)} %add_convert_fusion.inside, s32[1]{0:T(128)} %bitcast.9.odd, bf16[528,192]{1,0:T(8,128)(2,1)S(1)} %pad_maximum_fusion.mix_ref, f32[7,8,640]{2,1,0:T(8,128)S(1)} %get-tuple-element.21.a_ref, f32[7,8,512]{2,1,0:T(8,128)S(1)} %get-tuple-element.22.b_ref, ...), custom_call_target="tpu_custom_call" | custom-call | flops 10000000000 | bytes 5451776 | tf_op jit(solution)/shard_map/pallas_call | solution.py:532
  51.6 39.5 %all_to_all.10.in_ref = f32[16,2,22,4,128]{4,3,2,1,0:T(4,128)S(1)} all-to-all(f32[16,2,22,4,128]{4,3,2,1,0:T(4,128)S(1)} %bitcast.65), channel_id=1, replica_groups=mesh['groups'=2,'chaos'=4,'space'=4] {'chaos','space'}, dimensions={0} | all-to-all | bytes 2883584 | tf_op jit(solution)/shard_map/all_to_all | solution.py:689
  91.1 1.4 %shard_map.83 = (f32[22,16,4,128]{3,2,1,0:T(4,128)}, f32[22,16,4,128]{3,2,1,0:T(4,128)}) custom-call(f32[16,2,22,4,128]{4,3,2,1,0:T(4,128)S(1)} %all_to_all.10.in_ref), custom_call_target="tpu_custom_call" | custom-call | bytes 2883584 | tf_op jit(solution)/shard_map/pallas_call | solution.py:532
  (10 shorter events, 0.1 us)
Async XLA Ops:
  0.6 9.7 %copy-start.3 = (f32[2]{0:T(128)S(1)}, f32[2]{0:T(128)}, u32[]{:S(2)}) copy-start(f32[2]{0:T(128)} %param.11) | copy-start | bytes 28
  0.6 12.8 %copy-start.4 = (s32[88]{0:T(128)S(1)}, s32[88]{0:T(128)}, u32[]{:S(2)}) copy-start(s32[88]{0:T(128)} %param.10) | copy-start | bytes 1060
  0.7 13.1 %copy-start.2 = (s32[6,28,3]{1,2,0:T(4,128)S(1)}, s32[6,28,3]{1,2,0:T(4,128)}, u32[]{:S(2)}) copy-start(s32[6,28,3]{1,2,0:T(4,128)} %param.9) | copy-start | bytes 6052
  2.8 12.2 %copy-start = (f32[6,2,4096]{2,1,0:T(2,128)S(1)}, f32[6,2,4096]{2,1,0:T(2,128)}, u32[]{:S(2)}) copy-start(f32[6,2,4096]{2,1,0:T(2,128)} %param.8) | copy-start | bytes 589828
  2.8 12.2 %copy-start.1 = (f32[2,4096]{1,0:T(2,128)S(1)}, f32[2,4096]{1,0:T(2,128)}, u32[]{:S(2)}) copy-start(f32[2,4096]{1,0:T(2,128)} %param.7) | copy-start | bytes 98308
  2.8 24.9 %all-to-all-start = ((f32[16,22,4,128]{3,2,1,0:T(4,128)}), f32[16,22,4,128]{3,2,1,0:T(4,128)S(1)}, u32[]{:S(2)}, u32[]{:S(2)}) async-start(f32[16,22,4,128]{3,2,1,0:T(4,128)} %shard_map.79), calls=%async_computation | async-start | bytes 1441792 | tf_op jit(solution)/shard_map/all_to_all | solution.py:613
  15.7 3.1 %collective-permute-start = (f32[84,128]{1,0:T(8,128)S(1)}, f32[84,128]{1,0:T(8,128)S(1)}, u32[]{:S(2)}, u32[]{:S(2)}) collective-permute-start(f32[84,128]{1,0:T(8,128)S(1)} %get-tuple-element.18), channel_id=1, source_target_pairs={{0,1},{1,2},{2,3},{3,0},{4,5},{5,6},{6,7},{7,4},{8,9},{9,10},{10,1... | collective-permute-start | bytes 129032 | tf_op jit(solution)/shard_map/ppermute | solution.py:636
  17.3 3.9 %collective-permute-start.1 = (f32[84,128]{1,0:T(8,128)S(1)}, f32[84,128]{1,0:T(8,128)S(1)}, u32[]{:S(2)}, u32[]{:S(2)}) collective-permute-start(f32[84,128]{1,0:T(8,128)S(1)} %get-tuple-element.19), channel_id=1, source_target_pairs={{0,2},{1,3},{2,0},{3,1},{4,6},{5,7},{6,4},{7,5},{8,10},{9,11},{10,... | collective-permute-start | bytes 129032 | tf_op jit(solution)/shard_map/ppermute | solution.py:636
  17.3 4.2 %collective-permute-start.2 = (f32[84,128]{1,0:T(8,128)S(1)}, f32[84,128]{1,0:T(8,128)S(1)}, u32[]{:S(2)}, u32[]{:S(2)}) collective-permute-start(f32[84,128]{1,0:T(8,128)S(1)} %get-tuple-element.20), channel_id=1, source_target_pairs={{0,3},{1,0},{2,1},{3,2},{4,7},{5,4},{6,5},{7,6},{8,11},{9,8},{10,9... | collective-permute-start | bytes 129032 | tf_op jit(solution)/shard_map/ppermute | solution.py:636
  28.8 10.9 %collective-permute-start.3 = (f32[1056,128]{1,0:T(8,128)}, f32[1056,128]{1,0:T(8,128)S(1)}, u32[]{:S(2)}, u32[]{:S(2)}) collective-permute-start(f32[1056,128]{1,0:T(8,128)} %get-tuple-element.28), channel_id=1, source_target_pairs={{1,2},{3,7},{6,5},{4,8},{9,10},{11,15},{14,13},{2,1},{7,3},{5,6},{... | collective-permute-start | bytes 1622024 | tf_op jit(solution)/shard_map/ppermute | solution.py:658
  31.7 7.9 %collective-permute-start.4 = (f32[1056,128]{1,0:T(8,128)S(1)}, f32[1056,128]{1,0:T(8,128)S(1)}, u32[]{:S(2)}, u32[]{:S(2)}) collective-permute-start(f32[1056,128]{1,0:T(8,128)S(1)} %get-tuple-element.29), channel_id=1, source_target_pairs={{0,1},{2,3},{7,6},{5,4},{8,9},{10,11},{15,14},{13,12},{1,0},{3,2},... | collective-permute-start | bytes 1622024 | tf_op jit(solution)/shard_map/ppermute | solution.py:658

commit v7 on v6

--- a/solution.py
+++ b/solution.py
@@ -145,12 +145,17 @@
     return sums
 
 
-def neighbour_sums(read, layer, layers, count, masks, first=0):
+def neighbour_sums(read, layer, count, masks, first=0):
     sums = plane_sums([read(layer, t) for t in range(count)], masks, first)
-    for other in (layer - 1, layer + 1):
-        if 0 <= other < layers:
-            sums = [total + read(other, first + n) for n, total in enumerate(sums)]
-    return sums
+    return [
+        total + (read(layer - 1, first + n) + read(layer + 1, first + n))
+        for n, total in enumerate(sums)
+    ]
+
+
+def clear_ends(ref):
+    for end in (0, ref.shape[0] - 1):
+        ref[end] = jnp.zeros(ref.shape[1:], jnp.float32)
 
 
 def split_stack(tiles, depth):
@@ -219,8 +224,13 @@
 
 def coefficient_kernel(thick, sources, *refs):
     *ins, a_ref, b_ref, own_b_ref, face_ref, held_ref = refs
-    modes, layers, _ = a_ref.shape
-    tiles = held_ref.shape[1]
+    modes, tiles, layers, _ = held_ref.shape
+
+    def put(ref, k, t, value):
+        row = k * (ref.shape[1] // modes) + t
+        for l in range(layers):
+            ref[l, row : row + 1, :] = value[l : l + 1]
+
     layer = lax.broadcasted_iota(jnp.int32, (layers, LANES), 0)
     masks = lane_masks(layers)
     low_half = masks[0]
@@ -246,15 +256,15 @@
             values = [m * value for m, value in zip(mean, values)]
         sums = plane_sums(values, masks)
         for t in range(FOLDED):
-            a_ref[k, :, lanes(t)] = values[t]
+            put(a_ref, k, t, values[t])
         for t in range(FOLDED - 1):
-            b_ref[k, :, lanes(t)] = 6.0 * values[t] + (sums[t] + layer_sum(values[t], layer))
+            put(b_ref, k, t, 6.0 * values[t] + (sums[t] + layer_sum(values[t], layer)))
         outside = jnp.zeros((layers, LANES), jnp.float32)
         sums = plane_sums(values[:OWN_TILES] + [outside], masks)
         for t in range(OWN_TILES):
-            own_b_ref[k, :, lanes(t)] = 6.0 * values[t] + (sums[t] + layer_sum(values[t], layer))
-        face_ref[k, :, lanes(0)] = jnp.where(low_half, values[0], values[1])
-        face_ref[k, :, lanes(1)] = pltpu.roll(values[2], NY, 1)
+            put(own_b_ref, k, t, 6.0 * values[t] + (sums[t] + layer_sum(values[t], layer)))
+        put(face_ref, k, 0, jnp.where(low_half, values[0], values[1]))
+        put(face_ref, k, 1, pltpu.roll(values[2], NY, 1))
 
 
 def collect_kernel(blocks, in_ref, *rest):
@@ -281,12 +291,14 @@
 def start_kernel(chaos, spaces, odd, a_ref, weight_ref, in_ref, residual_ref, chip_ref, core_ref):
     upward = odd[0] > 0
     layers, tiles, slots, _ = residual_ref.shape
+    layers -= 2
     own = slots // chaos
     thick = layers // spaces
     pieces = tiles * thick
     half = layers // 2
     low_half = lane_masks(slots)[0]
     weight = weight_ref[...]
+    clear_ends(residual_ref)
 
     def put(place, up, down):
         rows = pl.ds(place * slots, slots)
@@ -307,15 +319,20 @@
                 ]
                 for c, slot, number, _ in slot_parts(own, chaos)
             ]
-            residual_ref[l, t] = weight * jnp.concatenate(rows, axis=0)
-        put(l, residual_ref[l, 1], residual_ref[l, 0])
+            residual_ref[l + 1, t] = weight * jnp.concatenate(rows, axis=0)
+        put(l, residual_ref[l + 1, 1], residual_ref[l + 1, 0])
     for l in range(half):
-        later = l + half
+        first, later = residual_ref.at[l + 1], residual_ref.at[l + 1 + half]
         put(
             layers + l,
-            jnp.where(low_half, pltpu.roll(residual_ref[later, 0], NY, 1), residual_ref[l, 0]),
-            jnp.where(low_half, residual_ref[l, 1], pltpu.roll(residual_ref[later, 1], NY, 1)),
+            jnp.where(low_half, pltpu.roll(later[0], NY, 1), first[0]),
+            jnp.where(low_half, first[1], pltpu.roll(later[1], NY, 1)),
         )
+
+
+def coefficient(ref, modes, l, k, t):
+    row = k * (ref.shape[1] // modes) + t
+    return ref[l, row : row + 1, :]
 
 
 def mode_part(mixed, modes, k, n):
@@ -347,20 +364,22 @@
 
 
 def own_kernel(scales, mix_ref, a_ref, b_ref, start_ref, total_ref, edge_ref):
-    layers, tiles, slots, _ = start_ref.shape
-    modes = a_ref.shape[0]
+    layers, tiles, slots, _ = total_ref.shape
+    modes = b_ref.shape[1] // tiles
     masks = lane_masks(slots)
-    mix = mix_ref[...]
     nothing = jnp.zeros((slots, LANES), jnp.float32)
+    clear_ends(edge_ref)
 
     def read(l, t):
-        return start_ref[l, t] * scales[0] if t < tiles else nothing
-
-    for l in range(layers):
+        return start_ref[l + 1, t] * scales[0] if t < tiles else nothing
+
+    def body(l, carry):
         direct = [read(l, t) for t in range(tiles)]
-        around = neighbour_sums(read, l, layers, tiles + 1, masks)
+        around = neighbour_sums(read, l, tiles + 1, masks)
         mixed = jnp.dot(
-            mix, split_stack(direct + around, mix.shape[1]), preferred_element_type=jnp.float32
+            mix_ref[...],
+            split_stack(direct + around, mix_ref.shape[1]),
+            preferred_element_type=jnp.float32,
         )
         results = weighted_tiles(
             mixed,
@@ -369,12 +388,15 @@
             tiles,
             direct,
             around,
-            lambda k, t: a_ref[k, l : l + 1, lanes(t)],
-            lambda k, t: b_ref[k, l : l + 1, lanes(t)],
+            lambda k, t: coefficient(a_ref, modes, l, k, t),
+            lambda k, t: coefficient(b_ref, modes, l, k, t),
         )
         for t, (total, edge) in enumerate(results):
             total_ref[l, t] = total
-            edge_ref[l, t] = edge
+            edge_ref[l + 1, t] = edge
+        return carry
+
+    lax.fori_loop(0, layers, body, 0)
 
 
 def iterate_kernel(
@@ -400,24 +422,24 @@
     edge_ref,
     x_ref,
 ):
-    layers, _, slots, _ = start_ref.shape
-    modes = a_ref.shape[0]
+    layers, _, slots, _ = own_total_ref.shape
+    modes = a_ref.shape[1] // FOLDED
     own = slots // chaos
     thick = layers // spaces
     pieces = OWN_TILES * thick
     half = layers // 2
     masks = lane_masks(slots)
     low_half = masks[0]
-    mix = mix_ref[...]
-    depth = mix.shape[1]
     upward = odd[0] > 0
+    clear_ends(d_ref)
+    clear_ends(edge_ref)
 
     def message(start, size):
         chip, core = chip_ref[pl.ds(start, size), :], core_ref[pl.ds(start, size), :]
         return jnp.where(upward, core, chip), jnp.where(upward, chip, core)
 
     def send(field, l, t, value):
-        i, z = divmod(l, thick)
+        i, z = lax.div(l, thick), lax.rem(l, thick)
         value = value * unweight_ref[...]
         for c, slot, number, row in slot_parts(own, chaos):
             first = (((c * spaces + i) * 2 + field) * own + slot) * pieces + t * thick + z
@@ -431,8 +453,8 @@
         else:
             far = pltpu.roll(jnp.where(low_half, far_below, far_above), NY, 1)
         tiles = [
-            start_ref[l, 0],
-            start_ref[l, 1],
+            start_ref[l + 1, 0],
+            start_ref[l + 1, 1],
             jnp.where(low_half, above, below),
             jnp.where(low_half, below, above),
             far,
@@ -440,64 +462,57 @@
         for t, tile in enumerate(tiles):
             if t < FOLDED - 1:
                 r_ref[l, t] = tile
-            d_ref[l, t] = tile * scales[0]
+            d_ref[l + 1, t] = tile * scales[0]
 
     def read(l, t):
-        return d_ref[l, t]
+        return d_ref[l + 1, t]
 
     zero = jnp.zeros((slots, LANES), jnp.float32)
     for step in range(ITERS):
         count = FOLDED - step
         full = count - 1
         first = OWN_TILES if step == 0 else 0
-        group = 1
-        for lowest in range(0, layers, group):
-            gathered, stacked = [], []
-            for l in range(lowest, lowest + group):
-                direct = [d_ref[l, t] for t in range(first, count)]
-                around = neighbour_sums(read, l, layers, count, masks, first)
-                extra = []
-                if step == 0:
-                    extra = [jnp.where(low_half, d_ref[l, 0], d_ref[l, 1])]
-                gathered.append((l, len(stacked), direct, extra, around))
-                stacked += direct + extra + around
+
+        def sums(l, carry):
+            direct = [read(l, t) for t in range(first, count)]
+            around = neighbour_sums(read, l, count, masks, first)
+            extra = [jnp.where(low_half, read(l, 0), read(l, 1))] if step == 0 else []
             mixed = jnp.dot(
-                mix, split_stack(stacked, depth), preferred_element_type=jnp.float32
+                mix_ref[...],
+                split_stack(direct + extra + around, mix_ref.shape[1]),
+                preferred_element_type=jnp.float32,
             )
-            for l, place, direct, extra, around in gathered:
-                results = weighted_tiles(
-                    mixed,
-                    modes,
-                    place,
-                    place + len(direct) + len(extra),
-                    direct,
-                    around,
-                    lambda k, t: a_ref[k, l : l + 1, lanes(first + t)],
-                    lambda k, t: b_ref[k, l : l + 1, lanes(first + t)],
-                )
-                for t, (total, edge) in enumerate(results):
-                    edge_ref[l, first + t] = edge
-                    if first + t < full:
-                        total_ref[l, first + t] = total
-                if not extra:
-                    continue
-                own_face = face_ref[0, l : l + 1, lanes(0)]
-                other_face = face_ref[0, l : l + 1, lanes(1)]
+            results = weighted_tiles(
+                mixed,
+                modes,
+                0,
+                len(direct) + len(extra),
+                direct,
+                around,
+                lambda k, t: coefficient(a_ref, modes, l, k, first + t),
+                lambda k, t: coefficient(b_ref, modes, l, k, first + t),
+            )
+            for t, (total, edge) in enumerate(results):
+                edge_ref[l + 1, first + t] = edge
+                if first + t < full:
+                    total_ref[l, first + t] = total
+            if step == 0:
+                own_face, other_face = [coefficient(face_ref, modes, l, 0, n) for n in range(2)]
                 part = other_face * extra[0] - own_face * pltpu.roll(direct[0], NY, 1)
                 for k in range(1, modes):
-                    own_face = face_ref[k, l : l + 1, lanes(0)]
-                    other_face = face_ref[k, l : l + 1, lanes(1)]
-                    own_mixed = mode_part(mixed, modes, k, place + len(direct))
-                    other_mixed = pltpu.roll(mode_part(mixed, modes, k, place), NY, 1)
+                    own_face, other_face = [coefficient(face_ref, modes, l, k, n) for n in range(2)]
+                    own_mixed = mode_part(mixed, modes, k, len(direct))
+                    other_mixed = pltpu.roll(mode_part(mixed, modes, k, 0), NY, 1)
                     part = part + (other_face * own_mixed - own_face * other_mixed)
                 total_ref[l, 0] = own_total_ref[l, 0] + jnp.where(low_half, part, zero)
                 total_ref[l, 1] = own_total_ref[l, 1] + jnp.where(low_half, zero, part)
+            return carry
 
         def read_edge(l, t):
-            return own_edge_ref[l, t] if t < first else edge_ref[l, t]
-
-        for l in range(layers):
-            spread = neighbour_sums(read_edge, l, layers, count, masks)
+            return (own_edge_ref if t < first else edge_ref)[l + 1, t]
+
+        def update(l, carry):
+            spread = neighbour_sums(read_edge, l, count, masks)
             for t in range(full):
                 diffused = total_ref[l, t] - spread[t]
                 if t >= OWN_TILES:
@@ -508,15 +523,19 @@
                     send(1, l, t, residual)
                     continue
                 r_ref[l, t] = residual
-                old = d_ref[l, t]
+                old = read(l, t)
                 direction = scales[1 + 2 * step] * old + scales[2 + 2 * step] * residual
-                d_ref[l, t] = direction
+                d_ref[l + 1, t] = direction
                 if t < OWN_TILES:
                     value = (old if step == 0 else x_ref[l, t]) + direction
                     if step == ITERS - 2:
                         send(0, l, t, value)
                     else:
                         x_ref[l, t] = value
+            return carry
+
+        lax.fori_loop(0, layers, sums, 0)
+        lax.fori_loop(0, layers, update, 0)
 
 
 def call(kernel, outs, scalars, arrays, scratch=(), flops=0, in_kinds=None, out_kind=pltpu.VMEM):
@@ -638,7 +657,7 @@
     ]
     a, b, own_b, face = call(
         functools.partial(coefficient_kernel, thick),
-        [shape(modes, layers, tiles * LANES) for tiles in (FOLDED, FOLDED - 1, OWN_TILES, 2)],
+        [shape(layers, modes * tiles, LANES) for tiles in (FOLDED, FOLDED - 1, OWN_TILES, 2)],
         [(column - steps) % spaces],
         picked,
         [pltpu.VMEM((modes, 3 * OWN_TILES, layers, LANES), f32)],
@@ -647,7 +666,7 @@
     message = shape((layers + layers // 2) * slots, LANES)
     start, to_chip, to_core = call(
         functools.partial(start_kernel, chaos, spaces),
-        [shape(layers, OWN_TILES, slots, LANES), message, message],
+        [shape(layers + 2, OWN_TILES, slots, LANES), message, message],
         [odd],
         [a, weight, gathered],
     )
@@ -659,17 +678,16 @@
 
     from_chip = swap(to_chip, 1)
     from_core = swap(to_core, 0)
-    own_field = shape(layers, OWN_TILES, slots, LANES)
     own_total, own_edge = call(
         own_kernel,
-        [own_field, own_field],
+        [shape(n, OWN_TILES, slots, LANES) for n in (layers, layers + 2)],
         [scales],
         [mix, a, own_b, start],
         flops=3000000000,
     )
 
-    def held(tiles):
-        return pltpu.VMEM((layers, tiles, slots, LANES), f32)
+    def held(tiles, depth=layers):
+        return pltpu.VMEM((depth, tiles, slots, LANES), f32)
 
     sent = call(
         functools.partial(iterate_kernel, chaos, spaces),
@@ -678,9 +696,9 @@
         [mix, a, b, face, unweight, start, own_total, own_edge, from_chip, from_core],
         [
             held(FOLDED - 1),
-            held(FOLDED),
+            held(FOLDED, layers + 2),
             held(FOLDED - 1),
-            held(FOLDED),
+            held(FOLDED, layers + 2),
             held(OWN_TILES),
         ],
         flops=10000000000,

time: 92.9 us -> 98.7 us (1.062)
  Pallas kernels: 20 us -> 27.5 us
  waiting for transfers between devices: 14.3 us -> 10.9 us
  local copies, waits for them, and re-layouts: 1.12 us -> 2.69 us
    pallas_call x7, Pallas kernels: 20 us -> 27.5 us  [call(): pl.pallas_call(kernel, out_shape=outs, in_specs=in_specs, out_specs=[pl.B...]
    ppermute x2, waiting for transfers between devices: 5.46 us -> 3.14 us  [swap(): return lax.ppermute(field, BOTH, pairs + [(b, a) for a, b in pairs])]
    unnamed x10 -> x14, local copies, waits for them, and re-layouts: 0.03 us -> 1.49 us
    all_to_all x1, waiting for transfers between devices: 5.42 us -> 4.23 us  [local_by_cells(): lax.all_to_all(scattered, BOTH, 0, 0, tiled=True).reshape(-1, LANES)]
  transfers between devices with their start and end apart: 6 -> 6, of which waited for: 5 -> 5; matrix products, arithmetic and copies ran while one was open for 2% -> 2% of each run, Pallas kernels for 4% -> 5%
where the time goes in v7:
time: 98.7 us; the launch traced here: 98.3 us
  blocking collectives  39.5 us (40%)
  Pallas kernels  27.5 us (28%)
  starting transfers between devices  12.5 us (13%)
  waiting for transfers between devices  10.9 us (11%)
  between operations  3.85 us (4%)
  local copies, waits for them, and re-layouts  2.69 us (3%)
    all_to_all x1, blocking collectives, local_by_cells(): received = lax.all_to_all(sent, BOTH, 0, 0, tiled=True)  39.5 us
    pallas_call x7, Pallas kernels, call(): pl.pallas_call(kernel, out_shape=outs, in_specs=in_specs, out_specs=[pl.B...  27.5 us
    all_to_all x1, starting transfers between devices, local_by_cells(): lax.all_to_all(scattered, BOTH, 0, 0, tiled=True).reshape(-1, LANES)  7.47 us
    all_to_all x1, waiting for transfers between devices, local_by_cells(): lax.all_to_all(scattered, BOTH, 0, 0, tiled=True).reshape(-1, LANES)  4.23 us
    ppermute x3, waiting for transfers between devices, local_by_cells(): lax.ppermute(picked[n], 'space', [(i, (i + n) % spaces) for i in range(sp...  3.55 us
    ppermute x2, waiting for transfers between devices, swap(): return lax.ppermute(field, BOTH, pairs + [(b, a) for a, b in pairs])  3.14 us
    ppermute x2, starting transfers between devices, swap(): return lax.ppermute(field, BOTH, pairs + [(b, a) for a, b in pairs])  2.84 us
    ppermute x3, starting transfers between devices, local_by_cells(): lax.ppermute(picked[n], 'space', [(i, (i + n) % spaces) for i in range(sp...  2.23 us
  transfers between devices with their start and end apart: 6, of which 5 were waited for; matrix products, arithmetic and copies ran while one was open for 2% of the time, Pallas kernels for 5%

profile of v7, /device:TPU:1, one launch (start us, length us, event | category | flops | bytes accessed | tf_op | source)
XLA Modules:
  0.0 98.3 jit_solution(17827356697688352857)
XLA Ops:
  0.6 0.0 copy-start.5
  0.6 0.0 copy-start.6
  0.7 0.0 copy-start.4
  0.7 2.1 %shard_map.79 = f32[16,22,4,128]{3,2,1,0:T(4,128)} custom-call(f32[22,16,4,128]{3,2,1,0:T(4,128)} %bitcast.68), custom_call_target="tpu_custom_call" | custom-call | bytes 1441792 | tf_op jit(solution)/shard_map/pallas_call | solution.py:551
  2.8 0.0 copy-start
  2.8 0.0 copy-start.1
  2.8 7.5 %all-to-all-start = ((f32[16,22,4,128]{3,2,1,0:T(4,128)}), f32[16,22,4,128]{3,2,1,0:T(4,128)S(1)}, u32[]{:S(2)}, u32[]{:S(2)}) async-start(f32[16,22,4,128]{3,2,1,0:T(4,128)} %shard_map.79), calls=%async_computation | async-start | bytes 1441792 | tf_op jit(solution)/shard_map/all_to_all | solution.py:632
  10.3 0.0 copy-done.5
  10.3 0.7 fusion.19
  13.8 0.0 copy-done.6
  13.8 0.1 reshape.177
  13.9 0.1 slice_bitcast_fusion
  14.1 0.0 copy-done.4
  14.1 0.1 concatenate.13
  14.2 0.4 fusion.2
  14.7 0.4 fusion
  15.2 0.1 stack.32.scales
  15.3 0.1 pad_maximum_fusion.mix_ref
  15.4 0.0 copy-done
  15.4 0.0 copy-done.1
  15.4 0.6 shard_map.77
  16.0 1.7 %collective-permute-start = (f32[84,128]{1,0:T(8,128)S(1)}, f32[84,128]{1,0:T(8,128)S(1)}, u32[]{:S(2)}, u32[]{:S(2)}) collective-permute-start(f32[84,128]{1,0:T(8,128)S(1)} %get-tuple-element.18), channel_id=1, source_target_pairs={{0,1},{1,2},{2,3},{3,0},{4,5},{5,6},{6,7},{7,4},{8,9},{9,10},{10,1... | collective-permute-start | bytes 129032 | tf_op jit(solution)/shard_map/ppermute | solution.py:655
  17.7 0.0 collective-permute-start.1
  17.7 0.5 collective-permute-start.2
  18.3 0.1 convert_reduce_fusion
  18.5 1.3 %collective-permute-done.refs_1_ = f32[84,128]{1,0:T(8,128)S(1)} collective-permute-done((f32[84,128]{1,0:T(8,128)S(1)}, f32[84,128]{1,0:T(8,128)S(1)}, u32[]{:S(2)}, u32[]{:S(2)}) %collective-permute-start) | collective-permute-done | bytes 43040 | tf_op jit(solution)/shard_map/ppermute | solution.py:655
  19.7 1.9 %collective-permute-done.1.refs_2_ = f32[84,128]{1,0:T(8,128)S(1)} collective-permute-done((f32[84,128]{1,0:T(8,128)S(1)}, f32[84,128]{1,0:T(8,128)S(1)}, u32[]{:S(2)}, u32[]{:S(2)}) %collective-permute-start.1) | collective-permute-done | bytes 43040 | tf_op jit(solution)/shard_map/ppermute | solution.py:655
  21.6 0.4 collective-permute-done.2.refs_3_
  22.0 0.8 shard_map.78
  22.8 0.0 copy-start.2
  22.8 0.6 copy-done.2
  23.5 4.2 %all-to-all-done = f32[16,22,4,128]{3,2,1,0:T(4,128)S(1)} async-done(((f32[16,22,4,128]{3,2,1,0:T(4,128)}), f32[16,22,4,128]{3,2,1,0:T(4,128)S(1)}, u32[]{:S(2)}, u32[]{:S(2)}) %all-to-all-start) | async-done | bytes 720928 | tf_op jit(solution)/shard_map/all_to_all | solution.py:632
  27.7 0.1 mul.69.weight_ref
  27.8 1.0 %shard_map.80 = (f32[10,2,88,128]{3,2,1,0:T(8,128)S(1)}, f32[1056,128]{1,0:T(8,128)}, f32[1056,128]{1,0:T(8,128)S(1)}) custom-call(s32[1]{0:T(128)} %bitcast.9.odd, f32[8,35,128]{2,1,0:T(8,128)S(1)} %get-tuple-element.21.a_ref, f32[88,128]{1,0:T(8,128)S(1)} %mul.69.weight_ref, f32[1408,128]{1,0:T(8,128)S(1)} %bitcast.64), custom_call_target="tpu_custom_call" | custom-call | bytes 2891776 | tf_op jit(solution)/shard_map/pallas_call | solution.py:551
  28.8 2.8 %collective-permute-start.3 = (f32[1056,128]{1,0:T(8,128)}, f32[1056,128]{1,0:T(8,128)S(1)}, u32[]{:S(2)}, u32[]{:S(2)}) collective-permute-start(f32[1056,128]{1,0:T(8,128)} %get-tuple-element.28), channel_id=1, source_target_pairs={{1,2},{3,7},{6,5},{4,8},{9,10},{11,15},{14,13},{2,1},{7,3},{5,6},{... | collective-permute-start | bytes 1622024 | tf_op jit(solution)/shard_map/ppermute | solution.py:677
  31.5 0.1 collective-permute-start.4
  31.6 0.1 add_convert_fusion.inside
  31.7 0.0 copy-start.3
  31.7 0.8 copy-done.3
  32.5 4.0 %shard_map.81 = (f32[8,2,88,128]{3,2,1,0:T(8,128)S(1)}, f32[10,2,88,128]{3,2,1,0:T(8,128)S(1)}) custom-call(f32[5]{0:T(128)S(1)} %stack.32.scales, bf16[528,192]{1,0:T(8,128)(2,1)S(1)} %pad_maximum_fusion.mix_ref, f32[8,35,128]{2,1,0:T(8,128)S(1)} %get-tuple-element.21.a_ref, f32[8,14,128]{2,1,0:T(8,128)S(1)} %copy-done.3, ...), custom_call_target="tpu_custom_call" | custom-call | flops 3000000000 | bytes 3129344 | tf_op jit(solution)/shard_map/pallas_call | solution.py:551
  36.5 3.1 %collective-permute-done.3.chip_ref = f32[1056,128]{1,0:T(8,128)S(1)} collective-permute-done((f32[1056,128]{1,0:T(8,128)}, f32[1056,128]{1,0:T(8,128)S(1)}, u32[]{:S(2)}, u32[]{:S(2)}) %collective-permute-start.3) | collective-permute-done | bytes 540704 | tf_op jit(solution)/shard_map/ppermute | solution.py:677
  39.6 0.0 collective-permute-done.4.core_ref
  39.6 0.1 mul.67.unweight_ref
  39.7 17.7 %shard_map.82 = f32[2816,128]{1,0:T(8,128)S(1)} custom-call(f32[5]{0:T(128)S(1)} %stack.32.scales, f32[2]{0:T(128)S(1)} %add_convert_fusion.inside, s32[1]{0:T(128)} %bitcast.9.odd, bf16[528,192]{1,0:T(8,128)(2,1)S(1)} %pad_maximum_fusion.mix_ref, f32[8,35,128]{2,1,0:T(8,128)S(1)} %get-tuple-element.21.a_ref, f32[8,28,128]{2,1,0:T(8,128)S(1)} %get-tuple-element.22.b_ref, ...), custom_call_target="tpu_custom_call" | custom-call | flops 10000000000 | bytes 5812224 | tf_op jit(solution)/shard_map/pallas_call | solution.py:551
  57.4 39.5 %all_to_all.10.in_ref = f32[16,2,22,4,128]{4,3,2,1,0:T(4,128)S(1)} all-to-all(f32[16,2,22,4,128]{4,3,2,1,0:T(4,128)S(1)} %bitcast.65), channel_id=1, replica_groups=mesh['groups'=2,'chaos'=4,'space'=4] {'chaos','space'}, dimensions={0} | all-to-all | bytes 2883584 | tf_op jit(solution)/shard_map/all_to_all | solution.py:707
  96.9 1.4 %shard_map.83 = (f32[22,16,4,128]{3,2,1,0:T(4,128)}, f32[22,16,4,128]{3,2,1,0:T(4,128)}) custom-call(f32[16,2,22,4,128]{4,3,2,1,0:T(4,128)S(1)} %all_to_all.10.in_ref), custom_call_target="tpu_custom_call" | custom-call | bytes 2883584 | tf_op jit(solution)/shard_map/pallas_call | solution.py:551
  (10 shorter events, 0.1 us)
Async XLA Ops:
  0.6 9.7 %copy-start.5 = (f32[2]{0:T(128)S(1)}, f32[2]{0:T(128)}, u32[]{:S(2)}) copy-start(f32[2]{0:T(128)} %param.11) | copy-start | bytes 28
  0.6 13.2 %copy-start.6 = (s32[88]{0:T(128)S(1)}, s32[88]{0:T(128)}, u32[]{:S(2)}) copy-start(s32[88]{0:T(128)} %param.10) | copy-start | bytes 1060
  0.7 13.5 %copy-start.4 = (s32[6,28,3]{1,2,0:T(4,128)S(1)}, s32[6,28,3]{1,2,0:T(4,128)}, u32[]{:S(2)}) copy-start(s32[6,28,3]{1,2,0:T(4,128)} %param.9) | copy-start | bytes 6052
  2.8 12.6 %copy-start = (f32[6,2,4096]{2,1,0:T(2,128)S(1)}, f32[6,2,4096]{2,1,0:T(2,128)}, u32[]{:S(2)}) copy-start(f32[6,2,4096]{2,1,0:T(2,128)} %param.8) | copy-start | bytes 589828
  2.8 12.6 %copy-start.1 = (f32[2,4096]{1,0:T(2,128)S(1)}, f32[2,4096]{1,0:T(2,128)}, u32[]{:S(2)}) copy-start(f32[2,4096]{1,0:T(2,128)} %param.7) | copy-start | bytes 98308
  2.8 24.9 %all-to-all-start = ((f32[16,22,4,128]{3,2,1,0:T(4,128)}), f32[16,22,4,128]{3,2,1,0:T(4,128)S(1)}, u32[]{:S(2)}, u32[]{:S(2)}) async-start(f32[16,22,4,128]{3,2,1,0:T(4,128)} %shard_map.79), calls=%async_computation | async-start | bytes 1441792 | tf_op jit(solution)/shard_map/all_to_all | solution.py:632
  16.0 3.7 %collective-permute-start = (f32[84,128]{1,0:T(8,128)S(1)}, f32[84,128]{1,0:T(8,128)S(1)}, u32[]{:S(2)}, u32[]{:S(2)}) collective-permute-start(f32[84,128]{1,0:T(8,128)S(1)} %get-tuple-element.18), channel_id=1, source_target_pairs={{0,1},{1,2},{2,3},{3,0},{4,5},{5,6},{6,7},{7,4},{8,9},{9,10},{10,1... | collective-permute-start | bytes 129032 | tf_op jit(solution)/shard_map/ppermute | solution.py:655
  17.7 3.9 %collective-permute-start.1 = (f32[84,128]{1,0:T(8,128)S(1)}, f32[84,128]{1,0:T(8,128)S(1)}, u32[]{:S(2)}, u32[]{:S(2)}) collective-permute-start(f32[84,128]{1,0:T(8,128)S(1)} %get-tuple-element.19), channel_id=1, source_target_pairs={{0,2},{1,3},{2,0},{3,1},{4,6},{5,7},{6,4},{7,5},{8,10},{9,11},{10,... | collective-permute-start | bytes 129032 | tf_op jit(solution)/shard_map/ppermute | solution.py:655
  17.7 4.3 %collective-permute-start.2 = (f32[84,128]{1,0:T(8,128)S(1)}, f32[84,128]{1,0:T(8,128)S(1)}, u32[]{:S(2)}, u32[]{:S(2)}) collective-permute-start(f32[84,128]{1,0:T(8,128)S(1)} %get-tuple-element.20), channel_id=1, source_target_pairs={{0,3},{1,0},{2,1},{3,2},{4,7},{5,4},{6,5},{7,6},{8,11},{9,8},{10,9... | collective-permute-start | bytes 129032 | tf_op jit(solution)/shard_map/ppermute | solution.py:655
  22.8 0.6 copy-start.2
  28.8 10.9 %collective-permute-start.3 = (f32[1056,128]{1,0:T(8,128)}, f32[1056,128]{1,0:T(8,128)S(1)}, u32[]{:S(2)}, u32[]{:S(2)}) collective-permute-start(f32[1056,128]{1,0:T(8,128)} %get-tuple-element.28), channel_id=1, source_target_pairs={{1,2},{3,7},{6,5},{4,8},{9,10},{11,15},{14,13},{2,1},{7,3},{5,6},{... | collective-permute-start | bytes 1622024 | tf_op jit(solution)/shard_map/ppermute | solution.py:677
  31.5 8.1 %collective-permute-start.4 = (f32[1056,128]{1,0:T(8,128)S(1)}, f32[1056,128]{1,0:T(8,128)S(1)}, u32[]{:S(2)}, u32[]{:S(2)}) collective-permute-start(f32[1056,128]{1,0:T(8,128)S(1)} %get-tuple-element.29), channel_id=1, source_target_pairs={{0,1},{2,3},{7,6},{5,4},{8,9},{10,11},{15,14},{13,12},{1,0},{3,2},... | collective-permute-start | bytes 1622024 | tf_op jit(solution)/shard_map/ppermute | solution.py:677
  31.7 0.8 copy-start.3

commit v8 on v6

--- a/solution.py
+++ b/solution.py
@@ -356,12 +356,19 @@
     def read(l, t):
         return start_ref[l, t] * scales[0] if t < tiles else nothing
 
-    for l in range(layers):
+    def prepare(l):
         direct = [read(l, t) for t in range(tiles)]
         around = neighbour_sums(read, l, layers, tiles + 1, masks)
         mixed = jnp.dot(
             mix, split_stack(direct + around, mix.shape[1]), preferred_element_type=jnp.float32
         )
+        return mixed, direct, around
+
+    ahead = prepare(0)
+    for l in range(layers):
+        mixed, direct, around = ahead
+        if l + 1 < layers:
+            ahead = prepare(l + 1)
         results = weighted_tiles(
             mixed,
             modes,
@@ -423,7 +430,7 @@
             first = (((c * spaces + i) * 2 + field) * own + slot) * pieces + t * thick + z
             sent_ref[pl.ds(first, number, stride=pieces), :] = value[row : row + number]
 
-    for l in range(layers):
+    def fold(l):
         below, above = message(l * slots, slots)
         far_below, far_above = message((layers + l % half) * slots, slots)
         if l < half:
@@ -446,77 +453,85 @@
         return d_ref[l, t]
 
     zero = jnp.zeros((slots, LANES), jnp.float32)
-    for step in range(ITERS):
+    prepared = {}
+
+    def prepare(step, l):
         count = FOLDED - step
-        full = count - 1
         first = OWN_TILES if step == 0 else 0
-        group = 1
-        for lowest in range(0, layers, group):
-            gathered, stacked = [], []
-            for l in range(lowest, lowest + group):
-                direct = [d_ref[l, t] for t in range(first, count)]
-                around = neighbour_sums(read, l, layers, count, masks, first)
-                extra = []
-                if step == 0:
-                    extra = [jnp.where(low_half, d_ref[l, 0], d_ref[l, 1])]
-                gathered.append((l, len(stacked), direct, extra, around))
-                stacked += direct + extra + around
-            mixed = jnp.dot(
-                mix, split_stack(stacked, depth), preferred_element_type=jnp.float32
-            )
-            for l, place, direct, extra, around in gathered:
-                results = weighted_tiles(
-                    mixed,
-                    modes,
-                    place,
-                    place + len(direct) + len(extra),
-                    direct,
-                    around,
-                    lambda k, t: a_ref[k, l : l + 1, lanes(first + t)],
-                    lambda k, t: b_ref[k, l : l + 1, lanes(first + t)],
-                )
-                for t, (total, edge) in enumerate(results):
-                    edge_ref[l, first + t] = edge
-                    if first + t < full:
-                        total_ref[l, first + t] = total
-                if not extra:
-                    continue
-                own_face = face_ref[0, l : l + 1, lanes(0)]
-                other_face = face_ref[0, l : l + 1, lanes(1)]
-                part = other_face * extra[0] - own_face * pltpu.roll(direct[0], NY, 1)
-                for k in range(1, modes):
-                    own_face = face_ref[k, l : l + 1, lanes(0)]
-                    other_face = face_ref[k, l : l + 1, lanes(1)]
-                    own_mixed = mode_part(mixed, modes, k, place + len(direct))
-                    other_mixed = pltpu.roll(mode_part(mixed, modes, k, place), NY, 1)
-                    part = part + (other_face * own_mixed - own_face * other_mixed)
-                total_ref[l, 0] = own_total_ref[l, 0] + jnp.where(low_half, part, zero)
-                total_ref[l, 1] = own_total_ref[l, 1] + jnp.where(low_half, zero, part)
+        direct = [d_ref[l, t] for t in range(first, count)]
+        around = neighbour_sums(read, l, layers, count, masks, first)
+        extra = [jnp.where(low_half, d_ref[l, 0], d_ref[l, 1])] if step == 0 else []
+        mixed = jnp.dot(
+            mix, split_stack(direct + extra + around, depth), preferred_element_type=jnp.float32
+        )
+        prepared[step, l] = (mixed, direct, extra, around)
+
+    def combine(step, l):
+        first = OWN_TILES if step == 0 else 0
+        mixed, direct, extra, around = prepared.pop((step, l))
+        results = weighted_tiles(
+            mixed,
+            modes,
+            0,
+            len(direct) + len(extra),
+            direct,
+            around,
+            lambda k, t: a_ref[k, l : l + 1, lanes(first + t)],
+            lambda k, t: b_ref[k, l : l + 1, lanes(first + t)],
+        )
+        for t, (total, edge) in enumerate(results):
+            edge_ref[l, first + t] = edge
+            if total is not None:
+                total_ref[l, first + t] = total
+        if step > 0:
+            return
+        own_face = face_ref[0, l : l + 1, lanes(0)]
+        other_face = face_ref[0, l : l + 1, lanes(1)]
+        part = other_face * extra[0] - own_face * pltpu.roll(direct[0], NY, 1)
+        for k in range(1, modes):
+            own_face = face_ref[k, l : l + 1, lanes(0)]
+            other_face = face_ref[k, l : l + 1, lanes(1)]
+            own_mixed = mode_part(mixed, modes, k, len(direct))
+            other_mixed = pltpu.roll(mode_part(mixed, modes, k, 0), NY, 1)
+            part = part + (other_face * own_mixed - own_face * other_mixed)
+        total_ref[l, 0] = own_total_ref[l, 0] + jnp.where(low_half, part, zero)
+        total_ref[l, 1] = own_total_ref[l, 1] + jnp.where(low_half, zero, part)
+
+    def update(step, l):
+        count = FOLDED - step
 
         def read_edge(l, t):
-            return own_edge_ref[l, t] if t < first else edge_ref[l, t]
-
-        for l in range(layers):
-            spread = neighbour_sums(read_edge, l, layers, count, masks)
-            for t in range(full):
-                diffused = total_ref[l, t] - spread[t]
-                if t >= OWN_TILES:
-                    lower, upper = inside[(t + 1) % 2], inside[t % 2]
-                    diffused = diffused * jnp.where(low_half, lower, upper)
-                residual = r_ref[l, t] - diffused
-                if step == ITERS - 1:
-                    send(1, l, t, residual)
-                    continue
-                r_ref[l, t] = residual
-                old = d_ref[l, t]
-                direction = scales[1 + 2 * step] * old + scales[2 + 2 * step] * residual
-                d_ref[l, t] = direction
-                if t < OWN_TILES:
-                    value = (old if step == 0 else x_ref[l, t]) + direction
-                    if step == ITERS - 2:
-                        send(0, l, t, value)
-                    else:
-                        x_ref[l, t] = value
+            return own_edge_ref[l, t] if step == 0 and t < OWN_TILES else edge_ref[l, t]
+
+        spread = neighbour_sums(read_edge, l, layers, count, masks)
+        for t in range(count - 1):
+            diffused = total_ref[l, t] - spread[t]
+            if t >= OWN_TILES:
+                lower, upper = inside[(t + 1) % 2], inside[t % 2]
+                diffused = diffused * jnp.where(low_half, lower, upper)
+            residual = r_ref[l, t] - diffused
+            if step == ITERS - 1:
+                send(1, l, t, residual)
+                continue
+            r_ref[l, t] = residual
+            old = d_ref[l, t]
+            direction = scales[1 + 2 * step] * old + scales[2 + 2 * step] * residual
+            d_ref[l, t] = direction
+            if t < OWN_TILES:
+                value = (old if step == 0 else x_ref[l, t]) + direction
+                if step == ITERS - 2:
+                    send(0, l, t, value)
+                else:
+                    x_ref[l, t] = value
+
+    tasks = []
+    for l in range(layers):
+        tasks.append((l - 1.5, lambda l=l: fold(l)))
+        for step in range(ITERS):
+            for wait, task in ((0, prepare), (1.25, combine), (2.5, update)):
+                tasks.append((l + 4 * step + wait, functools.partial(task, step, l)))
+    for _, task in sorted(tasks, key=lambda task: task[0]):
+        task()
 
 
 def call(kernel, outs, scalars, arrays, scratch=(), flops=0, in_kinds=None, out_kind=pltpu.VMEM):

time: 92.9 us -> 92.8 us (level)
  no operation moved by 1% of the time
where the time goes in v8:
time: 92.8 us; the launch traced here: 92.4 us
  blocking collectives  39.5 us (43%)
  Pallas kernels  19.8 us (21%)
  waiting for transfers between devices  14.3 us (15%)
  starting transfers between devices  12.7 us (14%)
  between operations  3.71 us (4%)
  local copies, waits for them, and re-layouts  1.12 us (1%)
    all_to_all x1, blocking collectives, local_by_cells(): received = lax.all_to_all(sent, BOTH, 0, 0, tiled=True)  39.5 us
    pallas_call x7, Pallas kernels, call(): pl.pallas_call(kernel, out_shape=outs, in_specs=in_specs, out_specs=[pl.B...  19.8 us
    all_to_all x1, starting transfers between devices, local_by_cells(): lax.all_to_all(scattered, BOTH, 0, 0, tiled=True).reshape(-1, LANES)  7.47 us
    ppermute x2, waiting for transfers between devices, swap(): return lax.ppermute(field, BOTH, pairs + [(b, a) for a, b in pairs])  5.46 us
    all_to_all x1, waiting for transfers between devices, local_by_cells(): lax.all_to_all(scattered, BOTH, 0, 0, tiled=True).reshape(-1, LANES)  5.42 us
    ppermute x3, waiting for transfers between devices, local_by_cells(): lax.ppermute(picked[n], 'space', [(i, (i + n) % spaces) for i in range(sp...  3.42 us
    ppermute x2, starting transfers between devices, swap(): return lax.ppermute(field, BOTH, pairs + [(b, a) for a, b in pairs])  3.02 us
    ppermute x3, starting transfers between devices, local_by_cells(): lax.ppermute(picked[n], 'space', [(i, (i + n) % spaces) for i in range(sp...  2.23 us
  transfers between devices with their start and end apart: 6, of which 5 were waited for; matrix products, arithmetic and copies ran while one was open for 2% of the time, Pallas kernels for 4%

profile of v8, /device:TPU:1, one launch (start us, length us, event | category | flops | bytes accessed | tf_op | source)
XLA Modules:
  0.0 92.4 jit_solution(18350732046960911044)
XLA Ops:
  0.6 0.0 copy-start.3
  0.6 0.0 copy-start.4
  0.7 0.0 copy-start.2
  0.7 2.1 %shard_map.79 = f32[16,22,4,128]{3,2,1,0:T(4,128)} custom-call(f32[22,16,4,128]{3,2,1,0:T(4,128)} %bitcast.68), custom_call_target="tpu_custom_call" | custom-call | bytes 1441792 | tf_op jit(solution)/shard_map/pallas_call | solution.py:547
  2.8 0.0 copy-start
  2.8 0.0 copy-start.1
  2.8 7.5 %all-to-all-start = ((f32[16,22,4,128]{3,2,1,0:T(4,128)}), f32[16,22,4,128]{3,2,1,0:T(4,128)S(1)}, u32[]{:S(2)}, u32[]{:S(2)}) async-start(f32[16,22,4,128]{3,2,1,0:T(4,128)} %shard_map.79), calls=%async_computation | async-start | bytes 1441792 | tf_op jit(solution)/shard_map/all_to_all | solution.py:628
  10.3 0.0 copy-done.3
  10.3 0.6 fusion.19
  13.4 0.0 copy-done.4
  13.4 0.1 reshape.177
  13.5 0.1 slice_bitcast_fusion
  13.7 0.0 copy-done.2
  13.8 0.1 concatenate.13
  13.8 0.4 fusion.2
  14.3 0.4 fusion
  14.8 0.1 stack.32.scales
  14.9 0.1 pad_maximum_fusion.mix_ref
  15.0 0.0 copy-done
  15.0 0.0 copy-done.1
  15.0 0.6 shard_map.77
  15.7 1.7 %collective-permute-start = (f32[84,128]{1,0:T(8,128)S(1)}, f32[84,128]{1,0:T(8,128)S(1)}, u32[]{:S(2)}, u32[]{:S(2)}) collective-permute-start(f32[84,128]{1,0:T(8,128)S(1)} %get-tuple-element.18), channel_id=1, source_target_pairs={{0,1},{1,2},{2,3},{3,0},{4,5},{5,6},{6,7},{7,4},{8,9},{9,10},{10,1... | collective-permute-start | bytes 129032 | tf_op jit(solution)/shard_map/ppermute | solution.py:651
  17.3 0.0 collective-permute-start.1
  17.3 0.5 collective-permute-start.2
  17.9 0.1 convert_reduce_fusion
  18.1 0.6 collective-permute-done.refs_1_
  18.7 2.6 %collective-permute-done.1.refs_2_ = f32[84,128]{1,0:T(8,128)S(1)} collective-permute-done((f32[84,128]{1,0:T(8,128)S(1)}, f32[84,128]{1,0:T(8,128)S(1)}, u32[]{:S(2)}, u32[]{:S(2)}) %collective-permute-start.1) | collective-permute-done | bytes 43040 | tf_op jit(solution)/shard_map/ppermute | solution.py:651
  21.3 0.2 collective-permute-done.2.refs_3_
  21.5 0.8 shard_map.78
  22.3 5.4 %all-to-all-done = f32[16,22,4,128]{3,2,1,0:T(4,128)S(1)} async-done(((f32[16,22,4,128]{3,2,1,0:T(4,128)}), f32[16,22,4,128]{3,2,1,0:T(4,128)S(1)}, u32[]{:S(2)}, u32[]{:S(2)}) %all-to-all-start) | async-done | bytes 720928 | tf_op jit(solution)/shard_map/all_to_all | solution.py:628
  27.7 0.1 mul.69.weight_ref
  27.8 1.0 %shard_map.80 = (f32[8,2,88,128]{3,2,1,0:T(8,128)S(1)}, f32[1056,128]{1,0:T(8,128)}, f32[1056,128]{1,0:T(8,128)S(1)}) custom-call(s32[1]{0:T(128)} %bitcast.9.odd, f32[7,8,640]{2,1,0:T(8,128)S(1)} %get-tuple-element.21.a_ref, f32[88,128]{1,0:T(8,128)S(1)} %mul.69.weight_ref, f32[1408,128]{1,0:T(8,128)S(1)} %bitcast.64), custom_call_target="tpu_custom_call" | custom-call | bytes 2711552 | tf_op jit(solution)/shard_map/pallas_call | solution.py:547
  28.8 3.0 %collective-permute-start.3 = (f32[1056,128]{1,0:T(8,128)}, f32[1056,128]{1,0:T(8,128)S(1)}, u32[]{:S(2)}, u32[]{:S(2)}) collective-permute-start(f32[1056,128]{1,0:T(8,128)} %get-tuple-element.28), channel_id=1, source_target_pairs={{1,2},{3,7},{6,5},{4,8},{9,10},{11,15},{14,13},{2,1},{7,3},{5,6},{... | collective-permute-start | bytes 1622024 | tf_op jit(solution)/shard_map/ppermute | solution.py:673
  31.7 0.1 collective-permute-start.4
  31.8 0.1 add_convert_fusion.inside
  31.9 2.3 %shard_map.81 = (f32[8,2,88,128]{3,2,1,0:T(8,128)S(1)}, f32[8,2,88,128]{3,2,1,0:T(8,128)S(1)}) custom-call(f32[5]{0:T(128)S(1)} %stack.32.scales, bf16[528,192]{1,0:T(8,128)(2,1)S(1)} %pad_maximum_fusion.mix_ref, f32[7,8,640]{2,1,0:T(8,128)S(1)} %get-tuple-element.21.a_ref, f32[7,8,256]{2,1,0:T(8,128)S(1)} %get-tuple-element.25.b_ref, ...), custom_call_target="tpu_custom_call" | custom-call | flops 3000000000 | bytes 2768896 | tf_op jit(solution)/shard_map/pallas_call | solution.py:547
  34.2 5.5 %collective-permute-done.3.chip_ref = f32[1056,128]{1,0:T(8,128)S(1)} collective-permute-done((f32[1056,128]{1,0:T(8,128)}, f32[1056,128]{1,0:T(8,128)S(1)}, u32[]{:S(2)}, u32[]{:S(2)}) %collective-permute-start.3) | collective-permute-done | bytes 540704 | tf_op jit(solution)/shard_map/ppermute | solution.py:673
  39.6 0.0 collective-permute-done.4.core_ref
  39.6 0.1 mul.67.unweight_ref
  39.7 11.7 %shard_map.82 = f32[2816,128]{1,0:T(8,128)S(1)} custom-call(f32[5]{0:T(128)S(1)} %stack.32.scales, f32[2]{0:T(128)S(1)} %add_convert_fusion.inside, s32[1]{0:T(128)} %bitcast.9.odd, bf16[528,192]{1,0:T(8,128)(2,1)S(1)} %pad_maximum_fusion.mix_ref, f32[7,8,640]{2,1,0:T(8,128)S(1)} %get-tuple-element.21.a_ref, f32[7,8,512]{2,1,0:T(8,128)S(1)} %get-tuple-element.22.b_ref, ...), custom_call_target="tpu_custom_call" | custom-call | flops 10000000000 | bytes 5451776 | tf_op jit(solution)/shard_map/pallas_call | solution.py:547
  51.4 39.5 %all_to_all.10.in_ref = f32[16,2,22,4,128]{4,3,2,1,0:T(4,128)S(1)} all-to-all(f32[16,2,22,4,128]{4,3,2,1,0:T(4,128)S(1)} %bitcast.65), channel_id=1, replica_groups=mesh['groups'=2,'chaos'=4,'space'=4] {'chaos','space'}, dimensions={0} | all-to-all | bytes 2883584 | tf_op jit(solution)/shard_map/all_to_all | solution.py:704
  90.9 1.4 %shard_map.83 = (f32[22,16,4,128]{3,2,1,0:T(4,128)}, f32[22,16,4,128]{3,2,1,0:T(4,128)}) custom-call(f32[16,2,22,4,128]{4,3,2,1,0:T(4,128)S(1)} %all_to_all.10.in_ref), custom_call_target="tpu_custom_call" | custom-call | bytes 2883584 | tf_op jit(solution)/shard_map/pallas_call | solution.py:547
  (10 shorter events, 0.1 us)
Async XLA Ops:
  0.6 9.7 %copy-start.3 = (f32[2]{0:T(128)S(1)}, f32[2]{0:T(128)}, u32[]{:S(2)}) copy-start(f32[2]{0:T(128)} %param.11) | copy-start | bytes 28
  0.6 12.8 %copy-start.4 = (s32[88]{0:T(128)S(1)}, s32[88]{0:T(128)}, u32[]{:S(2)}) copy-start(s32[88]{0:T(128)} %param.10) | copy-start | bytes 1060
  0.7 13.1 %copy-start.2 = (s32[6,28,3]{1,2,0:T(4,128)S(1)}, s32[6,28,3]{1,2,0:T(4,128)}, u32[]{:S(2)}) copy-start(s32[6,28,3]{1,2,0:T(4,128)} %param.9) | copy-start | bytes 6052
  2.8 12.2 %copy-start = (f32[6,2,4096]{2,1,0:T(2,128)S(1)}, f32[6,2,4096]{2,1,0:T(2,128)}, u32[]{:S(2)}) copy-start(f32[6,2,4096]{2,1,0:T(2,128)} %param.8) | copy-start | bytes 589828
  2.8 12.2 %copy-start.1 = (f32[2,4096]{1,0:T(2,128)S(1)}, f32[2,4096]{1,0:T(2,128)}, u32[]{:S(2)}) copy-start(f32[2,4096]{1,0:T(2,128)} %param.7) | copy-start | bytes 98308
  2.8 24.9 %all-to-all-start = ((f32[16,22,4,128]{3,2,1,0:T(4,128)}), f32[16,22,4,128]{3,2,1,0:T(4,128)S(1)}, u32[]{:S(2)}, u32[]{:S(2)}) async-start(f32[16,22,4,128]{3,2,1,0:T(4,128)} %shard_map.79), calls=%async_computation | async-start | bytes 1441792 | tf_op jit(solution)/shard_map/all_to_all | solution.py:628
  15.7 3.1 %collective-permute-start = (f32[84,128]{1,0:T(8,128)S(1)}, f32[84,128]{1,0:T(8,128)S(1)}, u32[]{:S(2)}, u32[]{:S(2)}) collective-permute-start(f32[84,128]{1,0:T(8,128)S(1)} %get-tuple-element.18), channel_id=1, source_target_pairs={{0,1},{1,2},{2,3},{3,0},{4,5},{5,6},{6,7},{7,4},{8,9},{9,10},{10,1... | collective-permute-start | bytes 129032 | tf_op jit(solution)/shard_map/ppermute | solution.py:651
  17.3 3.9 %collective-permute-start.1 = (f32[84,128]{1,0:T(8,128)S(1)}, f32[84,128]{1,0:T(8,128)S(1)}, u32[]{:S(2)}, u32[]{:S(2)}) collective-permute-start(f32[84,128]{1,0:T(8,128)S(1)} %get-tuple-element.19), channel_id=1, source_target_pairs={{0,2},{1,3},{2,0},{3,1},{4,6},{5,7},{6,4},{7,5},{8,10},{9,11},{10,... | collective-permute-start | bytes 129032 | tf_op jit(solution)/shard_map/ppermute | solution.py:651
  17.3 4.2 %collective-permute-start.2 = (f32[84,128]{1,0:T(8,128)S(1)}, f32[84,128]{1,0:T(8,128)S(1)}, u32[]{:S(2)}, u32[]{:S(2)}) collective-permute-start(f32[84,128]{1,0:T(8,128)S(1)} %get-tuple-element.20), channel_id=1, source_target_pairs={{0,3},{1,0},{2,1},{3,2},{4,7},{5,4},{6,5},{7,6},{8,11},{9,8},{10,9... | collective-permute-start | bytes 129032 | tf_op jit(solution)/shard_map/ppermute | solution.py:651
  28.8 10.9 %collective-permute-start.3 = (f32[1056,128]{1,0:T(8,128)}, f32[1056,128]{1,0:T(8,128)S(1)}, u32[]{:S(2)}, u32[]{:S(2)}) collective-permute-start(f32[1056,128]{1,0:T(8,128)} %get-tuple-element.28), channel_id=1, source_target_pairs={{1,2},{3,7},{6,5},{4,8},{9,10},{11,15},{14,13},{2,1},{7,3},{5,6},{... | collective-permute-start | bytes 1622024 | tf_op jit(solution)/shard_map/ppermute | solution.py:673
  31.7 7.9 %collective-permute-start.4 = (f32[1056,128]{1,0:T(8,128)S(1)}, f32[1056,128]{1,0:T(8,128)S(1)}, u32[]{:S(2)}, u32[]{:S(2)}) collective-permute-start(f32[1056,128]{1,0:T(8,128)S(1)} %get-tuple-element.29), channel_id=1, source_target_pairs={{0,1},{2,3},{7,6},{5,4},{8,9},{10,11},{15,14},{13,12},{1,0},{3,2},... | collective-permute-start | bytes 1622024 | tf_op jit(solution)/shard_map/ppermute | solution.py:673

commit v9 on v8

--- a/solution.py
+++ b/solution.py
@@ -534,7 +534,9 @@
         task()
 
 
-def call(kernel, outs, scalars, arrays, scratch=(), flops=0, in_kinds=None, out_kind=pltpu.VMEM):
+def call(
+    kernel, outs, scalars, arrays, scratch=(), flops=0, in_kinds=None, out_kind=pltpu.VMEM, mebi=8
+):
     kinds = in_kinds or [pltpu.VMEM] * len(arrays)
     in_specs = [pl.BlockSpec(memory_space=pltpu.SMEM)] * len(scalars) + [
         pl.BlockSpec(memory_space=kind) for kind in kinds
@@ -550,7 +552,7 @@
         in_specs=in_specs,
         out_specs=[pl.BlockSpec(memory_space=out_kind)] * len(outs),
         scratch_shapes=scratch,
-        compiler_params=pltpu.CompilerParams(vmem_limit_bytes=40 * 1024 * 1024),
+        compiler_params=pltpu.CompilerParams(vmem_limit_bytes=mebi * 1024 * 1024),
         cost_estimate=pl.CostEstimate(flops=flops, bytes_accessed=moved, transcendentals=0),
     )(*scalars, *arrays)
 
@@ -681,6 +683,7 @@
         [scales],
         [mix, a, own_b, start],
         flops=3000000000,
+        mebi=16,
     )
 
     def held(tiles):
@@ -699,6 +702,7 @@
             held(OWN_TILES),
         ],
         flops=10000000000,
+        mebi=24,
     )[0]
     sent = sent.reshape(devices, 2, own, pieces, LANES)
     received = lax.all_to_all(sent, BOTH, 0, 0, tiled=True)

time: 92.8 us -> 92.8 us (level)
  no operation moved by 1% of the time
where the time goes in v9:
time: 92.8 us; the launch traced here: 92.4 us
  blocking collectives  39.5 us (43%)
  Pallas kernels  19.8 us (21%)
  waiting for transfers between devices  14.3 us (15%)
  starting transfers between devices  12.7 us (14%)
  between operations  3.71 us (4%)
  local copies, waits for them, and re-layouts  1.12 us (1%)
    all_to_all x1, blocking collectives, local_by_cells(): received = lax.all_to_all(sent, BOTH, 0, 0, tiled=True)  39.5 us
    pallas_call x7, Pallas kernels, call(): pl.pallas_call(kernel, out_shape=outs, in_specs=in_specs, out_specs=[pl.B...  19.8 us
    all_to_all x1, starting transfers between devices, local_by_cells(): lax.all_to_all(scattered, BOTH, 0, 0, tiled=True).reshape(-1, LANES)  7.47 us
    ppermute x2, waiting for transfers between devices, swap(): return lax.ppermute(field, BOTH, pairs + [(b, a) for a, b in pairs])  5.46 us
    all_to_all x1, waiting for transfers between devices, local_by_cells(): lax.all_to_all(scattered, BOTH, 0, 0, tiled=True).reshape(-1, LANES)  5.42 us
    ppermute x3, waiting for transfers between devices, local_by_cells(): lax.ppermute(picked[n], 'space', [(i, (i + n) % spaces) for i in range(sp...  3.42 us
    ppermute x2, starting transfers between devices, swap(): return lax.ppermute(field, BOTH, pairs + [(b, a) for a, b in pairs])  3.02 us
    ppermute x3, starting transfers between devices, local_by_cells(): lax.ppermute(picked[n], 'space', [(i, (i + n) % spaces) for i in range(sp...  2.23 us
  transfers between devices with their start and end apart: 6, of which 5 were waited for; matrix products, arithmetic and copies ran while one was open for 2% of the time, Pallas kernels for 4%

profile of v9, /device:TPU:1, one launch (start us, length us, event | category | flops | bytes accessed | tf_op | source)
XLA Modules:
  0.0 92.4 jit_solution(7349876736600666897)
XLA Ops:
  0.6 0.0 copy-start.3
  0.6 0.0 copy-start.4
  0.7 0.0 copy-start.2
  0.7 2.1 %shard_map.79 = f32[16,22,4,128]{3,2,1,0:T(4,128)} custom-call(f32[22,16,4,128]{3,2,1,0:T(4,128)} %bitcast.68), custom_call_target="tpu_custom_call" | custom-call | bytes 1441792 | tf_op jit(solution)/shard_map/pallas_call | solution.py:549
  2.8 0.0 copy-start
  2.8 0.0 copy-start.1
  2.8 7.5 %all-to-all-start = ((f32[16,22,4,128]{3,2,1,0:T(4,128)}), f32[16,22,4,128]{3,2,1,0:T(4,128)S(1)}, u32[]{:S(2)}, u32[]{:S(2)}) async-start(f32[16,22,4,128]{3,2,1,0:T(4,128)} %shard_map.79), calls=%async_computation | async-start | bytes 1441792 | tf_op jit(solution)/shard_map/all_to_all | solution.py:630
  10.3 0.0 copy-done.3
  10.3 0.6 fusion.19
  13.4 0.0 copy-done.4
  13.4 0.1 reshape.177
  13.5 0.1 slice_bitcast_fusion
  13.7 0.0 copy-done.2
  13.8 0.1 concatenate.13
  13.8 0.4 fusion.2
  14.3 0.4 fusion
  14.8 0.1 stack.32.scales
  14.9 0.1 pad_maximum_fusion.mix_ref
  15.0 0.0 copy-done
  15.0 0.0 copy-done.1
  15.0 0.6 shard_map.77
  15.7 1.7 %collective-permute-start = (f32[84,128]{1,0:T(8,128)S(1)}, f32[84,128]{1,0:T(8,128)S(1)}, u32[]{:S(2)}, u32[]{:S(2)}) collective-permute-start(f32[84,128]{1,0:T(8,128)S(1)} %get-tuple-element.18), channel_id=1, source_target_pairs={{0,1},{1,2},{2,3},{3,0},{4,5},{5,6},{6,7},{7,4},{8,9},{9,10},{10,1... | collective-permute-start | bytes 129032 | tf_op jit(solution)/shard_map/ppermute | solution.py:653
  17.3 0.0 collective-permute-start.1
  17.3 0.5 collective-permute-start.2
  17.9 0.1 convert_reduce_fusion
  18.1 0.6 collective-permute-done.refs_1_
  18.7 2.6 %collective-permute-done.1.refs_2_ = f32[84,128]{1,0:T(8,128)S(1)} collective-permute-done((f32[84,128]{1,0:T(8,128)S(1)}, f32[84,128]{1,0:T(8,128)S(1)}, u32[]{:S(2)}, u32[]{:S(2)}) %collective-permute-start.1) | collective-permute-done | bytes 43040 | tf_op jit(solution)/shard_map/ppermute | solution.py:653
  21.3 0.2 collective-permute-done.2.refs_3_
  21.5 0.8 shard_map.78
  22.3 5.4 %all-to-all-done = f32[16,22,4,128]{3,2,1,0:T(4,128)S(1)} async-done(((f32[16,22,4,128]{3,2,1,0:T(4,128)}), f32[16,22,4,128]{3,2,1,0:T(4,128)S(1)}, u32[]{:S(2)}, u32[]{:S(2)}) %all-to-all-start) | async-done | bytes 720928 | tf_op jit(solution)/shard_map/all_to_all | solution.py:630
  27.7 0.1 mul.69.weight_ref
  27.8 1.0 %shard_map.80 = (f32[8,2,88,128]{3,2,1,0:T(8,128)S(1)}, f32[1056,128]{1,0:T(8,128)}, f32[1056,128]{1,0:T(8,128)S(1)}) custom-call(s32[1]{0:T(128)} %bitcast.9.odd, f32[7,8,640]{2,1,0:T(8,128)S(1)} %get-tuple-element.21.a_ref, f32[88,128]{1,0:T(8,128)S(1)} %mul.69.weight_ref, f32[1408,128]{1,0:T(8,128)S(1)} %bitcast.64), custom_call_target="tpu_custom_call" | custom-call | bytes 2711552 | tf_op jit(solution)/shard_map/pallas_call | solution.py:549
  28.8 3.0 %collective-permute-start.3 = (f32[1056,128]{1,0:T(8,128)}, f32[1056,128]{1,0:T(8,128)S(1)}, u32[]{:S(2)}, u32[]{:S(2)}) collective-permute-start(f32[1056,128]{1,0:T(8,128)} %get-tuple-element.28), channel_id=1, source_target_pairs={{1,2},{3,7},{6,5},{4,8},{9,10},{11,15},{14,13},{2,1},{7,3},{5,6},{... | collective-permute-start | bytes 1622024 | tf_op jit(solution)/shard_map/ppermute | solution.py:675
  31.7 0.1 collective-permute-start.4
  31.8 0.1 add_convert_fusion.inside
  31.9 2.3 %shard_map.81 = (f32[8,2,88,128]{3,2,1,0:T(8,128)S(1)}, f32[8,2,88,128]{3,2,1,0:T(8,128)S(1)}) custom-call(f32[5]{0:T(128)S(1)} %stack.32.scales, bf16[528,192]{1,0:T(8,128)(2,1)S(1)} %pad_maximum_fusion.mix_ref, f32[7,8,640]{2,1,0:T(8,128)S(1)} %get-tuple-element.21.a_ref, f32[7,8,256]{2,1,0:T(8,128)S(1)} %get-tuple-element.25.b_ref, ...), custom_call_target="tpu_custom_call" | custom-call | flops 3000000000 | bytes 2768896 | tf_op jit(solution)/shard_map/pallas_call | solution.py:549
  34.2 5.5 %collective-permute-done.3.chip_ref = f32[1056,128]{1,0:T(8,128)S(1)} collective-permute-done((f32[1056,128]{1,0:T(8,128)}, f32[1056,128]{1,0:T(8,128)S(1)}, u32[]{:S(2)}, u32[]{:S(2)}) %collective-permute-start.3) | collective-permute-done | bytes 540704 | tf_op jit(solution)/shard_map/ppermute | solution.py:675
  39.6 0.0 collective-permute-done.4.core_ref
  39.6 0.1 mul.67.unweight_ref
  39.7 11.7 %shard_map.82 = f32[2816,128]{1,0:T(8,128)S(1)} custom-call(f32[5]{0:T(128)S(1)} %stack.32.scales, f32[2]{0:T(128)S(1)} %add_convert_fusion.inside, s32[1]{0:T(128)} %bitcast.9.odd, bf16[528,192]{1,0:T(8,128)(2,1)S(1)} %pad_maximum_fusion.mix_ref, f32[7,8,640]{2,1,0:T(8,128)S(1)} %get-tuple-element.21.a_ref, f32[7,8,512]{2,1,0:T(8,128)S(1)} %get-tuple-element.22.b_ref, ...), custom_call_target="tpu_custom_call" | custom-call | flops 10000000000 | bytes 5451776 | tf_op jit(solution)/shard_map/pallas_call | solution.py:549
  51.4 39.5 %all_to_all.10.in_ref = f32[16,2,22,4,128]{4,3,2,1,0:T(4,128)S(1)} all-to-all(f32[16,2,22,4,128]{4,3,2,1,0:T(4,128)S(1)} %bitcast.65), channel_id=1, replica_groups=mesh['groups'=2,'chaos'=4,'space'=4] {'chaos','space'}, dimensions={0} | all-to-all | bytes 2883584 | tf_op jit(solution)/shard_map/all_to_all | solution.py:708
  90.9 1.4 %shard_map.83 = (f32[22,16,4,128]{3,2,1,0:T(4,128)}, f32[22,16,4,128]{3,2,1,0:T(4,128)}) custom-call(f32[16,2,22,4,128]{4,3,2,1,0:T(4,128)S(1)} %all_to_all.10.in_ref), custom_call_target="tpu_custom_call" | custom-call | bytes 2883584 | tf_op jit(solution)/shard_map/pallas_call | solution.py:549
  (10 shorter events, 0.1 us)
Async XLA Ops:
  0.6 9.7 %copy-start.3 = (f32[2]{0:T(128)S(1)}, f32[2]{0:T(128)}, u32[]{:S(2)}) copy-start(f32[2]{0:T(128)} %param.11) | copy-start | bytes 28
  0.6 12.8 %copy-start.4 = (s32[88]{0:T(128)S(1)}, s32[88]{0:T(128)}, u32[]{:S(2)}) copy-start(s32[88]{0:T(128)} %param.10) | copy-start | bytes 1060
  0.7 13.1 %copy-start.2 = (s32[6,28,3]{1,2,0:T(4,128)S(1)}, s32[6,28,3]{1,2,0:T(4,128)}, u32[]{:S(2)}) copy-start(s32[6,28,3]{1,2,0:T(4,128)} %param.9) | copy-start | bytes 6052
  2.8 12.2 %copy-start = (f32[6,2,4096]{2,1,0:T(2,128)S(1)}, f32[6,2,4096]{2,1,0:T(2,128)}, u32[]{:S(2)}) copy-start(f32[6,2,4096]{2,1,0:T(2,128)} %param.8) | copy-start | bytes 589828
  2.8 12.2 %copy-start.1 = (f32[2,4096]{1,0:T(2,128)S(1)}, f32[2,4096]{1,0:T(2,128)}, u32[]{:S(2)}) copy-start(f32[2,4096]{1,0:T(2,128)} %param.7) | copy-start | bytes 98308
  2.8 24.9 %all-to-all-start = ((f32[16,22,4,128]{3,2,1,0:T(4,128)}), f32[16,22,4,128]{3,2,1,0:T(4,128)S(1)}, u32[]{:S(2)}, u32[]{:S(2)}) async-start(f32[16,22,4,128]{3,2,1,0:T(4,128)} %shard_map.79), calls=%async_computation | async-start | bytes 1441792 | tf_op jit(solution)/shard_map/all_to_all | solution.py:630
  15.7 3.1 %collective-permute-start = (f32[84,128]{1,0:T(8,128)S(1)}, f32[84,128]{1,0:T(8,128)S(1)}, u32[]{:S(2)}, u32[]{:S(2)}) collective-permute-start(f32[84,128]{1,0:T(8,128)S(1)} %get-tuple-element.18), channel_id=1, source_target_pairs={{0,1},{1,2},{2,3},{3,0},{4,5},{5,6},{6,7},{7,4},{8,9},{9,10},{10,1... | collective-permute-start | bytes 129032 | tf_op jit(solution)/shard_map/ppermute | solution.py:653
  17.3 3.9 %collective-permute-start.1 = (f32[84,128]{1,0:T(8,128)S(1)}, f32[84,128]{1,0:T(8,128)S(1)}, u32[]{:S(2)}, u32[]{:S(2)}) collective-permute-start(f32[84,128]{1,0:T(8,128)S(1)} %get-tuple-element.19), channel_id=1, source_target_pairs={{0,2},{1,3},{2,0},{3,1},{4,6},{5,7},{6,4},{7,5},{8,10},{9,11},{10,... | collective-permute-start | bytes 129032 | tf_op jit(solution)/shard_map/ppermute | solution.py:653
  17.3 4.2 %collective-permute-start.2 = (f32[84,128]{1,0:T(8,128)S(1)}, f32[84,128]{1,0:T(8,128)S(1)}, u32[]{:S(2)}, u32[]{:S(2)}) collective-permute-start(f32[84,128]{1,0:T(8,128)S(1)} %get-tuple-element.20), channel_id=1, source_target_pairs={{0,3},{1,0},{2,1},{3,2},{4,7},{5,4},{6,5},{7,6},{8,11},{9,8},{10,9... | collective-permute-start | bytes 129032 | tf_op jit(solution)/shard_map/ppermute | solution.py:653
  28.8 10.9 %collective-permute-start.3 = (f32[1056,128]{1,0:T(8,128)}, f32[1056,128]{1,0:T(8,128)S(1)}, u32[]{:S(2)}, u32[]{:S(2)}) collective-permute-start(f32[1056,128]{1,0:T(8,128)} %get-tuple-element.28), channel_id=1, source_target_pairs={{1,2},{3,7},{6,5},{4,8},{9,10},{11,15},{14,13},{2,1},{7,3},{5,6},{... | collective-permute-start | bytes 1622024 | tf_op jit(solution)/shard_map/ppermute | solution.py:675
  31.7 7.9 %collective-permute-start.4 = (f32[1056,128]{1,0:T(8,128)S(1)}, f32[1056,128]{1,0:T(8,128)S(1)}, u32[]{:S(2)}, u32[]{:S(2)}) collective-permute-start(f32[1056,128]{1,0:T(8,128)S(1)} %get-tuple-element.29), channel_id=1, source_target_pairs={{0,1},{2,3},{7,6},{5,4},{8,9},{10,11},{15,14},{13,12},{1,0},{3,2},... | collective-permute-start | bytes 1622024 | tf_op jit(solution)/shard_map/ppermute | solution.py:675

commit v10 on v9

--- a/solution.py
+++ b/solution.py
@@ -174,21 +174,15 @@
         copy.wait()
 
 
-def scatter_kernel(blocks, in_ref, out_ref, held_ref, sems):
-    own = in_ref.shape[0]
-    parts = sems.shape[0]
-    bounds = [own * n // parts for n in range(parts + 1)]
-    spans = [pl.ds(a, b - a) for a, b in zip(bounds[:-1], bounds[1:])]
+def scatter_kernel(blocks, in_ref, out_ref, sems):
     copies = [
-        pltpu.make_async_copy(in_ref.at[span], held_ref.at[span], sems.at[n])
-        for n, span in enumerate(spans)
+        pltpu.make_async_copy(in_ref.at[:, block], out_ref.at[device], sems.at[device])
+        for device, block in enumerate(blocks)
     ]
     for copy in copies:
         copy.start()
-    for copy, span in zip(copies, spans):
+    for copy in copies:
         copy.wait()
-        for device, block in enumerate(blocks):
-            out_ref[device, span] = held_ref[span, block]
 
 
 def pick_kernel(targets, scales, mix_ref, mean_ref, modes_ref, *outs):
@@ -218,7 +212,7 @@
 
 
 def coefficient_kernel(thick, sources, *refs):
-    *ins, a_ref, b_ref, own_b_ref, face_ref, held_ref = refs
+    *ins, a_ref, b_ref, face_ref, held_ref = refs
     modes, layers, _ = a_ref.shape
     tiles = held_ref.shape[1]
     layer = lax.broadcasted_iota(jnp.int32, (layers, LANES), 0)
@@ -249,12 +243,7 @@
             a_ref[k, :, lanes(t)] = values[t]
         for t in range(FOLDED - 1):
             b_ref[k, :, lanes(t)] = 6.0 * values[t] + (sums[t] + layer_sum(values[t], layer))
-        outside = jnp.zeros((layers, LANES), jnp.float32)
-        sums = plane_sums(values[:OWN_TILES] + [outside], masks)
-        for t in range(OWN_TILES):
-            own_b_ref[k, :, lanes(t)] = 6.0 * values[t] + (sums[t] + layer_sum(values[t], layer))
-        face_ref[k, :, lanes(0)] = jnp.where(low_half, values[0], values[1])
-        face_ref[k, :, lanes(1)] = pltpu.roll(values[2], NY, 1)
+        face_ref[k] = pltpu.roll(jnp.where(low_half, values[0], values[1]), NY, 1)
 
 
 def collect_kernel(blocks, in_ref, *rest):
@@ -460,20 +449,19 @@
         first = OWN_TILES if step == 0 else 0
         direct = [d_ref[l, t] for t in range(first, count)]
         around = neighbour_sums(read, l, layers, count, masks, first)
-        extra = [jnp.where(low_half, d_ref[l, 0], d_ref[l, 1])] if step == 0 else []
         mixed = jnp.dot(
-            mix, split_stack(direct + extra + around, depth), preferred_element_type=jnp.float32
+            mix, split_stack(direct + around, depth), preferred_element_type=jnp.float32
         )
-        prepared[step, l] = (mixed, direct, extra, around)
+        prepared[step, l] = (mixed, direct, around)
 
     def combine(step, l):
         first = OWN_TILES if step == 0 else 0
-        mixed, direct, extra, around = prepared.pop((step, l))
+        mixed, direct, around = prepared.pop((step, l))
         results = weighted_tiles(
             mixed,
             modes,
             0,
-            len(direct) + len(extra),
+            len(direct),
             direct,
             around,
             lambda k, t: a_ref[k, l : l + 1, lanes(first + t)],
@@ -485,17 +473,12 @@
                 total_ref[l, first + t] = total
         if step > 0:
             return
-        own_face = face_ref[0, l : l + 1, lanes(0)]
-        other_face = face_ref[0, l : l + 1, lanes(1)]
-        part = other_face * extra[0] - own_face * pltpu.roll(direct[0], NY, 1)
+        part = face_ref[0, l : l + 1, :] * direct[0]
         for k in range(1, modes):
-            own_face = face_ref[k, l : l + 1, lanes(0)]
-            other_face = face_ref[k, l : l + 1, lanes(1)]
-            own_mixed = mode_part(mixed, modes, k, len(direct))
-            other_mixed = pltpu.roll(mode_part(mixed, modes, k, 0), NY, 1)
-            part = part + (other_face * own_mixed - own_face * other_mixed)
-        total_ref[l, 0] = own_total_ref[l, 0] + jnp.where(low_half, part, zero)
-        total_ref[l, 1] = own_total_ref[l, 1] + jnp.where(low_half, zero, part)
+            part = part + face_ref[k, l : l + 1, :] * mode_part(mixed, modes, k, 0)
+        part = pltpu.roll(part, NY, 1)
+        total_ref[l, 0] = own_total_ref[l, 0] - jnp.where(low_half, part, zero)
+        total_ref[l, 1] = own_total_ref[l, 1] - jnp.where(low_half, zero, part)
 
     def update(step, l):
         count = FOLDED - step
@@ -624,8 +607,9 @@
         [shape(devices, own, pieces, LANES)],
         [],
         [by_columns(source_chaos_terms).reshape(own, devices, pieces, LANES)],
-        [pltpu.VMEM((own, devices, pieces, LANES), f32), pltpu.SemaphoreType.DMA((4,))],
+        [pltpu.SemaphoreType.DMA((devices,))],
         in_kinds=[pltpu.HBM],
+        out_kind=pltpu.HBM,
     )[0]
     gathered = lax.all_to_all(scattered, BOTH, 0, 0, tiled=True).reshape(-1, LANES)
 
@@ -653,9 +637,9 @@
         lax.ppermute(picked[n], "space", [(i, (i + n) % spaces) for i in range(spaces)])
         for n in range(1, spaces)
     ]
-    a, b, own_b, face = call(
+    a, b, face = call(
         functools.partial(coefficient_kernel, thick),
-        [shape(modes, layers, tiles * LANES) for tiles in (FOLDED, FOLDED - 1, OWN_TILES, 2)],
+        [shape(modes, layers, tiles * LANES) for tiles in (FOLDED, FOLDED - 1, 1)],
         [(column - steps) % spaces],
         picked,
         [pltpu.VMEM((modes, 3 * OWN_TILES, layers, LANES), f32)],
@@ -681,7 +665,7 @@
         own_kernel,
         [own_field, own_field],
         [scales],
-        [mix, a, own_b, start],
+        [mix, a, b, start],
         flops=3000000000,
         mebi=16,
     )

time: 92.8 us -> 113 us (1.22)
  Pallas kernels: 19.8 us -> 40.1 us
    pallas_call x7, Pallas kernels: 19.8 us -> 40.1 us  [call(): pl.pallas_call(kernel, out_shape=outs, in_specs=in_specs, out_specs=[pl.B...]
  transfers between devices with their start and end apart: 6 -> 6, of which waited for: 5 -> 5; matrix products, arithmetic and copies ran while one was open for 2% -> 2% of each run, Pallas kernels for 4% -> 3%
where the time goes in v10:
time: 113 us
  Pallas kernels  40.1 us (35%)
  blocking collectives  39.5 us (35%)
  waiting for transfers between devices  14.3 us (13%)
  starting transfers between devices  12.7 us (11%)
  between operations  3.71 us (3%)
    pallas_call x7, Pallas kernels, call(): pl.pallas_call(kernel, out_shape=outs, in_specs=in_specs, out_specs=[pl.B...  40.1 us
    all_to_all x1, blocking collectives, local_by_cells(): received = lax.all_to_all(sent, BOTH, 0, 0, tiled=True)  39.5 us
    all_to_all x1, starting transfers between devices, local_by_cells(): lax.all_to_all(scattered, BOTH, 0, 0, tiled=True).reshape(-1, LANES)  7.47 us
    ppermute x2, waiting for transfers between devices, swap(): return lax.ppermute(field, BOTH, pairs + [(b, a) for a, b in pairs])  5.51 us
    all_to_all x1, waiting for transfers between devices, local_by_cells(): lax.all_to_all(scattered, BOTH, 0, 0, tiled=True).reshape(-1, LANES)  5.41 us
    ppermute x3, waiting for transfers between devices, local_by_cells(): lax.ppermute(picked[n], 'space', [(i, (i + n) % spaces) for i in range(sp...  3.42 us
    ppermute x2, starting transfers between devices, swap(): return lax.ppermute(field, BOTH, pairs + [(b, a) for a, b in pairs])  3.02 us
  transfers between devices with their start and end apart: 6, of which 5 were waited for; matrix products, arithmetic and copies ran while one was open for 2% of the time, Pallas kernels for 3%

profile of v10, /device:TPU:1, one launch (start us, length us, event | category | flops | bytes accessed | tf_op | source)
XLA Modules:
  0.0 112.8 jit_solution(11195305239537788800)
XLA Ops:
  0.6 0.0 copy-start.3
  0.6 0.0 copy-start.4
  0.7 0.0 copy-start.2
  0.7 23.1 %shard_map.79 = f32[16,22,4,128]{3,2,1,0:T(4,128)} custom-call(f32[22,16,4,128]{3,2,1,0:T(4,128)} %bitcast.68), custom_call_target="tpu_custom_call" | custom-call | bytes 1441792 | tf_op jit(solution)/shard_map/pallas_call | solution.py:532
  23.8 0.0 copy-start
  23.8 0.0 copy-start.1
  23.8 7.5 %all-to-all-start = ((f32[16,22,4,128]{3,2,1,0:T(4,128)}), f32[16,22,4,128]{3,2,1,0:T(4,128)S(1)}, u32[]{:S(2)}, u32[]{:S(2)}) async-start(f32[16,22,4,128]{3,2,1,0:T(4,128)} %shard_map.79), calls=%async_computation | async-start | bytes 1441792 | tf_op jit(solution)/shard_map/all_to_all | solution.py:614
  31.2 0.0 copy-done.3
  31.3 0.6 fusion.19
  34.4 0.0 copy-done.4
  34.4 0.1 reshape.177
  34.5 0.1 slice_bitcast_fusion
  34.7 0.0 copy-done.2
  34.7 0.1 concatenate.13
  34.8 0.4 fusion.2
  35.2 0.4 fusion
  35.7 0.1 stack.32.scales
  35.8 0.1 pad_maximum_fusion.mix_ref
  36.0 0.0 copy-done
  36.0 0.0 copy-done.1
  36.0 0.6 shard_map.77
  36.6 1.7 %collective-permute-start = (f32[84,128]{1,0:T(8,128)S(1)}, f32[84,128]{1,0:T(8,128)S(1)}, u32[]{:S(2)}, u32[]{:S(2)}) collective-permute-start(f32[84,128]{1,0:T(8,128)S(1)} %get-tuple-element.17), channel_id=1, source_target_pairs={{0,1},{1,2},{2,3},{3,0},{4,5},{5,6},{6,7},{7,4},{8,9},{9,10},{10,1... | collective-permute-start | bytes 129032 | tf_op jit(solution)/shard_map/ppermute | solution.py:637
  38.3 0.0 collective-permute-start.1
  38.3 0.5 collective-permute-start.2
  38.8 0.1 convert_reduce_fusion
  39.0 0.6 collective-permute-done.refs_1_
  39.7 2.6 %collective-permute-done.1.refs_2_ = f32[84,128]{1,0:T(8,128)S(1)} collective-permute-done((f32[84,128]{1,0:T(8,128)S(1)}, f32[84,128]{1,0:T(8,128)S(1)}, u32[]{:S(2)}, u32[]{:S(2)}) %collective-permute-start.1) | collective-permute-done | bytes 43040 | tf_op jit(solution)/shard_map/ppermute | solution.py:637
  42.2 0.2 collective-permute-done.2.refs_3_
  42.5 0.8 shard_map.78
  43.2 5.4 %all-to-all-done = f32[16,22,4,128]{3,2,1,0:T(4,128)S(1)} async-done(((f32[16,22,4,128]{3,2,1,0:T(4,128)}), f32[16,22,4,128]{3,2,1,0:T(4,128)S(1)}, u32[]{:S(2)}, u32[]{:S(2)}) %all-to-all-start) | async-done | bytes 720928 | tf_op jit(solution)/shard_map/all_to_all | solution.py:614
  48.7 0.1 mul.69.weight_ref
  48.7 1.0 shard_map.80
  49.7 3.0 %collective-permute-start.3 = (f32[1056,128]{1,0:T(8,128)}, f32[1056,128]{1,0:T(8,128)S(1)}, u32[]{:S(2)}, u32[]{:S(2)}) collective-permute-start(f32[1056,128]{1,0:T(8,128)} %get-tuple-element.26), channel_id=1, source_target_pairs={{1,2},{3,7},{6,5},{4,8},{9,10},{11,15},{14,13},{2,1},{7,3},{5,6},{... | collective-permute-start | bytes 1622024 | tf_op jit(solution)/shard_map/ppermute | solution.py:659
  52.7 0.1 collective-permute-start.4
  52.8 0.1 add_convert_fusion.inside
  52.8 2.2 %shard_map.81 = (f32[8,2,88,128]{3,2,1,0:T(8,128)S(1)}, f32[8,2,88,128]{3,2,1,0:T(8,128)S(1)}) custom-call(f32[5]{0:T(128)S(1)} %stack.32.scales, bf16[528,192]{1,0:T(8,128)(2,1)S(1)} %pad_maximum_fusion.mix_ref, f32[7,8,640]{2,1,0:T(8,128)S(1)} %get-tuple-element.20.a_ref, f32[7,8,512]{2,1,0:T(8,128)S(1)} %get-tuple-element.21.b_ref, ...), custom_call_target="tpu_custom_call" | custom-call | flops 3000000000 | bytes 2826240 | tf_op jit(solution)/shard_map/pallas_call | solution.py:532
  55.1 5.5 %collective-permute-done.3.chip_ref = f32[1056,128]{1,0:T(8,128)S(1)} collective-permute-done((f32[1056,128]{1,0:T(8,128)}, f32[1056,128]{1,0:T(8,128)S(1)}, u32[]{:S(2)}, u32[]{:S(2)}) %collective-permute-start.3) | collective-permute-done | bytes 540704 | tf_op jit(solution)/shard_map/ppermute | solution.py:659
  60.6 0.0 collective-permute-done.4.core_ref
  60.6 0.1 mul.67.unweight_ref
  60.7 11.1 %shard_map.82 = f32[2816,128]{1,0:T(8,128)S(1)} custom-call(f32[5]{0:T(128)S(1)} %stack.32.scales, f32[2]{0:T(128)S(1)} %add_convert_fusion.inside, s32[1]{0:T(128)} %bitcast.9.odd, bf16[528,192]{1,0:T(8,128)(2,1)S(1)} %pad_maximum_fusion.mix_ref, f32[7,8,640]{2,1,0:T(8,128)S(1)} %get-tuple-element.20.a_ref, f32[7,8,512]{2,1,0:T(8,128)S(1)} %get-tuple-element.21.b_ref, ...), custom_call_target="tpu_custom_call" | custom-call | flops 10000000000 | bytes 5423104 | tf_op jit(solution)/shard_map/pallas_call | solution.py:532
  71.8 39.5 %all_to_all.10.in_ref = f32[16,2,22,4,128]{4,3,2,1,0:T(4,128)S(1)} all-to-all(f32[16,2,22,4,128]{4,3,2,1,0:T(4,128)S(1)} %bitcast.65), channel_id=1, replica_groups=mesh['groups'=2,'chaos'=4,'space'=4] {'chaos','space'}, dimensions={0} | all-to-all | bytes 2883584 | tf_op jit(solution)/shard_map/all_to_all | solution.py:692
  111.2 1.4 %shard_map.83 = (f32[22,16,4,128]{3,2,1,0:T(4,128)}, f32[22,16,4,128]{3,2,1,0:T(4,128)}) custom-call(f32[16,2,22,4,128]{4,3,2,1,0:T(4,128)S(1)} %all_to_all.10.in_ref), custom_call_target="tpu_custom_call" | custom-call | bytes 2883584 | tf_op jit(solution)/shard_map/pallas_call | solution.py:532
  (10 shorter events, 0.1 us)
Async XLA Ops:
  0.6 30.6 %copy-start.3 = (f32[2]{0:T(128)S(1)}, f32[2]{0:T(128)}, u32[]{:S(2)}) copy-start(f32[2]{0:T(128)} %param.11) | copy-start | bytes 28
  0.6 33.8 %copy-start.4 = (s32[88]{0:T(128)S(1)}, s32[88]{0:T(128)}, u32[]{:S(2)}) copy-start(s32[88]{0:T(128)} %param.10) | copy-start | bytes 1060
  0.7 34.0 %copy-start.2 = (s32[6,28,3]{1,2,0:T(4,128)S(1)}, s32[6,28,3]{1,2,0:T(4,128)}, u32[]{:S(2)}) copy-start(s32[6,28,3]{1,2,0:T(4,128)} %param.9) | copy-start | bytes 6052
  23.8 12.2 %copy-start = (f32[6,2,4096]{2,1,0:T(2,128)S(1)}, f32[6,2,4096]{2,1,0:T(2,128)}, u32[]{:S(2)}) copy-start(f32[6,2,4096]{2,1,0:T(2,128)} %param.8) | copy-start | bytes 589828
  23.8 12.2 %copy-start.1 = (f32[2,4096]{1,0:T(2,128)S(1)}, f32[2,4096]{1,0:T(2,128)}, u32[]{:S(2)}) copy-start(f32[2,4096]{1,0:T(2,128)} %param.7) | copy-start | bytes 98308
  23.8 24.9 %all-to-all-start = ((f32[16,22,4,128]{3,2,1,0:T(4,128)}), f32[16,22,4,128]{3,2,1,0:T(4,128)S(1)}, u32[]{:S(2)}, u32[]{:S(2)}) async-start(f32[16,22,4,128]{3,2,1,0:T(4,128)} %shard_map.79), calls=%async_computation | async-start | bytes 1441792 | tf_op jit(solution)/shard_map/all_to_all | solution.py:614
  36.6 3.1 %collective-permute-start = (f32[84,128]{1,0:T(8,128)S(1)}, f32[84,128]{1,0:T(8,128)S(1)}, u32[]{:S(2)}, u32[]{:S(2)}) collective-permute-start(f32[84,128]{1,0:T(8,128)S(1)} %get-tuple-element.17), channel_id=1, source_target_pairs={{0,1},{1,2},{2,3},{3,0},{4,5},{5,6},{6,7},{7,4},{8,9},{9,10},{10,1... | collective-permute-start | bytes 129032 | tf_op jit(solution)/shard_map/ppermute | solution.py:637
  38.3 3.9 %collective-permute-start.1 = (f32[84,128]{1,0:T(8,128)S(1)}, f32[84,128]{1,0:T(8,128)S(1)}, u32[]{:S(2)}, u32[]{:S(2)}) collective-permute-start(f32[84,128]{1,0:T(8,128)S(1)} %get-tuple-element.18), channel_id=1, source_target_pairs={{0,2},{1,3},{2,0},{3,1},{4,6},{5,7},{6,4},{7,5},{8,10},{9,11},{10,... | collective-permute-start | bytes 129032 | tf_op jit(solution)/shard_map/ppermute | solution.py:637
  38.3 4.2 %collective-permute-start.2 = (f32[84,128]{1,0:T(8,128)S(1)}, f32[84,128]{1,0:T(8,128)S(1)}, u32[]{:S(2)}, u32[]{:S(2)}) collective-permute-start(f32[84,128]{1,0:T(8,128)S(1)} %get-tuple-element.19), channel_id=1, source_target_pairs={{0,3},{1,0},{2,1},{3,2},{4,7},{5,4},{6,5},{7,6},{8,11},{9,8},{10,9... | collective-permute-start | bytes 129032 | tf_op jit(solution)/shard_map/ppermute | solution.py:637
  49.7 10.9 %collective-permute-start.3 = (f32[1056,128]{1,0:T(8,128)}, f32[1056,128]{1,0:T(8,128)S(1)}, u32[]{:S(2)}, u32[]{:S(2)}) collective-permute-start(f32[1056,128]{1,0:T(8,128)} %get-tuple-element.26), channel_id=1, source_target_pairs={{1,2},{3,7},{6,5},{4,8},{9,10},{11,15},{14,13},{2,1},{7,3},{5,6},{... | collective-permute-start | bytes 1622024 | tf_op jit(solution)/shard_map/ppermute | solution.py:659
  52.7 7.9 %collective-permute-start.4 = (f32[1056,128]{1,0:T(8,128)S(1)}, f32[1056,128]{1,0:T(8,128)S(1)}, u32[]{:S(2)}, u32[]{:S(2)}) collective-permute-start(f32[1056,128]{1,0:T(8,128)S(1)} %get-tuple-element.27), channel_id=1, source_target_pairs={{0,1},{2,3},{7,6},{5,4},{8,9},{10,11},{15,14},{13,12},{1,0},{3,2},... | collective-permute-start | bytes 1622024 | tf_op jit(solution)/shard_map/ppermute | solution.py:659

commit v11 on v10

--- a/solution.py
+++ b/solution.py
@@ -174,15 +174,21 @@
         copy.wait()
 
 
-def scatter_kernel(blocks, in_ref, out_ref, sems):
+def scatter_kernel(blocks, in_ref, out_ref, held_ref, sems):
+    own = in_ref.shape[0]
+    parts = sems.shape[0]
+    bounds = [own * n // parts for n in range(parts + 1)]
+    spans = [pl.ds(a, b - a) for a, b in zip(bounds[:-1], bounds[1:])]
     copies = [
-        pltpu.make_async_copy(in_ref.at[:, block], out_ref.at[device], sems.at[device])
-        for device, block in enumerate(blocks)
+        pltpu.make_async_copy(in_ref.at[span], held_ref.at[span], sems.at[n])
+        for n, span in enumerate(spans)
     ]
     for copy in copies:
         copy.start()
-    for copy in copies:
+    for copy, span in zip(copies, spans):
         copy.wait()
+        for device, block in enumerate(blocks):
+            out_ref[device, span] = held_ref[span, block]
 
 
 def pick_kernel(targets, scales, mix_ref, mean_ref, modes_ref, *outs):
@@ -607,9 +613,8 @@
         [shape(devices, own, pieces, LANES)],
         [],
         [by_columns(source_chaos_terms).reshape(own, devices, pieces, LANES)],
-        [pltpu.SemaphoreType.DMA((devices,))],
+        [pltpu.VMEM((own, devices, pieces, LANES), f32), pltpu.SemaphoreType.DMA((4,))],
         in_kinds=[pltpu.HBM],
-        out_kind=pltpu.HBM,
     )[0]
     gathered = lax.all_to_all(scattered, BOTH, 0, 0, tiled=True).reshape(-1, LANES)
 

time: 113 us -> 92.1 us (0.82)
  Pallas kernels: 40.1 us -> 19.2 us
    pallas_call x7, Pallas kernels: 40.1 us -> 19.2 us  [call(): pl.pallas_call(kernel, out_shape=outs, in_specs=in_specs, out_specs=[pl.B...]
  transfers between devices with their start and end apart: 6 -> 6, of which waited for: 5 -> 5; matrix products, arithmetic and copies ran while one was open for 2% -> 2% of each run, Pallas kernels for 3% -> 4%
where the time goes in v11:
time: 92.1 us; the launch traced here: 91.8 us
  blocking collectives  39.5 us (43%)
  Pallas kernels  19.2 us (21%)
  waiting for transfers between devices  14.3 us (16%)
  starting transfers between devices  12.7 us (14%)
  between operations  3.71 us (4%)
  local copies, waits for them, and re-layouts  1.12 us (1%)
    all_to_all x1, blocking collectives, local_by_cells(): received = lax.all_to_all(sent, BOTH, 0, 0, tiled=True)  39.5 us
    pallas_call x7, Pallas kernels, call(): pl.pallas_call(kernel, out_shape=outs, in_specs=in_specs, out_specs=[pl.B...  19.2 us
    all_to_all x1, starting transfers between devices, local_by_cells(): lax.all_to_all(scattered, BOTH, 0, 0, tiled=True).reshape(-1, LANES)  7.47 us
    ppermute x2, waiting for transfers between devices, swap(): return lax.ppermute(field, BOTH, pairs + [(b, a) for a, b in pairs])  5.51 us
    all_to_all x1, waiting for transfers between devices, local_by_cells(): lax.all_to_all(scattered, BOTH, 0, 0, tiled=True).reshape(-1, LANES)  5.42 us
    ppermute x3, waiting for transfers between devices, local_by_cells(): lax.ppermute(picked[n], 'space', [(i, (i + n) % spaces) for i in range(sp...  3.42 us
    ppermute x2, starting transfers between devices, swap(): return lax.ppermute(field, BOTH, pairs + [(b, a) for a, b in pairs])  3.02 us
    ppermute x3, starting transfers between devices, local_by_cells(): lax.ppermute(picked[n], 'space', [(i, (i + n) % spaces) for i in range(sp...  2.23 us
  transfers between devices with their start and end apart: 6, of which 5 were waited for; matrix products, arithmetic and copies ran while one was open for 2% of the time, Pallas kernels for 4%

profile of v11, /device:TPU:1, one launch (start us, length us, event | category | flops | bytes accessed | tf_op | source)
XLA Modules:
  0.0 91.8 jit_solution(12976894791627818883)
XLA Ops:
  0.6 0.0 copy-start.3
  0.6 0.0 copy-start.4
  0.7 0.0 copy-start.2
  0.7 2.1 %shard_map.79 = f32[16,22,4,128]{3,2,1,0:T(4,128)} custom-call(f32[22,16,4,128]{3,2,1,0:T(4,128)} %bitcast.68), custom_call_target="tpu_custom_call" | custom-call | bytes 1441792 | tf_op jit(solution)/shard_map/pallas_call | solution.py:538
  2.8 0.0 copy-start
  2.8 0.0 copy-start.1
  2.8 7.5 %all-to-all-start = ((f32[16,22,4,128]{3,2,1,0:T(4,128)}), f32[16,22,4,128]{3,2,1,0:T(4,128)S(1)}, u32[]{:S(2)}, u32[]{:S(2)}) async-start(f32[16,22,4,128]{3,2,1,0:T(4,128)} %shard_map.79), calls=%async_computation | async-start | bytes 1441792 | tf_op jit(solution)/shard_map/all_to_all | solution.py:619
  10.3 0.0 copy-done.3
  10.3 0.6 fusion.19
  13.4 0.0 copy-done.4
  13.4 0.1 reshape.177
  13.5 0.1 slice_bitcast_fusion
  13.7 0.0 copy-done.2
  13.8 0.1 concatenate.13
  13.8 0.4 fusion.2
  14.3 0.4 fusion
  14.8 0.1 stack.32.scales
  14.9 0.1 pad_maximum_fusion.mix_ref
  15.0 0.0 copy-done
  15.0 0.0 copy-done.1
  15.0 0.6 shard_map.77
  15.7 1.7 %collective-permute-start = (f32[84,128]{1,0:T(8,128)S(1)}, f32[84,128]{1,0:T(8,128)S(1)}, u32[]{:S(2)}, u32[]{:S(2)}) collective-permute-start(f32[84,128]{1,0:T(8,128)S(1)} %get-tuple-element.17), channel_id=1, source_target_pairs={{0,1},{1,2},{2,3},{3,0},{4,5},{5,6},{6,7},{7,4},{8,9},{9,10},{10,1... | collective-permute-start | bytes 129032 | tf_op jit(solution)/shard_map/ppermute | solution.py:642
  17.3 0.0 collective-permute-start.1
  17.3 0.5 collective-permute-start.2
  17.9 0.1 convert_reduce_fusion
  18.1 0.6 collective-permute-done.refs_1_
  18.7 2.6 %collective-permute-done.1.refs_2_ = f32[84,128]{1,0:T(8,128)S(1)} collective-permute-done((f32[84,128]{1,0:T(8,128)S(1)}, f32[84,128]{1,0:T(8,128)S(1)}, u32[]{:S(2)}, u32[]{:S(2)}) %collective-permute-start.1) | collective-permute-done | bytes 43040 | tf_op jit(solution)/shard_map/ppermute | solution.py:642
  21.3 0.2 collective-permute-done.2.refs_3_
  21.5 0.8 shard_map.78
  22.3 5.4 %all-to-all-done = f32[16,22,4,128]{3,2,1,0:T(4,128)S(1)} async-done(((f32[16,22,4,128]{3,2,1,0:T(4,128)}), f32[16,22,4,128]{3,2,1,0:T(4,128)S(1)}, u32[]{:S(2)}, u32[]{:S(2)}) %all-to-all-start) | async-done | bytes 720928 | tf_op jit(solution)/shard_map/all_to_all | solution.py:619
  27.7 0.1 mul.69.weight_ref
  27.8 1.0 %shard_map.80 = (f32[8,2,88,128]{3,2,1,0:T(8,128)S(1)}, f32[1056,128]{1,0:T(8,128)}, f32[1056,128]{1,0:T(8,128)S(1)}) custom-call(s32[1]{0:T(128)} %bitcast.9.odd, f32[7,8,640]{2,1,0:T(8,128)S(1)} %get-tuple-element.20.a_ref, f32[88,128]{1,0:T(8,128)S(1)} %mul.69.weight_ref, f32[1408,128]{1,0:T(8,128)S(1)} %bitcast.64), custom_call_target="tpu_custom_call" | custom-call | bytes 2711552 | tf_op jit(solution)/shard_map/pallas_call | solution.py:538
  28.8 3.0 %collective-permute-start.3 = (f32[1056,128]{1,0:T(8,128)}, f32[1056,128]{1,0:T(8,128)S(1)}, u32[]{:S(2)}, u32[]{:S(2)}) collective-permute-start(f32[1056,128]{1,0:T(8,128)} %get-tuple-element.26), channel_id=1, source_target_pairs={{1,2},{3,7},{6,5},{4,8},{9,10},{11,15},{14,13},{2,1},{7,3},{5,6},{... | collective-permute-start | bytes 1622024 | tf_op jit(solution)/shard_map/ppermute | solution.py:664
  31.7 0.1 collective-permute-start.4
  31.8 0.1 add_convert_fusion.inside
  31.9 2.2 %shard_map.81 = (f32[8,2,88,128]{3,2,1,0:T(8,128)S(1)}, f32[8,2,88,128]{3,2,1,0:T(8,128)S(1)}) custom-call(f32[5]{0:T(128)S(1)} %stack.32.scales, bf16[528,192]{1,0:T(8,128)(2,1)S(1)} %pad_maximum_fusion.mix_ref, f32[7,8,640]{2,1,0:T(8,128)S(1)} %get-tuple-element.20.a_ref, f32[7,8,512]{2,1,0:T(8,128)S(1)} %get-tuple-element.21.b_ref, ...), custom_call_target="tpu_custom_call" | custom-call | flops 3000000000 | bytes 2826240 | tf_op jit(solution)/shard_map/pallas_call | solution.py:538
  34.1 5.5 %collective-permute-done.3.chip_ref = f32[1056,128]{1,0:T(8,128)S(1)} collective-permute-done((f32[1056,128]{1,0:T(8,128)}, f32[1056,128]{1,0:T(8,128)S(1)}, u32[]{:S(2)}, u32[]{:S(2)}) %collective-permute-start.3) | collective-permute-done | bytes 540704 | tf_op jit(solution)/shard_map/ppermute | solution.py:664
  39.6 0.0 collective-permute-done.4.core_ref
  39.6 0.1 mul.67.unweight_ref
  39.7 11.1 %shard_map.82 = f32[2816,128]{1,0:T(8,128)S(1)} custom-call(f32[5]{0:T(128)S(1)} %stack.32.scales, f32[2]{0:T(128)S(1)} %add_convert_fusion.inside, s32[1]{0:T(128)} %bitcast.9.odd, bf16[528,192]{1,0:T(8,128)(2,1)S(1)} %pad_maximum_fusion.mix_ref, f32[7,8,640]{2,1,0:T(8,128)S(1)} %get-tuple-element.20.a_ref, f32[7,8,512]{2,1,0:T(8,128)S(1)} %get-tuple-element.21.b_ref, ...), custom_call_target="tpu_custom_call" | custom-call | flops 10000000000 | bytes 5423104 | tf_op jit(solution)/shard_map/pallas_call | solution.py:538
  50.8 39.5 %all_to_all.10.in_ref = f32[16,2,22,4,128]{4,3,2,1,0:T(4,128)S(1)} all-to-all(f32[16,2,22,4,128]{4,3,2,1,0:T(4,128)S(1)} %bitcast.65), channel_id=1, replica_groups=mesh['groups'=2,'chaos'=4,'space'=4] {'chaos','space'}, dimensions={0} | all-to-all | bytes 2883584 | tf_op jit(solution)/shard_map/all_to_all | solution.py:697
  90.3 1.4 %shard_map.83 = (f32[22,16,4,128]{3,2,1,0:T(4,128)}, f32[22,16,4,128]{3,2,1,0:T(4,128)}) custom-call(f32[16,2,22,4,128]{4,3,2,1,0:T(4,128)S(1)} %all_to_all.10.in_ref), custom_call_target="tpu_custom_call" | custom-call | bytes 2883584 | tf_op jit(solution)/shard_map/pallas_call | solution.py:538
  (10 shorter events, 0.1 us)
Async XLA Ops:
  0.6 9.7 %copy-start.3 = (f32[2]{0:T(128)S(1)}, f32[2]{0:T(128)}, u32[]{:S(2)}) copy-start(f32[2]{0:T(128)} %param.11) | copy-start | bytes 28
  0.6 12.8 %copy-start.4 = (s32[88]{0:T(128)S(1)}, s32[88]{0:T(128)}, u32[]{:S(2)}) copy-start(s32[88]{0:T(128)} %param.10) | copy-start | bytes 1060
  0.7 13.1 %copy-start.2 = (s32[6,28,3]{1,2,0:T(4,128)S(1)}, s32[6,28,3]{1,2,0:T(4,128)}, u32[]{:S(2)}) copy-start(s32[6,28,3]{1,2,0:T(4,128)} %param.9) | copy-start | bytes 6052
  2.8 12.2 %copy-start = (f32[6,2,4096]{2,1,0:T(2,128)S(1)}, f32[6,2,4096]{2,1,0:T(2,128)}, u32[]{:S(2)}) copy-start(f32[6,2,4096]{2,1,0:T(2,128)} %param.8) | copy-start | bytes 589828
  2.8 12.2 %copy-start.1 = (f32[2,4096]{1,0:T(2,128)S(1)}, f32[2,4096]{1,0:T(2,128)}, u32[]{:S(2)}) copy-start(f32[2,4096]{1,0:T(2,128)} %param.7) | copy-start | bytes 98308
  2.8 24.9 %all-to-all-start = ((f32[16,22,4,128]{3,2,1,0:T(4,128)}), f32[16,22,4,128]{3,2,1,0:T(4,128)S(1)}, u32[]{:S(2)}, u32[]{:S(2)}) async-start(f32[16,22,4,128]{3,2,1,0:T(4,128)} %shard_map.79), calls=%async_computation | async-start | bytes 1441792 | tf_op jit(solution)/shard_map/all_to_all | solution.py:619
  15.7 3.1 %collective-permute-start = (f32[84,128]{1,0:T(8,128)S(1)}, f32[84,128]{1,0:T(8,128)S(1)}, u32[]{:S(2)}, u32[]{:S(2)}) collective-permute-start(f32[84,128]{1,0:T(8,128)S(1)} %get-tuple-element.17), channel_id=1, source_target_pairs={{0,1},{1,2},{2,3},{3,0},{4,5},{5,6},{6,7},{7,4},{8,9},{9,10},{10,1... | collective-permute-start | bytes 129032 | tf_op jit(solution)/shard_map/ppermute | solution.py:642
  17.3 3.9 %collective-permute-start.1 = (f32[84,128]{1,0:T(8,128)S(1)}, f32[84,128]{1,0:T(8,128)S(1)}, u32[]{:S(2)}, u32[]{:S(2)}) collective-permute-start(f32[84,128]{1,0:T(8,128)S(1)} %get-tuple-element.18), channel_id=1, source_target_pairs={{0,2},{1,3},{2,0},{3,1},{4,6},{5,7},{6,4},{7,5},{8,10},{9,11},{10,... | collective-permute-start | bytes 129032 | tf_op jit(solution)/shard_map/ppermute | solution.py:642
  17.3 4.2 %collective-permute-start.2 = (f32[84,128]{1,0:T(8,128)S(1)}, f32[84,128]{1,0:T(8,128)S(1)}, u32[]{:S(2)}, u32[]{:S(2)}) collective-permute-start(f32[84,128]{1,0:T(8,128)S(1)} %get-tuple-element.19), channel_id=1, source_target_pairs={{0,3},{1,0},{2,1},{3,2},{4,7},{5,4},{6,5},{7,6},{8,11},{9,8},{10,9... | collective-permute-start | bytes 129032 | tf_op jit(solution)/shard_map/ppermute | solution.py:642
  28.8 10.9 %collective-permute-start.3 = (f32[1056,128]{1,0:T(8,128)}, f32[1056,128]{1,0:T(8,128)S(1)}, u32[]{:S(2)}, u32[]{:S(2)}) collective-permute-start(f32[1056,128]{1,0:T(8,128)} %get-tuple-element.26), channel_id=1, source_target_pairs={{1,2},{3,7},{6,5},{4,8},{9,10},{11,15},{14,13},{2,1},{7,3},{5,6},{... | collective-permute-start | bytes 1622024 | tf_op jit(solution)/shard_map/ppermute | solution.py:664
  31.7 7.9 %collective-permute-start.4 = (f32[1056,128]{1,0:T(8,128)S(1)}, f32[1056,128]{1,0:T(8,128)S(1)}, u32[]{:S(2)}, u32[]{:S(2)}) collective-permute-start(f32[1056,128]{1,0:T(8,128)S(1)} %get-tuple-element.27), channel_id=1, source_target_pairs={{0,1},{2,3},{7,6},{5,4},{8,9},{10,11},{15,14},{13,12},{1,0},{3,2},... | collective-permute-start | bytes 1622024 | tf_op jit(solution)/shard_map/ppermute | solution.py:664

commit v12 on v11

--- a/solution.py
+++ b/solution.py
@@ -174,21 +174,29 @@
         copy.wait()
 
 
-def scatter_kernel(blocks, in_ref, out_ref, held_ref, sems):
+def scatter_kernel(blocks, in_ref, out_ref, held_ref, in_sems, out_sems):
     own = in_ref.shape[0]
-    parts = sems.shape[0]
+    parts = in_sems.shape[0]
     bounds = [own * n // parts for n in range(parts + 1)]
     spans = [pl.ds(a, b - a) for a, b in zip(bounds[:-1], bounds[1:])]
     copies = [
-        pltpu.make_async_copy(in_ref.at[span], held_ref.at[span], sems.at[n])
+        pltpu.make_async_copy(in_ref.at[span], held_ref.at[span], in_sems.at[n])
         for n, span in enumerate(spans)
     ]
     for copy in copies:
         copy.start()
-    for copy, span in zip(copies, spans):
+    leaving = []
+    for n, (copy, span) in enumerate(zip(copies, spans)):
         copy.wait()
         for device, block in enumerate(blocks):
-            out_ref[device, span] = held_ref[span, block]
+            leaving.append(
+                pltpu.make_async_copy(
+                    held_ref.at[span, block], out_ref.at[device, span], out_sems.at[n, device]
+                )
+            )
+            leaving[-1].start()
+    for copy in leaving:
+        copy.wait()
 
 
 def pick_kernel(targets, scales, mix_ref, mean_ref, modes_ref, *outs):
@@ -613,8 +621,13 @@
         [shape(devices, own, pieces, LANES)],
         [],
         [by_columns(source_chaos_terms).reshape(own, devices, pieces, LANES)],
-        [pltpu.VMEM((own, devices, pieces, LANES), f32), pltpu.SemaphoreType.DMA((4,))],
+        [
+            pltpu.VMEM((own, devices, pieces, LANES), f32),
+            pltpu.SemaphoreType.DMA((2,)),
+            pltpu.SemaphoreType.DMA((2, devices)),
+        ],
         in_kinds=[pltpu.HBM],
+        out_kind=pltpu.HBM,
     )[0]
     gathered = lax.all_to_all(scattered, BOTH, 0, 0, tiled=True).reshape(-1, LANES)
 

time: 92.1 us -> 92.1 us (level)
  no operation moved by 1% of the time
where the time goes in v12:
time: 92.1 us; the launch traced here: 91.8 us
  blocking collectives  39.5 us (43%)
  Pallas kernels  19.2 us (21%)
  waiting for transfers between devices  14.3 us (16%)
  starting transfers between devices  12.7 us (14%)
  between operations  3.71 us (4%)
  local copies, waits for them, and re-layouts  1.12 us (1%)
    all_to_all x1, blocking collectives, local_by_cells(): received = lax.all_to_all(sent, BOTH, 0, 0, tiled=True)  39.5 us
    pallas_call x7, Pallas kernels, call(): pl.pallas_call(kernel, out_shape=outs, in_specs=in_specs, out_specs=[pl.B...  19.2 us
    all_to_all x1, starting transfers between devices, local_by_cells(): lax.all_to_all(scattered, BOTH, 0, 0, tiled=True).reshape(-1, LANES)  7.47 us
    ppermute x2, waiting for transfers between devices, swap(): return lax.ppermute(field, BOTH, pairs + [(b, a) for a, b in pairs])  5.51 us
    all_to_all x1, waiting for transfers between devices, local_by_cells(): lax.all_to_all(scattered, BOTH, 0, 0, tiled=True).reshape(-1, LANES)  5.42 us
    ppermute x3, waiting for transfers between devices, local_by_cells(): lax.ppermute(picked[n], 'space', [(i, (i + n) % spaces) for i in range(sp...  3.42 us
    ppermute x2, starting transfers between devices, swap(): return lax.ppermute(field, BOTH, pairs + [(b, a) for a, b in pairs])  3.02 us
    ppermute x3, starting transfers between devices, local_by_cells(): lax.ppermute(picked[n], 'space', [(i, (i + n) % spaces) for i in range(sp...  2.23 us
  transfers between devices with their start and end apart: 6, of which 5 were waited for; matrix products, arithmetic and copies ran while one was open for 2% of the time, Pallas kernels for 4%

profile of v12, /device:TPU:1, one launch (start us, length us, event | category | flops | bytes accessed | tf_op | source)
XLA Modules:
  0.0 91.8 jit_solution(2780790098344975196)
XLA Ops:
  0.6 0.0 copy-start.3
  0.6 0.0 copy-start.4
  0.7 0.0 copy-start.2
  0.7 2.1 %shard_map.79 = f32[16,22,4,128]{3,2,1,0:T(4,128)} custom-call(f32[22,16,4,128]{3,2,1,0:T(4,128)} %bitcast.68), custom_call_target="tpu_custom_call" | custom-call | bytes 1441792 | tf_op jit(solution)/shard_map/pallas_call | solution.py:546
  2.8 0.0 copy-start
  2.8 0.0 copy-start.1
  2.8 7.5 %all-to-all-start = ((f32[16,22,4,128]{3,2,1,0:T(4,128)}), f32[16,22,4,128]{3,2,1,0:T(4,128)S(1)}, u32[]{:S(2)}, u32[]{:S(2)}) async-start(f32[16,22,4,128]{3,2,1,0:T(4,128)} %shard_map.79), calls=%async_computation | async-start | bytes 1441792 | tf_op jit(solution)/shard_map/all_to_all | solution.py:632
  10.3 0.0 copy-done.3
  10.3 0.6 fusion.19
  13.4 0.0 copy-done.4
  13.5 0.1 reshape.177
  13.6 0.1 slice_bitcast_fusion
  13.7 0.0 copy-done.2
  13.8 0.1 concatenate.13
  13.8 0.4 fusion.2
  14.3 0.4 fusion
  14.8 0.1 stack.32.scales
  14.9 0.1 pad_maximum_fusion.mix_ref
  15.0 0.0 copy-done
  15.1 0.0 copy-done.1
  15.1 0.6 shard_map.77
  15.7 1.7 %collective-permute-start = (f32[84,128]{1,0:T(8,128)S(1)}, f32[84,128]{1,0:T(8,128)S(1)}, u32[]{:S(2)}, u32[]{:S(2)}) collective-permute-start(f32[84,128]{1,0:T(8,128)S(1)} %get-tuple-element.17), channel_id=1, source_target_pairs={{0,1},{1,2},{2,3},{3,0},{4,5},{5,6},{6,7},{7,4},{8,9},{9,10},{10,1... | collective-permute-start | bytes 129032 | tf_op jit(solution)/shard_map/ppermute | solution.py:655
  17.3 0.0 collective-permute-start.1
  17.4 0.5 collective-permute-start.2
  17.9 0.1 convert_reduce_fusion
  18.1 0.6 collective-permute-done.refs_1_
  18.7 2.6 %collective-permute-done.1.refs_2_ = f32[84,128]{1,0:T(8,128)S(1)} collective-permute-done((f32[84,128]{1,0:T(8,128)S(1)}, f32[84,128]{1,0:T(8,128)S(1)}, u32[]{:S(2)}, u32[]{:S(2)}) %collective-permute-start.1) | collective-permute-done | bytes 43040 | tf_op jit(solution)/shard_map/ppermute | solution.py:655
  21.3 0.2 collective-permute-done.2.refs_3_
  21.5 0.8 shard_map.78
  22.3 5.4 %all-to-all-done = f32[16,22,4,128]{3,2,1,0:T(4,128)S(1)} async-done(((f32[16,22,4,128]{3,2,1,0:T(4,128)}), f32[16,22,4,128]{3,2,1,0:T(4,128)S(1)}, u32[]{:S(2)}, u32[]{:S(2)}) %all-to-all-start) | async-done | bytes 720928 | tf_op jit(solution)/shard_map/all_to_all | solution.py:632
  27.7 0.1 mul.69.weight_ref
  27.8 1.0 %shard_map.80 = (f32[8,2,88,128]{3,2,1,0:T(8,128)S(1)}, f32[1056,128]{1,0:T(8,128)}, f32[1056,128]{1,0:T(8,128)S(1)}) custom-call(s32[1]{0:T(128)} %bitcast.9.odd, f32[7,8,640]{2,1,0:T(8,128)S(1)} %get-tuple-element.20.a_ref, f32[88,128]{1,0:T(8,128)S(1)} %mul.69.weight_ref, f32[1408,128]{1,0:T(8,128)S(1)} %bitcast.64), custom_call_target="tpu_custom_call" | custom-call | bytes 2711552 | tf_op jit(solution)/shard_map/pallas_call | solution.py:546
  28.8 3.0 %collective-permute-start.3 = (f32[1056,128]{1,0:T(8,128)}, f32[1056,128]{1,0:T(8,128)S(1)}, u32[]{:S(2)}, u32[]{:S(2)}) collective-permute-start(f32[1056,128]{1,0:T(8,128)} %get-tuple-element.26), channel_id=1, source_target_pairs={{1,2},{3,7},{6,5},{4,8},{9,10},{11,15},{14,13},{2,1},{7,3},{5,6},{... | collective-permute-start | bytes 1622024 | tf_op jit(solution)/shard_map/ppermute | solution.py:677
  31.7 0.1 collective-permute-start.4
  31.8 0.1 add_convert_fusion.inside
  31.9 2.2 %shard_map.81 = (f32[8,2,88,128]{3,2,1,0:T(8,128)S(1)}, f32[8,2,88,128]{3,2,1,0:T(8,128)S(1)}) custom-call(f32[5]{0:T(128)S(1)} %stack.32.scales, bf16[528,192]{1,0:T(8,128)(2,1)S(1)} %pad_maximum_fusion.mix_ref, f32[7,8,640]{2,1,0:T(8,128)S(1)} %get-tuple-element.20.a_ref, f32[7,8,512]{2,1,0:T(8,128)S(1)} %get-tuple-element.21.b_ref, ...), custom_call_target="tpu_custom_call" | custom-call | flops 3000000000 | bytes 2826240 | tf_op jit(solution)/shard_map/pallas_call | solution.py:546
  34.1 5.5 %collective-permute-done.3.chip_ref = f32[1056,128]{1,0:T(8,128)S(1)} collective-permute-done((f32[1056,128]{1,0:T(8,128)}, f32[1056,128]{1,0:T(8,128)S(1)}, u32[]{:S(2)}, u32[]{:S(2)}) %collective-permute-start.3) | collective-permute-done | bytes 540704 | tf_op jit(solution)/shard_map/ppermute | solution.py:677
  39.7 0.0 collective-permute-done.4.core_ref
  39.7 0.1 mul.67.unweight_ref
  39.7 11.1 %shard_map.82 = f32[2816,128]{1,0:T(8,128)S(1)} custom-call(f32[5]{0:T(128)S(1)} %stack.32.scales, f32[2]{0:T(128)S(1)} %add_convert_fusion.inside, s32[1]{0:T(128)} %bitcast.9.odd, bf16[528,192]{1,0:T(8,128)(2,1)S(1)} %pad_maximum_fusion.mix_ref, f32[7,8,640]{2,1,0:T(8,128)S(1)} %get-tuple-element.20.a_ref, f32[7,8,512]{2,1,0:T(8,128)S(1)} %get-tuple-element.21.b_ref, ...), custom_call_target="tpu_custom_call" | custom-call | flops 10000000000 | bytes 5423104 | tf_op jit(solution)/shard_map/pallas_call | solution.py:546
  50.8 39.5 %all_to_all.10.in_ref = f32[16,2,22,4,128]{4,3,2,1,0:T(4,128)S(1)} all-to-all(f32[16,2,22,4,128]{4,3,2,1,0:T(4,128)S(1)} %bitcast.65), channel_id=1, replica_groups=mesh['groups'=2,'chaos'=4,'space'=4] {'chaos','space'}, dimensions={0} | all-to-all | bytes 2883584 | tf_op jit(solution)/shard_map/all_to_all | solution.py:710
  90.3 1.4 %shard_map.83 = (f32[22,16,4,128]{3,2,1,0:T(4,128)}, f32[22,16,4,128]{3,2,1,0:T(4,128)}) custom-call(f32[16,2,22,4,128]{4,3,2,1,0:T(4,128)S(1)} %all_to_all.10.in_ref), custom_call_target="tpu_custom_call" | custom-call | bytes 2883584 | tf_op jit(solution)/shard_map/pallas_call | solution.py:546
  (10 shorter events, 0.1 us)
Async XLA Ops:
  0.6 9.7 %copy-start.3 = (f32[2]{0:T(128)S(1)}, f32[2]{0:T(128)}, u32[]{:S(2)}) copy-start(f32[2]{0:T(128)} %param.11) | copy-start | bytes 28
  0.6 12.8 %copy-start.4 = (s32[88]{0:T(128)S(1)}, s32[88]{0:T(128)}, u32[]{:S(2)}) copy-start(s32[88]{0:T(128)} %param.10) | copy-start | bytes 1060
  0.7 13.1 %copy-start.2 = (s32[6,28,3]{1,2,0:T(4,128)S(1)}, s32[6,28,3]{1,2,0:T(4,128)}, u32[]{:S(2)}) copy-start(s32[6,28,3]{1,2,0:T(4,128)} %param.9) | copy-start | bytes 6052
  2.8 12.2 %copy-start = (f32[6,2,4096]{2,1,0:T(2,128)S(1)}, f32[6,2,4096]{2,1,0:T(2,128)}, u32[]{:S(2)}) copy-start(f32[6,2,4096]{2,1,0:T(2,128)} %param.8) | copy-start | bytes 589828
  2.8 12.2 %copy-start.1 = (f32[2,4096]{1,0:T(2,128)S(1)}, f32[2,4096]{1,0:T(2,128)}, u32[]{:S(2)}) copy-start(f32[2,4096]{1,0:T(2,128)} %param.7) | copy-start | bytes 98308
  2.8 24.9 %all-to-all-start = ((f32[16,22,4,128]{3,2,1,0:T(4,128)}), f32[16,22,4,128]{3,2,1,0:T(4,128)S(1)}, u32[]{:S(2)}, u32[]{:S(2)}) async-start(f32[16,22,4,128]{3,2,1,0:T(4,128)} %shard_map.79), calls=%async_computation | async-start | bytes 1441792 | tf_op jit(solution)/shard_map/all_to_all | solution.py:632
  15.7 3.1 %collective-permute-start = (f32[84,128]{1,0:T(8,128)S(1)}, f32[84,128]{1,0:T(8,128)S(1)}, u32[]{:S(2)}, u32[]{:S(2)}) collective-permute-start(f32[84,128]{1,0:T(8,128)S(1)} %get-tuple-element.17), channel_id=1, source_target_pairs={{0,1},{1,2},{2,3},{3,0},{4,5},{5,6},{6,7},{7,4},{8,9},{9,10},{10,1... | collective-permute-start | bytes 129032 | tf_op jit(solution)/shard_map/ppermute | solution.py:655
  17.3 3.9 %collective-permute-start.1 = (f32[84,128]{1,0:T(8,128)S(1)}, f32[84,128]{1,0:T(8,128)S(1)}, u32[]{:S(2)}, u32[]{:S(2)}) collective-permute-start(f32[84,128]{1,0:T(8,128)S(1)} %get-tuple-element.18), channel_id=1, source_target_pairs={{0,2},{1,3},{2,0},{3,1},{4,6},{5,7},{6,4},{7,5},{8,10},{9,11},{10,... | collective-permute-start | bytes 129032 | tf_op jit(solution)/shard_map/ppermute | solution.py:655
  17.4 4.2 %collective-permute-start.2 = (f32[84,128]{1,0:T(8,128)S(1)}, f32[84,128]{1,0:T(8,128)S(1)}, u32[]{:S(2)}, u32[]{:S(2)}) collective-permute-start(f32[84,128]{1,0:T(8,128)S(1)} %get-tuple-element.19), channel_id=1, source_target_pairs={{0,3},{1,0},{2,1},{3,2},{4,7},{5,4},{6,5},{7,6},{8,11},{9,8},{10,9... | collective-permute-start | bytes 129032 | tf_op jit(solution)/shard_map/ppermute | solution.py:655
  28.8 10.9 %collective-permute-start.3 = (f32[1056,128]{1,0:T(8,128)}, f32[1056,128]{1,0:T(8,128)S(1)}, u32[]{:S(2)}, u32[]{:S(2)}) collective-permute-start(f32[1056,128]{1,0:T(8,128)} %get-tuple-element.26), channel_id=1, source_target_pairs={{1,2},{3,7},{6,5},{4,8},{9,10},{11,15},{14,13},{2,1},{7,3},{5,6},{... | collective-permute-start | bytes 1622024 | tf_op jit(solution)/shard_map/ppermute | solution.py:677
  31.7 7.9 %collective-permute-start.4 = (f32[1056,128]{1,0:T(8,128)S(1)}, f32[1056,128]{1,0:T(8,128)S(1)}, u32[]{:S(2)}, u32[]{:S(2)}) collective-permute-start(f32[1056,128]{1,0:T(8,128)S(1)} %get-tuple-element.27), channel_id=1, source_target_pairs={{0,1},{2,3},{7,6},{5,4},{8,9},{10,11},{15,14},{13,12},{1,0},{3,2},... | collective-permute-start | bytes 1622024 | tf_op jit(solution)/shard_map/ppermute | solution.py:677
